TPU v7x, 512 devices: a whole 4x8x8 slice. The times are simulated.
512 devices in a mesh: dp: 32 (over y, z_lo, core), tensor: 16 (over z_hi, x).
Axes of the slice: x: 4, y: 8, z: 8 (z_hi: 4, z_lo: 2; z = z_hi * 2 + z_lo), core: 2. Of those that a mesh axis runs over, the one named last changes fastest.
Arguments:
- tokens: bfloat16 [4096, 14336], P('dp', 'tensor'), may hold values from -22 to 22
- frozen_matrix: bfloat16 [14336, 4096], P('tensor', 'dp')
- adapter_down_factor: bfloat16 [14336, 64], P('tensor'), may hold values from -0.046875 to 0.046875
- adapter_up_factor: bfloat16 [64, 4096], P(None, 'tensor'), may hold values from -3 to 3
- magnitude: bfloat16 [4096], P('tensor'), may hold values from 0.5 to 2
- cotangent: bfloat16 [4096, 4096], P('dp'), may hold values from -6 to 6
Outputs:
- output: bfloat16 [4096, 4096], P('dp', 'tensor')
- input_gradient: bfloat16 [4096, 14336], P('dp', 'tensor')
- grad_down: float32 [14336, 64], P('tensor')
- grad_up: float32 [64, 4096], P(None, 'tensor')
- grad_magnitude: float32 [4096], P('tensor')
All inputs are finite; a program needn't handle non-finite values.
Results may differ from a plain program's by a relative error of at most 0.0056.
Values may be sent and summed in bfloat16 or wider, within the bound.
No kernel may reach another device: no remote copies, remote signals or barrier semaphores. Data moves between devices by JAX's collectives and lax.ppermute only.
A program may use at most 64 MiB of HBM per device.

v0:
```python
import math

import jax
import jax.numpy as jnp
from jax import lax
from jax.sharding import PartitionSpec as P

epsilon = 1e-06


def on_device(tokens, frozen_matrix, adapter_down_factor, adapter_up_factor, magnitude, cotangent):
    tok_rows = tokens.shape[0]
    local_portion = adapter_up_factor.shape[1]
    gathered_up_factor, full_magnitude = (
        lax.all_gather(adapter_up_factor, "tensor", axis=1, tiled=True),
        lax.all_gather(magnitude, "tensor", axis=0, tiled=True),
    )
    rank_partial = jnp.dot(tokens, adapter_down_factor, preferred_element_type=jnp.float32)
    rank_activation = lax.psum(rank_partial, "tensor").astype(jnp.bfloat16)
    piece = lax.all_gather(frozen_matrix, "dp", axis=1, tiled=True)
    result = jnp.dot(tokens, piece, preferred_element_type=jnp.float32)
    combined_output = piece.astype(jnp.float32) + jnp.dot(
        adapter_down_factor, gathered_up_factor, preferred_element_type=jnp.float32
    )
    squares = jnp.sum(combined_output * combined_output, axis=0)
    square_part = squares
    squares = lax.psum(square_part, "tensor")
    norm = jnp.sqrt(squares + epsilon)
    scale = full_magnitude.astype(jnp.float32) / norm
    frozen_output = lax.psum_scatter(result, "tensor", scatter_dimension=1, tiled=True)
    shard_start = lax.axis_index("tensor") * local_portion
    merged_weight = frozen_output + jnp.dot(
        rank_activation, adapter_up_factor, preferred_element_type=jnp.float32
    )
    own_scale = lax.dynamic_slice_in_dim(scale, shard_start, local_portion, 0)
    own_norm_vals = lax.dynamic_slice_in_dim(norm, shard_start, local_portion, 0)
    output = (merged_weight * own_scale).astype(jnp.bfloat16)
    rescaled_gradient = (cotangent.astype(jnp.float32) * scale).astype(jnp.bfloat16)
    rank_gradient = jnp.dot(
        rescaled_gradient, gathered_up_factor.T, preferred_element_type=jnp.float32
    ).astype(jnp.bfloat16)
    gradient_running_total = lax.dot_general(
        rescaled_gradient,
        lax.all_gather(frozen_matrix, "dp", axis=1, tiled=True),
        (((1,), (1,)), ((), ())),
        preferred_element_type=jnp.float32,
    )
    input_gradient = (
        gradient_running_total
        + jnp.dot(rank_gradient, adapter_down_factor.T, preferred_element_type=jnp.float32)
    ).astype(jnp.bfloat16)
    own_grad = lax.dynamic_slice_in_dim(rescaled_gradient, shard_start, local_portion, 1)
    own_cotangent = lax.dynamic_slice_in_dim(cotangent, shard_start, local_portion, 1).astype(
        jnp.float32
    )
    down_part = lax.dot_general(
        tokens, rank_gradient, (((0,), (0,)), ((), ())), preferred_element_type=jnp.float32
    )
    up_part = lax.dot_general(
        rank_activation, own_grad, (((0,), (0,)), ((), ())), preferred_element_type=jnp.float32
    )
    magnitude_part = jnp.sum(own_cotangent * merged_weight / own_norm_vals, axis=0)
    grad_down, grad_up, grad_magnitude = lax.psum((down_part, up_part, magnitude_part), "dp")
    factor = 1.0 / math.sqrt(tok_rows * lax.axis_size("dp"))
    return (output, input_gradient, grad_down * factor, grad_up * factor, grad_magnitude * factor)


def solution(mesh):
    return jax.shard_map(
        on_device,
        mesh=mesh,
        in_specs=(
            P("dp", "tensor"),
            P("tensor", "dp"),
            P("tensor", None),
            P(None, "tensor"),
            P("tensor"),
            P("dp", None),
        ),
        out_specs=(
            P("dp", "tensor"),
            P("dp", "tensor"),
            P("tensor", None),
            P(None, "tensor"),
            P("tensor"),
        ),
        check_vma=False,
    )
```

profile of v0, /device:TPU:1, one launch (start us, length us, event | category | flops | bytes accessed | tf_op | source)
XLA Modules:
  0.0 562.1 jit_solution(1411043609496526643)
XLA Ops:
  7.2 0.0 copy-start
  7.2 0.0 all-gather.3.cloned.1.call-start
  7.2 0.7 all-gather.3.cloned.1.call-update
  7.9 0.0 all-reduce.4.cloned.1.call-start
  8.0 0.7 reshape.13
  8.6 42.8 %all-gather = bf16[16,1,256]{2,1,0:T(2,128)(2,1)S(1)} all-gather(bf16[1,1,256]{2,1,0:T(2,128)(2,1)S(1)} %reshape.13), channel_id=1, replica_groups=mesh['dp'=32,'tensor'=16] {'tensor'}, dimensions={0}, use_global_device_ids=true | all-gather | bytes 8704 | tf_op jit(solution)/shard_map/all_gather | solution.py:16
  51.4 0.0 copy-done
  51.4 1.1 fusion.9
  52.6 36.6 %all_gather.12 = bf16[64,4096]{1,0:T(8,128)(2,1)S(1)} all-gather(bf16[64,256]{1,0:T(8,128)(2,1)} %param.9), channel_id=1, replica_groups=mesh['dp'=32,'tensor'=16] {'tensor'}, dimensions={1}, use_global_device_ids=true | all-gather | bytes 557056 | tf_op jit(solution)/shard_map/all_gather | solution.py:15
  89.2 0.0 copy-start.1
  89.2 16.3 %all-gather.3.cloned.1.call-done = bf16[896,4096]{1,0:T(8,128)(2,1)} async-done(((bf16[896,128]{1,0:T(8,128)(2,1)}), bf16[896,4096]{1,0:T(8,128)(2,1)}) %all-gather.3.cloned.1.call-update) | async-done | bytes 7340048 | tf_op jit(solution)/shard_map/all_gather | solution.py:20
  105.5 5.3 multiply_reduce_fusion
  110.8 67.4 %all-reduce.1 = (bf16[128,64]{0,1:T(8,128)(2,1)S(1)}, f32[4096]{0:T(1024)S(1)}) all-reduce(f32[128,64]{0,1:T(8,128)S(1)} %fusion.9, f32[4096]{0:T(1024)S(1)} %multiply_reduce_fusion), channel_id=1, replica_groups=mesh['dp'=32,'tensor'=16] {'tensor'}, use_global_device_ids=true, to_apply=%region_1.0 | all-reduce | flops 12288 | bytes 81920 | tf_op jit(solution)/shard_map/psum | solution.py:19
  178.2 0.0 copy-done.1
  178.2 0.2 multiply_convert_fusion
  178.4 0.5 convolution_convert_fusion
  178.9 0.9 convolution_bitcast_fusion
  179.8 0.8 fusion.2
  180.6 0.0 all-reduce.4.cloned.1.call-update
  180.6 0.0 reduce-scatter.2.cloned.1.call-start
  180.6 5.7 %fusion.8 = f32[128,4096]{1,0:T(8,128)} fusion(bf16[128,896]{1,0:T(8,128)(2,1)S(1)} %copy-done, bf16[896,4096]{1,0:T(8,128)(2,1)} %all-gather.3.cloned.1.call-done), kind=kOutput, calls=%fused_computation.20 | convolution fusion | flops 939524096 | bytes 9666560 | tf_op jit(solution)/shard_map/dot_general | solution.py:21
  186.4 0.0 copy-start.2
  186.4 0.0 copy-start.3
  186.4 0.0 reduce-scatter.2.cloned.1.call-update
  186.4 0.1 dynamic_slice.12
  186.5 0.1 dynamic_slice.15
  186.5 5.5 fusion.10
  192.1 0.0 copy-done.2
  192.1 0.9 fusion
  193.0 206.8 %all-reduce.4.cloned.1.call-done = (f32[896,64]{0,1:T(8,128)}, f32[64,256]{1,0:T(8,128)}) async-done(((f32[896,64]{0,1:T(8,128)}, f32[64,256]{1,0:T(8,128)}), (f32[896,64]{0,1:T(8,128)}, f32[64,256]{1,0:T(8,128)})) %all-reduce.4.cloned.1.call-update) | async-done | bytes 294928 | tf_op jit(solution)/shard_map/psum | solution.py:63
  399.8 1.5 broadcast_multiply_fusion.1
  401.3 1.6 broadcast_multiply_fusion
  403.0 96.2 %reduce-scatter.2.cloned.1.call-done = f32[128,256]{1,0:T(8,128)} async-done(((f32[128,4096]{1,0:T(8,128)}), f32[128,256]{1,0:T(8,128)}) %reduce-scatter.2.cloned.1.call-update) | async-done | bytes 131088 | tf_op jit(solution)/shard_map/reduce_scatter | solution.py:30
  499.1 0.0 copy-done.3
  499.1 1.7 fusion.1
  500.9 54.1 %psum.39 = f32[256]{0:T(256)S(1)} all-reduce(f32[256]{0:T(256)S(1)} %get-tuple-element.9), channel_id=1, replica_groups=mesh['dp'=32,'tensor'=16] {'dp'}, use_global_device_ids=true, to_apply=%region_7.0 | all-reduce | flops 256 | bytes 2048 | tf_op jit(solution)/shard_map/psum | solution.py:63
  555.0 0.6 broadcast_multiply_fusion.2
  (2 shorter events, 0.0 us)
Async XLA Ops:
  7.2 44.3 %copy-start = (bf16[128,896]{1,0:T(8,128)(2,1)S(1)}, bf16[128,896]{1,0:T(8,128)(2,1)}, u32[]{:S(2)}) copy-start(bf16[128,896]{1,0:T(8,128)(2,1)} %param.6) | copy-start | bytes 688132
  7.2 98.3 %all-gather.3.cloned.1.call-start = ((), (), s32[]{:S(2)}) async-start(), calls=%async_computation.1 | async-start | bytes 7569408 | tf_op jit(solution)/shard_map/all_gather | solution.py:20
  7.9 391.9 %all-reduce.4.cloned.1.call-start = ((), (), s32[]{:S(2)}) async-start(), calls=%async_computation.3 | async-start | bytes 589824 | tf_op jit(solution)/shard_map/psum | solution.py:63
  89.2 89.1 %copy-start.1 = (bf16[128,4096]{1,0:T(8,128)(2,1)S(1)}, bf16[128,4096]{1,0:T(8,128)(2,1)}, u32[]{:S(2)}) copy-start(bf16[128,4096]{1,0:T(8,128)(2,1)} %param.11) | copy-start | bytes 3145732
  180.6 318.5 %reduce-scatter.2.cloned.1.call-start = ((), (), s32[]{:S(2)}) async-start(), calls=%async_computation.2 | async-start | bytes 2228224 | tf_op jit(solution)/shard_map/reduce_scatter | solution.py:30
  186.4 5.7 %copy-start.2 = (bf16[896,64]{0,1:T(8,128)(2,1)S(1)}, bf16[896,64]{0,1:T(8,128)(2,1)}, u32[]{:S(2)}) copy-start(bf16[896,64]{0,1:T(8,128)(2,1)} %param.8) | copy-start | bytes 344068
  186.4 312.7 %copy-start.3 = (bf16[64,256]{1,0:T(8,128)(2,1)S(1)}, bf16[64,256]{1,0:T(8,128)(2,1)}, u32[]{:S(2)}) copy-start(bf16[64,256]{1,0:T(8,128)(2,1)} %param.9) | copy-start | bytes 98308
Sparse Core Ops, SparseCore 0:
  10.1 95.3 all-gather.2
  180.7 219.0 all-reduce.3
  404.6 94.5 reduce-scatter.1
where the time goes:
time: 562 us
  waiting for transfers between devices  320 us (57%)
  blocking collectives  201 us (36%)
  matrix products  22.5 us (4%)
  between operations  13.8 us (2%)
    psum x1, waiting for transfers between devices, on_device(): lax.psum((down_part, up_part, magnitude_part), 'dp')  207 us
    reduce_scatter x1, waiting for transfers between devices, on_device(): lax.psum_scatter(result, 'tensor', scatter_dimension=1, tiled=True)  96.2 us
    psum x1, blocking collectives, on_device(): rank_activation = lax.psum(rank_partial, 'tensor').astype(jnp.bfloat16)  67.4 us
    psum x1, blocking collectives, on_device(): lax.psum((down_part, up_part, magnitude_part), 'dp')  54.1 us
    all_gather x1, blocking collectives, on_device(): lax.all_gather(magnitude, 'tensor', axis=0, tiled=True)  42.8 us
    all_gather x1, blocking collectives, on_device(): lax.all_gather(adapter_up_factor, 'tensor', axis=1, tiled=True)  36.6 us
    all_gather x1, waiting for transfers between devices, on_device(): piece = lax.all_gather(frozen_matrix, 'dp', axis=1, tiled=True)  16.3 us
  transfers between devices with their start and end apart: 3, of which 3 were waited for; matrix products, arithmetic and copies ran while one was open for 3% of the time, Pallas kernels for 0%

commit v1 on v0

v1 whole, which is shorter than its diff:
```python
import functools
import math

import jax
import jax.numpy as jnp
from jax import lax
from jax.experimental import pallas as pl
from jax.experimental.pallas import tpu as pltpu
from jax.sharding import PartitionSpec as P

epsilon = 1e-06
F32 = jnp.float32
BF16 = jnp.bfloat16


def spread(block, axis):
    n = lax.axis_size(axis)
    return lax.all_to_all(jnp.broadcast_to(block[None], (n,) + block.shape), axis, 0, 0)


def forward_kernel(x_ref, w_ref, y_ref):
    for h in range(2):
        y_ref[0, :, h * 128 : (h + 1) * 128] = jnp.dot(
            x_ref[...], w_ref[h], preferred_element_type=F32
        ).astype(BF16)


def forward(x, gathered):
    t, f = x.shape
    n = gathered.shape[0]
    return pl.pallas_call(
        forward_kernel,
        grid=(n // 2,),
        in_specs=[
            pl.BlockSpec((t, f), lambda i: (0, 0)),
            pl.BlockSpec((2, f, 128), lambda i: (i, 0, 0)),
        ],
        out_specs=pl.BlockSpec((1, t, 256), lambda i: (i, 0, 0)),
        out_shape=jax.ShapeDtypeStruct((n // 2, t, 256), BF16),
        cost_estimate=pl.CostEstimate(
            flops=2 * t * f * n * 128, bytes_accessed=2 * f * n * 128, transcendentals=0
        ),
        name="forward",
    )(x, gathered)


def backward_kernel(g_ref, w_ref, r_ref, a_ref, o_ref, acc):
    i = pl.program_id(0)
    dims = (((1,), (1,)), ((), ()))

    @pl.when(i == 0)
    def _():
        acc[...] = lax.dot_general(r_ref[...], a_ref[...], dims, preferred_element_type=F32)

    wide = jnp.concatenate([w_ref[0], w_ref[1]], axis=1)
    acc[...] += lax.dot_general(g_ref[...], wide, dims, preferred_element_type=F32)

    @pl.when(i == pl.num_programs(0) - 1)
    def _():
        o_ref[...] = acc[...].astype(BF16)


def backward(g, gathered, r, a):
    t = g.shape[0]
    n, f, _ = gathered.shape
    return pl.pallas_call(
        backward_kernel,
        grid=(n // 2,),
        in_specs=[
            pl.BlockSpec((t, 256), lambda i: (0, i)),
            pl.BlockSpec((2, f, 128), lambda i: (i, 0, 0)),
            pl.BlockSpec(r.shape, lambda i: (0, 0)),
            pl.BlockSpec(a.shape, lambda i: (0, 0)),
        ],
        out_specs=pl.BlockSpec((t, f), lambda i: (0, 0)),
        out_shape=jax.ShapeDtypeStruct((t, f), BF16),
        scratch_shapes=[pltpu.VMEM((t, f), F32)],
        cost_estimate=pl.CostEstimate(
            flops=2 * t * f * n * 128, bytes_accessed=2 * f * n * 128, transcendentals=0
        ),
        name="backward",
    )(g, gathered, r, a)


def on_device(tokens, frozen_matrix, adapter_down_factor, adapter_up_factor, magnitude, cotangent):
    t, f = tokens.shape
    n_dp, n_tp = lax.axis_size("dp"), lax.axis_size("tensor")
    p, q = lax.axis_index("dp"), lax.axis_index("tensor")
    rank, own = adapter_up_factor.shape
    half = f // 2

    gathered = lax.all_gather(frozen_matrix, "dp", axis=0)

    rank_partial = lax.dot_general(
        adapter_down_factor, tokens, (((0,), (1,)), ((), ())), preferred_element_type=F32
    ).astype(BF16)
    first = jnp.concatenate(
        [
            adapter_up_factor[:, :128],
            adapter_up_factor[:, 128:],
            rank_partial,
            magnitude.reshape(2, 128),
            jnp.zeros((14, 128), BF16),
        ],
        axis=0,
    )
    first = spread(first, "tensor")
    up_blocks = first[:, : 2 * rank].reshape(2 * n_tp, rank, 128)
    full_up = jnp.moveaxis(up_blocks, 0, 1).reshape(rank, -1)
    full_magnitude = first[:, 3 * rank : 3 * rank + 2].reshape(-1)
    rank_activation = jnp.sum(first[:, 2 * rank : 3 * rank].astype(F32), axis=0).astype(BF16)

    own_up = lax.dynamic_index_in_dim(up_blocks, p, 0, keepdims=False)
    combined = frozen_matrix.astype(F32) + jnp.dot(
        adapter_down_factor, own_up, preferred_element_type=F32
    )
    squares = jnp.sum(combined * combined, axis=0, keepdims=True)
    squares = jnp.sum(spread(squares, "tensor"), axis=0)
    squares = spread(squares, "dp").reshape(-1)
    norm = jnp.sqrt(squares + epsilon)
    scale = full_magnitude.astype(F32) / norm

    scaled = (cotangent.astype(F32) * scale).astype(BF16)
    rank_back = lax.dot_general(
        scaled, full_up, (((1,), (1,)), ((), ())), preferred_element_type=F32
    ).astype(BF16)
    down = lax.dot_general(
        tokens, rank_back, (((0,), (0,)), ((), ())), preferred_element_type=F32
    )
    start = q * own
    own_scaled = lax.dynamic_slice_in_dim(scaled, start, own, 1)
    up = jnp.dot(rank_activation, own_scaled, preferred_element_type=F32)
    shares = jnp.concatenate(
        [jnp.concatenate([down[:half], down[half:]], axis=1), up[:, :128], up[:, 128:]], axis=0
    ).astype(BF16)
    rows = shares.shape[0] // n_dp
    shares = lax.all_to_all(shares.reshape(n_dp, rows, 128), "dp", 0, 0)
    shares = jnp.sum(shares.astype(F32), axis=0)

    parts = lax.all_to_all(forward(tokens, gathered), "tensor", 0, 0)
    input_gradient = backward(scaled, gathered, rank_back, adapter_down_factor)
    merged = jnp.sum(parts.astype(F32), axis=0) + lax.dot_general(
        rank_activation, adapter_up_factor, (((0,), (0,)), ((), ())), preferred_element_type=F32
    )
    own_scale = lax.dynamic_slice_in_dim(scale, start, own, 0)
    own_norm = lax.dynamic_slice_in_dim(norm, start, own, 0)
    own_cotangent = lax.dynamic_slice_in_dim(cotangent, start, own, 1).astype(F32)
    output = (merged * own_scale).astype(BF16)
    mag_part = jnp.sum(own_cotangent * merged, axis=0) / own_norm

    high = mag_part.astype(BF16)
    low = (mag_part - high.astype(F32)).astype(BF16)
    last = jnp.concatenate(
        [shares.astype(BF16), high.reshape(2, 128), low.reshape(2, 128)], axis=0
    )
    last = spread(last, "dp").astype(F32)
    factor = 1.0 / math.sqrt(t * n_dp)
    sums = last[:, :rows].reshape(-1, 128) * factor
    grad_down = jnp.concatenate([sums[:half, :rank], sums[:half, rank:]], axis=0)
    grad_up = jnp.concatenate([sums[half : half + rank], sums[half + rank :]], axis=1)
    mags = jnp.sum(last[:, rows : rows + 2] + last[:, rows + 2 : rows + 4], axis=0)
    grad_magnitude = mags.reshape(-1) * factor
    return (output, input_gradient, grad_down, grad_up, grad_magnitude)


def solution(mesh):
    return jax.shard_map(
        on_device,
        mesh=mesh,
        in_specs=(
            P("dp", "tensor"),
            P("tensor", "dp"),
            P("tensor", None),
            P(None, "tensor"),
            P("tensor"),
            P("dp", None),
        ),
        out_specs=(
            P("dp", "tensor"),
            P("dp", "tensor"),
            P("tensor", None),
            P(None, "tensor"),
            P("tensor"),
        ),
        check_vma=False,
    )
```

time: 562 us -> 185 us (0.33)
  waiting for transfers between devices: 320 us -> 73.7 us
  blocking collectives: 201 us -> 0 us
  starting transfers between devices: 0.12 us -> 58.3 us
  Pallas kernels: 0 us -> 24.5 us
  matrix products: 22.5 us -> 3.21 us
  local copies, waits for them, and re-layouts: 0.83 us -> 7.66 us
    psum x1 -> x0, waiting for transfers between devices: 207 us -> none  [on_device(): lax.psum((down_part, up_part, magnitude_part), 'dp')]
    psum x2 -> x0, blocking collectives: 121 us -> none  [the longest x1 67.4 us: on_device(): rank_activation = lax.psum(rank_partial, 'tensor').astype(jnp.bfloat16)]
    reduce_scatter x1 -> x0, waiting for transfers between devices: 96.2 us -> none  [on_device(): lax.psum_scatter(result, 'tensor', scatter_dimension=1, tiled=True)]
    all_gather x2 -> x0, blocking collectives: 79.4 us -> none  [the longest x1 42.8 us: on_device(): lax.all_gather(magnitude, 'tensor', axis=0, tiled=True)]
    all_to_all x0 -> x6, waiting for transfers between devices: none -> 68.1 us  [the longest x4 42.5 us: spread(): lax.all_to_all(jnp.broadcast_to(block[None], (n,) + block.shape), axis, 0...]
    all_to_all x0 -> x6, starting transfers between devices: none -> 58.2 us  [the longest x4 43.5 us: spread(): lax.all_to_all(jnp.broadcast_to(block[None], (n,) + block.shape), axis, 0...]
    pallas_call x0 -> x2, Pallas kernels: none -> 24.5 us  [the longest x1 12.5 us: backward(): pl.pallas_call(backward_kernel, grid=(n // 2,), in_specs=[pl.BlockSpec((t...]
    dot_general x9 -> x6, matrix products: 22.5 us -> 3.21 us  [the longest x1 1.19 us: on_device(): lax.dot_general(adapter_down_factor, tokens, (((0,), (1,)), ((), ())), pr...]
  transfers between devices with their start and end apart: 3 -> 7, of which waited for: 3 -> 5; matrix products, arithmetic and copies ran while one was open for 3% -> 5% of each run, Pallas kernels for 0% -> 13%
where the time goes in v1:
time: 185 us; the launch traced here: 184 us
  waiting for transfers between devices  73.7 us (40%)
  starting transfers between devices  58.3 us (32%)
  Pallas kernels  24.5 us (13%)
  between operations  14.3 us (8%)
  local copies, waits for them, and re-layouts  7.66 us (4%)
  matrix products  3.21 us (2%)
  other arithmetic  2.11 us (1%)
    all_to_all x4, starting transfers between devices, spread(): lax.all_to_all(jnp.broadcast_to(block[None], (n,) + block.shape), axis, 0...  43.5 us
    all_to_all x4, waiting for transfers between devices, spread(): lax.all_to_all(jnp.broadcast_to(block[None], (n,) + block.shape), axis, 0...  42.5 us
    all_to_all x1, waiting for transfers between devices, on_device(): parts = lax.all_to_all(forward(tokens, gathered), 'tensor', 0, 0)  25.5 us
    pallas_call x1, Pallas kernels, backward(): pl.pallas_call(backward_kernel, grid=(n // 2,), in_specs=[pl.BlockSpec((t...  12.5 us
    pallas_call x1, Pallas kernels, forward(): pl.pallas_call(forward_kernel, grid=(n // 2,), in_specs=[pl.BlockSpec((t,...  12.1 us
    all_to_all x1, starting transfers between devices, on_device(): parts = lax.all_to_all(forward(tokens, gathered), 'tensor', 0, 0)  10.6 us
    all_gather x1, waiting for transfers between devices, on_device(): gathered = lax.all_gather(frozen_matrix, 'dp', axis=0)  4.97 us
    all_to_all x1, starting transfers between devices, on_device(): shares = lax.all_to_all(shares.reshape(n_dp, rows, 128), 'dp', 0, 0)  4.14 us
  transfers between devices with their start and end apart: 7, of which 5 were waited for; matrix products, arithmetic and copies ran while one was open for 5% of the time, Pallas kernels for 13%

profile of v1, /device:TPU:1, one launch (start us, length us, event | category | flops | bytes accessed | tf_op | source)
XLA Modules:
  0.0 183.9 jit_solution(12688010833616753322)
XLA Ops:
  7.2 0.0 copy-start.3
  7.2 0.0 all-gather.3.cloned.1.call-start
  7.2 0.7 all-gather.3.cloned.1.call-update
  7.9 0.7 fusion.17
  8.7 1.2 convolution_convert_fusion.3
  9.9 0.0 copy-start.4
  9.9 0.8 concatenate.20
  10.7 1.0 broadcast_in_dim.11
  11.7 0.0 copy-start.2
  11.7 13.6 %all-to-all-start.1 = ((bf16[16,208,128]{2,1,0:T(8,128)(2,1)}), bf16[16,208,128]{2,1,0:T(8,128)(2,1)S(1)}, u32[]{:S(2)}, u32[]{:S(2)}) async-start(bf16[16,208,128]{2,1,0:T(8,128)(2,1)} %broadcast_in_dim.11), calls=%async_computation.1 | async-start | bytes 1703936 | tf_op jit(solution)/shard_map/all_to_all | solution.py:18
  25.3 0.0 copy-done.3
  25.3 0.2 copy.36
  25.5 26.1 %all-to-all-done.1 = bf16[16,208,128]{2,1,0:T(8,128)(2,1)S(1)} async-done(((bf16[16,208,128]{2,1,0:T(8,128)(2,1)}), bf16[16,208,128]{2,1,0:T(8,128)(2,1)S(1)}, u32[]{:S(2)}, u32[]{:S(2)}) %all-to-all-start.1) | async-done | bytes 852000 | tf_op jit(solution)/shard_map/all_to_all | solution.py:18
  51.6 0.0 copy-done.4
  51.6 0.3 fusion.2
  51.9 0.6 broadcast_in_dim.12
  52.6 7.2 %all-to-all-start.2 = ((f32[16,1,128]{2,1,0:T(1,128)}), f32[16,1,128]{2,1,0:T(1,128)S(1)}, u32[]{:S(2)}, u32[]{:S(2)}) async-start(f32[16,1,128]{2,1,0:T(1,128)} %broadcast_in_dim.12), calls=%async_computation.2 | async-start | bytes 16384 | tf_op jit(solution)/shard_map/all_to_all | solution.py:18
  59.8 8.7 %all-to-all-done.2 = f32[16,1,128]{2,1,0:T(1,128)S(1)} async-done(((f32[16,1,128]{2,1,0:T(1,128)}), f32[16,1,128]{2,1,0:T(1,128)S(1)}, u32[]{:S(2)}, u32[]{:S(2)}) %all-to-all-start.2) | async-done | bytes 8224 | tf_op jit(solution)/shard_map/all_to_all | solution.py:18
  68.6 0.6 broadcast_in_dim.13
  69.2 10.9 %all-to-all-start.3 = ((f32[32,1,128]{2,1,0:T(1,128)}), f32[32,1,128]{2,1,0:T(1,128)S(1)}, u32[]{:S(2)}, u32[]{:S(2)}) async-start(f32[32,1,128]{2,1,0:T(1,128)} %broadcast_in_dim.13), calls=%async_computation.3 | async-start | bytes 32768 | tf_op jit(solution)/shard_map/all_to_all | solution.py:18
  80.1 7.7 %all-to-all-done.3 = f32[32,1,128]{2,1,0:T(1,128)S(1)} async-done(((f32[32,1,128]{2,1,0:T(1,128)}), f32[32,1,128]{2,1,0:T(1,128)S(1)}, u32[]{:S(2)}, u32[]{:S(2)}) %all-to-all-start.3) | async-done | bytes 16416 | tf_op jit(solution)/shard_map/all_to_all | solution.py:18
  87.9 0.0 copy-start.1
  87.9 0.0 copy-done.2
  87.9 0.2 multiply_convert_fusion.g_ref
  88.2 0.0 copy-start
  88.2 0.2 convolution_convert_fusion.1
  88.4 0.4 convolution_convert_fusion.2.r_ref
  88.8 0.0 copy-done.1
  88.9 0.0 copy-start.5
  88.9 0.2 fusion.3
  89.1 0.1 fusion.15
  89.2 0.1 pad_maximum_fusion.1
  89.3 0.1 copy.42
  89.4 0.7 convert_element_type.64
  90.1 4.1 %all-to-all-start.4 = ((bf16[32,18,128]{2,1,0:T(8,128)(2,1)}), bf16[32,18,128]{2,1,0:T(8,128)(2,1)S(1)}, u32[]{:S(2)}, u32[]{:S(2)}) async-start(bf16[32,18,128]{2,1,0:T(8,128)(2,1)} %convert_element_type.64), calls=%async_computation.4 | async-start | bytes 393216 | tf_op jit(solution)/shard_map/all_to_all | solution.py:137
  94.3 5.0 %all-gather.3.cloned.1.call-done = bf16[28672,128]{1,0:T(8,128)(2,1)} async-done(((bf16[896,128]{1,0:T(8,128)(2,1)}), bf16[28672,128]{1,0:T(8,128)(2,1)}) %all-gather.3.cloned.1.call-update) | async-done | bytes 7340048 | tf_op jit(solution)/shard_map/all_gather | solution.py:92
  99.3 12.1 %forward.1 = bf16[16,128,256]{2,1,0:T(8,128)(2,1)} custom-call(bf16[128,896]{1,0:T(8,128)(2,1)} %x_ref.1, bf16[32,896,128]{2,1,0:T(8,128)(2,1)} %bitcast.42), custom_call_target="tpu_custom_call" | custom-call | flops 939524096 | bytes 7340032 | tf_op jit(solution)/shard_map/forward/pallas_call | solution.py:31
  111.3 0.0 copy-done
  111.3 0.0 copy-done.5
  111.3 0.0 copy-start.6
  111.4 0.0 all-to-all-done.4
  111.4 10.6 %all-to-all-start = ((bf16[16,128,256]{2,1,0:T(8,128)(2,1)}), bf16[16,128,256]{2,1,0:T(8,128)(2,1)S(1)}, u32[]{:S(2)}, u32[]{:S(2)}) async-start(bf16[16,128,256]{2,1,0:T(8,128)(2,1)} %forward.1), calls=%async_computation | async-start | bytes 2097152 | tf_op jit(solution)/shard_map/all_to_all | solution.py:140
  122.0 0.1 dynamic-slice_divide_fusion
  122.1 0.1 reduce_sum.73
  122.1 25.5 %all-to-all-done = bf16[16,128,256]{2,1,0:T(8,128)(2,1)S(1)} async-done(((bf16[16,128,256]{2,1,0:T(8,128)(2,1)}), bf16[16,128,256]{2,1,0:T(8,128)(2,1)S(1)}, u32[]{:S(2)}, u32[]{:S(2)}) %all-to-all-start) | async-done | bytes 1048608 | tf_op jit(solution)/shard_map/all_to_all | solution.py:140
  147.7 0.1 convert_reduce_fusion
  147.8 0.0 copy-done.6
  147.8 0.8 multiply_reduce_fusion
  148.7 0.1 convert_bitcast_fusion
  148.8 0.7 broadcast_in_dim.14
  149.5 11.8 %all-to-all-start.5 = ((bf16[32,22,128]{2,1,0:T(8,128)(2,1)}), bf16[32,22,128]{2,1,0:T(8,128)(2,1)S(1)}, u32[]{:S(2)}, u32[]{:S(2)}) async-start(bf16[32,22,128]{2,1,0:T(8,128)(2,1)} %broadcast_in_dim.14), calls=%async_computation.5 | async-start | bytes 393216 | tf_op jit(solution)/shard_map/all_to_all | solution.py:18
  161.3 0.8 copy.40.a_ref
  162.2 12.5 %backward.1 = bf16[128,896]{1,0:T(8,128)(2,1)} custom-call(bf16[128,4096]{1,0:T(8,128)(2,1)} %copy-done, bf16[32,896,128]{2,1,0:T(8,128)(2,1)} %bitcast.43, bf16[128,64]{1,0:T(8,128)(2,1)} %copy-done.5, bf16[896,64]{1,0:T(8,128)(2,1)} %copy.40.a_ref), custom_call_target="tpu_custom_call" | custom-call | flops 939524096 | bytes 7340032 | tf_op jit(solution)/shard_map/backward/pallas_call | solution.py:66
  174.6 0.0 all-to-all-done.5
  174.8 0.1 fusion.14
  174.9 0.6 multiply_bitcast_fusion
  175.5 0.9 copy.43
  176.4 0.6 pad_maximum_fusion.2
  (17 shorter events, 0.4 us)
Async XLA Ops:
  7.2 18.1 %copy-start.3 = (bf16[896,128]{1,0:T(8,128)(2,1)S(1)}, bf16[896,128]{1,0:T(8,128)(2,1)}, u32[]{:S(2)}) copy-start(bf16[896,128]{1,0:T(8,128)(2,1)} %param.7) | copy-start | bytes 688132
  7.2 92.1 %all-gather.3.cloned.1.call-start = ((), (), s32[]{:S(2)}) async-start(), calls=%async_computation.6 | async-start | bytes 7569408 | tf_op jit(solution)/shard_map/all_gather | solution.py:92
  9.9 41.7 %copy-start.4 = (bf16[896,64]{0,1:T(8,128)(2,1)S(1)}, bf16[896,64]{0,1:T(8,128)(2,1)}, u32[]{:S(2)}) copy-start(bf16[896,64]{0,1:T(8,128)(2,1)} %param.8) | copy-start | bytes 344068
  11.7 76.2 %copy-start.2 = (bf16[128,4096]{1,0:T(8,128)(2,1)S(1)}, bf16[128,4096]{1,0:T(8,128)(2,1)}, u32[]{:S(2)}) copy-start(bf16[128,4096]{1,0:T(8,128)(2,1)} %param.11) | copy-start | bytes 3145732
  11.7 39.8 %all-to-all-start.1 = ((bf16[16,208,128]{2,1,0:T(8,128)(2,1)}), bf16[16,208,128]{2,1,0:T(8,128)(2,1)S(1)}, u32[]{:S(2)}, u32[]{:S(2)}) async-start(bf16[16,208,128]{2,1,0:T(8,128)(2,1)} %broadcast_in_dim.11), calls=%async_computation.1 | async-start | bytes 1703936 | tf_op jit(solution)/shard_map/all_to_all | solution.py:18
  52.6 16.0 %all-to-all-start.2 = ((f32[16,1,128]{2,1,0:T(1,128)}), f32[16,1,128]{2,1,0:T(1,128)S(1)}, u32[]{:S(2)}, u32[]{:S(2)}) async-start(f32[16,1,128]{2,1,0:T(1,128)} %broadcast_in_dim.12), calls=%async_computation.2 | async-start | bytes 16384 | tf_op jit(solution)/shard_map/all_to_all | solution.py:18
  69.2 18.7 %all-to-all-start.3 = ((f32[32,1,128]{2,1,0:T(1,128)}), f32[32,1,128]{2,1,0:T(1,128)S(1)}, u32[]{:S(2)}, u32[]{:S(2)}) async-start(f32[32,1,128]{2,1,0:T(1,128)} %broadcast_in_dim.13), calls=%async_computation.3 | async-start | bytes 32768 | tf_op jit(solution)/shard_map/all_to_all | solution.py:18
  87.9 0.9 copy-start.1
  88.2 23.2 %copy-start = (bf16[128,4096]{1,0:T(8,128)(2,1)}, bf16[128,4096]{1,0:T(8,128)(2,1)S(1)}, u32[]{:S(2)}) copy-start(bf16[128,4096]{1,0:T(8,128)(2,1)S(1)} %multiply_convert_fusion.g_ref) | copy-start | bytes 3145732
  88.9 22.5 %copy-start.5 = (bf16[128,64]{1,0:T(8,128)(2,1)}, bf16[128,64]{1,0:T(8,128)(2,1)S(1)}, u32[]{:S(2)}) copy-start(bf16[128,64]{1,0:T(8,128)(2,1)S(1)} %convolution_convert_fusion.2.r_ref) | copy-start | bytes 49156
  90.1 21.2 %all-to-all-start.4 = ((bf16[32,18,128]{2,1,0:T(8,128)(2,1)}), bf16[32,18,128]{2,1,0:T(8,128)(2,1)S(1)}, u32[]{:S(2)}, u32[]{:S(2)}) async-start(bf16[32,18,128]{2,1,0:T(8,128)(2,1)} %convert_element_type.64), calls=%async_computation.4 | async-start | bytes 393216 | tf_op jit(solution)/shard_map/all_to_all | solution.py:137
  111.3 36.5 %copy-start.6 = (bf16[64,256]{1,0:T(8,128)(2,1)S(1)}, bf16[64,256]{1,0:T(8,128)(2,1)}, u32[]{:S(2)}) copy-start(bf16[64,256]{1,0:T(8,128)(2,1)} %param.9) | copy-start | bytes 98308
  111.4 36.3 %all-to-all-start = ((bf16[16,128,256]{2,1,0:T(8,128)(2,1)}), bf16[16,128,256]{2,1,0:T(8,128)(2,1)S(1)}, u32[]{:S(2)}, u32[]{:S(2)}) async-start(bf16[16,128,256]{2,1,0:T(8,128)(2,1)} %forward.1), calls=%async_computation | async-start | bytes 2097152 | tf_op jit(solution)/shard_map/all_to_all | solution.py:140
  149.5 25.1 %all-to-all-start.5 = ((bf16[32,22,128]{2,1,0:T(8,128)(2,1)}), bf16[32,22,128]{2,1,0:T(8,128)(2,1)S(1)}, u32[]{:S(2)}, u32[]{:S(2)}) async-start(bf16[32,22,128]{2,1,0:T(8,128)(2,1)} %broadcast_in_dim.14), calls=%async_computation.5 | async-start | bytes 393216 | tf_op jit(solution)/shard_map/all_to_all | solution.py:18
Sparse Core Ops, SparseCore 0:
  10.2 89.0 all-gather.2

commit v2 on v1

v2 whole, which is shorter than its diff:
```python
import math

import jax
import jax.numpy as jnp
from jax import lax
from jax.experimental import pallas as pl
from jax.experimental.pallas import tpu as pltpu
from jax.sharding import Mesh
from jax.sharding import PartitionSpec as P

epsilon = 1e-06
F32 = jnp.float32
BF16 = jnp.bfloat16
DP = ("y", "w", "c")
TP = ("z", "u", "v")


def spread(block, axis):
    n = lax.axis_size(axis)
    return lax.all_to_all(jnp.broadcast_to(block[None], (n,) + block.shape), axis, 0, 0)


def forward_kernel(x_ref, w_ref, y_ref):
    t = x_ref.shape[0] // 2
    for k in range(w_ref.shape[0] // 2):
        wide = jnp.concatenate([w_ref[2 * k], w_ref[2 * k + 1]], axis=1)
        y = jnp.dot(x_ref[...], wide, preferred_element_type=F32).astype(BF16)
        y_ref[2 * k] = y[:t]
        y_ref[2 * k + 1] = y[t:]


def forward(x, gathered, step=4):
    t, f = x.shape
    n = gathered.shape[0]
    return pl.pallas_call(
        forward_kernel,
        grid=(n // step,),
        in_specs=[
            pl.BlockSpec((t, f), lambda i: (0, 0)),
            pl.BlockSpec((step, f, 128), lambda i: (i, 0, 0)),
        ],
        out_specs=pl.BlockSpec((step, t // 2, 256), lambda i: (i, 0, 0)),
        out_shape=jax.ShapeDtypeStruct((n, t // 2, 256), BF16),
        cost_estimate=pl.CostEstimate(
            flops=2 * t * f * n * 128, bytes_accessed=2 * f * n * 128, transcendentals=0
        ),
        name="forward",
    )(x, gathered)


def backward_kernel(g_ref, h_ref, w_ref, r_ref, a_ref, own_ref, other_ref, acc):
    i = pl.program_id(0)
    dims = (((1,), (1,)), ((), ()))
    t = g_ref.shape[0]

    @pl.when(i == 0)
    def _():
        acc[:t] = lax.dot_general(r_ref[...], a_ref[...], dims, preferred_element_type=F32)
        acc[t:] = jnp.zeros_like(acc[t:])

    n = w_ref.shape[0]
    wide = jnp.concatenate([w_ref[k] for k in range(n)], axis=1)
    g = jnp.concatenate([g_ref[...], h_ref[...]], axis=0)
    acc[...] += lax.dot_general(g, wide, dims, preferred_element_type=F32)

    @pl.when(i == pl.num_programs(0) - 1)
    def _():
        own_ref[...] = acc[:t]
        other_ref[...] = acc[t:].astype(BF16)


def backward(g, h, gathered, r, a, step=4):
    t = g.shape[0]
    n, f, _ = gathered.shape
    return pl.pallas_call(
        backward_kernel,
        grid=(n // step,),
        in_specs=[
            pl.BlockSpec((t, step * 128), lambda i: (0, i)),
            pl.BlockSpec((t, step * 128), lambda i: (0, i)),
            pl.BlockSpec((step, f, 128), lambda i: (i, 0, 0)),
            pl.BlockSpec(r.shape, lambda i: (0, 0)),
            pl.BlockSpec(a.shape, lambda i: (0, 0)),
        ],
        out_specs=[pl.BlockSpec((t, f), lambda i: (0, 0))] * 2,
        out_shape=[
            jax.ShapeDtypeStruct((t, f), F32),
            jax.ShapeDtypeStruct((t, f), BF16),
        ],
        scratch_shapes=[pltpu.VMEM((2 * t, f), F32)],
        cost_estimate=pl.CostEstimate(
            flops=4 * t * f * n * 128, bytes_accessed=2 * f * n * 128, transcendentals=0
        ),
        name="backward",
    )(g, h, gathered, r, a)


def swap(x, axis):
    return lax.ppermute(x, axis, [(0, 1), (1, 0)])


def cross(x):
    return lax.ppermute(x, ("w", "v"), [(0, 0), (1, 2), (2, 1), (3, 3)])


def every_other(x, which):
    n = x.shape[-1] // 256
    pick = lambda s: jnp.concatenate(
        [x[..., i * 256 : (i + 1) * 256] for i in range(s, n, 2)], axis=-1
    )
    return jnp.where(which == 0, pick(0), pick(1))


def in_order(which, own, other, axis):
    return jnp.where(
        which == 0,
        jnp.concatenate([own, other], axis=axis),
        jnp.concatenate([other, own], axis=axis),
    )


def on_device(tokens, frozen_matrix, adapter_down_factor, adapter_up_factor, magnitude, cotangent):
    t, f = tokens.shape
    n_dp, n_tp = lax.axis_size(DP), lax.axis_size(TP)
    y, w, c, z, u, v = (lax.axis_index(a) for a in DP + TP)
    rank, own = adapter_up_factor.shape
    half = f // 2

    gathered = lax.all_gather(frozen_matrix, ("y", "c"), axis=0)
    other_tokens = swap(tokens, "w")
    own_cotangent = every_other(cotangent, w)
    other_cotangent = swap(every_other(cotangent, 1 - w), "w")

    rank_partial = lax.dot_general(
        adapter_down_factor, tokens, (((0,), (1,)), ((), ())), preferred_element_type=F32
    ).astype(BF16)
    first = jnp.concatenate(
        [
            jnp.where(c == 0, adapter_up_factor[:, :128], adapter_up_factor[:, 128:]),
            rank_partial,
            magnitude.reshape(2, 128),
            jnp.zeros((6, 128), BF16),
        ],
        axis=0,
    )
    first = spread(first, TP)
    own_half = first[:, :rank]
    full_magnitude = first[:, 2 * rank : 2 * rank + 2].reshape(-1)
    rank_activation = jnp.sum(first[:, rank : 2 * rank].astype(F32), axis=0).astype(BF16)
    other_rank_activation = swap(rank_activation, "w")
    other_half = swap(own_half, "c")
    up_blocks = in_order(c, own_half[:, None], other_half[:, None], 1)
    full_up = jnp.moveaxis(up_blocks, 2, 0).reshape(rank, -1)

    own_up = lax.dynamic_index_in_dim(own_half, 2 * y + w, 0, keepdims=False)
    combined = frozen_matrix.astype(F32) + jnp.dot(
        adapter_down_factor, own_up, preferred_element_type=F32
    )
    squares = jnp.sum(combined * combined, axis=0, keepdims=True)
    squares = jnp.sum(spread(squares, TP), axis=0)
    squares = spread(squares, DP).reshape(-1)
    norm = jnp.sqrt(squares + epsilon)
    scale = full_magnitude.astype(F32) / norm

    scaled = (cotangent.astype(F32) * scale).astype(BF16)
    rank_back = lax.dot_general(
        scaled, full_up, (((1,), (1,)), ((), ())), preferred_element_type=F32
    ).astype(BF16)
    down = lax.dot_general(
        tokens, rank_back, (((0,), (0,)), ((), ())), preferred_element_type=F32
    )
    q = (2 * z + u) * 2 + v
    up = jnp.dot(
        rank_activation,
        lax.dynamic_slice_in_dim(scaled, q * own, own, 1),
        preferred_element_type=F32,
    )
    shares = jnp.concatenate(
        [jnp.concatenate([down[:half], down[half:]], axis=1), up[:, :128], up[:, 128:]], axis=0
    ).astype(BF16)
    rows = shares.shape[0] // n_dp
    shares = lax.all_to_all(shares.reshape(n_dp, rows, 128), DP, 0, 0)
    shares = jnp.sum(shares.astype(F32), axis=0).astype(BF16)
    factor = 1.0 / math.sqrt(t * n_dp)
    sums = spread(shares, DP).astype(F32).reshape(-1, 128) * factor
    grad_down = jnp.concatenate([sums[:half, :rank], sums[:half, rank:]], axis=0)
    grad_up = jnp.concatenate([sums[half : half + rank], sums[half + rank :]], axis=1)

    other_scaled = (other_cotangent.astype(F32) * every_other(scale, w)).astype(BF16)
    own_part, other_part = backward(
        every_other(scaled, w), other_scaled, gathered, rank_back, adapter_down_factor
    )
    input_gradient = (own_part + swap(other_part, "w").astype(F32)).astype(BF16)

    parts = lax.all_to_all(forward(in_order(w, tokens, other_tokens, 0), gathered), TP, 0, 0)
    block = 2 * z + u
    here = 2 * block + w
    at = lambda x: lax.dynamic_slice_in_dim(x, here * own, own, 0)
    here_up = lax.dynamic_index_in_dim(up_blocks, here, 0, keepdims=False)
    here_rank = jnp.where(v == w, rank_activation, other_rank_activation)
    adapter = [
        lax.dot_general(here_rank, here_up[h], (((0,), (0,)), ((), ())), preferred_element_type=F32)
        for h in range(2)
    ]
    merged = jnp.sum(parts.astype(F32), axis=0) + jnp.concatenate(adapter, axis=1)
    output = cross((merged * at(scale)).astype(BF16))
    here_cotangent = lax.dynamic_slice_in_dim(
        jnp.where(v == w, own_cotangent, other_cotangent), block * own, own, 1
    ).astype(F32)
    mag_part = jnp.sum(here_cotangent * merged, axis=0) / at(norm)
    mags = spread(mag_part.reshape(2, 128), DP + ("v",))
    mags = mags.reshape(lax.axis_size("y"), 2, 4, 2, 128)
    mags = jnp.where(v == 0, mags[:, 0], mags[:, 1])
    grad_magnitude = jnp.sum(mags, axis=(0, 1)).reshape(-1) * factor
    return (output, input_gradient, grad_down, grad_up, grad_magnitude)


def solution(mesh):
    fine = Mesh(mesh.devices.reshape(8, 2, 2, 4, 2, 2), DP + TP)
    return jax.shard_map(
        on_device,
        mesh=fine,
        in_specs=(P(DP, TP), P(TP, DP), P(TP, None), P(None, TP), P(TP), P(DP, None)),
        out_specs=(P(DP, TP), P(DP, TP), P(TP, None), P(None, TP), P(TP)),
        check_vma=False,
    )
```

time: 185 us -> 178 us (0.962)
  waiting for transfers between devices: 73.7 us -> 56.3 us
  Pallas kernels: 24.5 us -> 10.2 us
  starting transfers between devices: 58.3 us -> 71.8 us
  other arithmetic: 2.11 us -> 11.7 us
    ppermute x0 -> x6, starting transfers between devices: none -> 15.9 us  [the longest x5 15.2 us: swap(): return lax.ppermute(x, axis, [(0, 1), (1, 0)])]
    pallas_call x2, Pallas kernels: 24.5 us -> 10.2 us  [the longest x1 5.36 us: backward(): pl.pallas_call(backward_kernel, grid=(n // step,), in_specs=[pl.BlockSpec...]
    all_to_all x4 -> x5, waiting for transfers between devices: 42.5 us -> 35.1 us  [spread(): lax.all_to_all(jnp.broadcast_to(block[None], (n,) + block.shape), axis, 0...]
    all_to_all x2, waiting for transfers between devices: 25.5 us -> 20.5 us  [the longest x1 10.2 us: on_device(): shares = lax.all_to_all(shares.reshape(n_dp, rows, 128), DP, 0, 0)]
    all_gather x1, waiting for transfers between devices: 4.97 us -> 0.02 us  [on_device(): gathered = lax.all_gather(frozen_matrix, ('y', 'c'), axis=0)]
    select_n x0 -> x6, other arithmetic: none -> 4.48 us  [the longest x2 2 us: in_order(): jnp.where(which == 0, jnp.concatenate([own, other], axis=axis), jnp.conca...]
    all_to_all x2, starting transfers between devices: 14.8 us -> 11.6 us  [the longest x1 7.02 us: on_device(): shares = lax.all_to_all(shares.reshape(n_dp, rows, 128), DP, 0, 0)]
    convert_element_type x2, other arithmetic: 0.03 us -> 2.68 us  [the longest x1 1.95 us: on_device(): (other_cotangent.astype(F32) * every_other(scale, w)).astype(BF16)]
  transfers between devices with their start and end apart: 7 -> 14, of which waited for: 5 -> 7; matrix products, arithmetic and copies ran while one was open for 5% -> 13% of each run, Pallas kernels for 13% -> 6%
where the time goes in v2:
time: 178 us; the launch traced here: 177 us
  starting transfers between devices  71.8 us (40%)
  waiting for transfers between devices  56.3 us (32%)
  between operations  14.6 us (8%)
  other arithmetic  11.7 us (7%)
  Pallas kernels  10.2 us (6%)
  local copies, waits for them, and re-layouts  9.14 us (5%)
  matrix products  3.72 us (2%)
    all_to_all x5, starting transfers between devices, spread(): lax.all_to_all(jnp.broadcast_to(block[None], (n,) + block.shape), axis, 0...  44.2 us
    all_to_all x5, waiting for transfers between devices, spread(): lax.all_to_all(jnp.broadcast_to(block[None], (n,) + block.shape), axis, 0...  35.1 us
    ppermute x5, starting transfers between devices, swap(): return lax.ppermute(x, axis, [(0, 1), (1, 0)])  15.2 us
    all_to_all x1, waiting for transfers between devices, on_device(): shares = lax.all_to_all(shares.reshape(n_dp, rows, 128), DP, 0, 0)  10.2 us
    all_to_all x1, waiting for transfers between devices, on_device(): lax.all_to_all(forward(in_order(w, tokens, other_tokens, 0), gathered), T...  10.2 us
    all_to_all x1, starting transfers between devices, on_device(): shares = lax.all_to_all(shares.reshape(n_dp, rows, 128), DP, 0, 0)  7.02 us
    pallas_call x1, Pallas kernels, backward(): pl.pallas_call(backward_kernel, grid=(n // step,), in_specs=[pl.BlockSpec...  5.36 us
    pallas_call x1, Pallas kernels, forward(): pl.pallas_call(forward_kernel, grid=(n // step,), in_specs=[pl.BlockSpec(...  4.83 us
  transfers between devices with their start and end apart: 14, of which 7 were waited for; matrix products, arithmetic and copies ran while one was open for 13% of the time, Pallas kernels for 6%

profile of v2, /device:TPU:1, one launch (start us, length us, event | category | flops | bytes accessed | tf_op | source)
XLA Modules:
  0.0 177.4 jit_solution(12520410094135974633)
XLA Ops:
  7.2 0.7 all-gather.3.cloned.1.call-update
  7.9 4.8 %collective-permute-start = (bf16[128,896]{1,0:T(8,128)(2,1)}, bf16[128,896]{1,0:T(8,128)(2,1)}, u32[]{:S(2)}, u32[]{:S(2)}) collective-permute-start(bf16[128,896]{1,0:T(8,128)(2,1)} %param.6), channel_id=1, source_target_pairs={{0,32},{32,0},{1,33},{33,1},{2,34},{34,2},{3,35},{35,3},{4,36},{36... | collective-permute-start | bytes 688136 | tf_op jit(solution)/shard_map/ppermute | solution.py:99
  12.8 1.2 convolution_convert_fusion.3
  14.0 0.1 pad.17.clone
  14.1 0.7 slice_select_fusion.1
  14.8 0.7 maximum_maximum_fusion
  15.5 0.9 broadcast_in_dim.19
  16.4 11.7 %all-to-all-start.1 = ((bf16[16,136,128]{2,1,0:T(8,128)(2,1)}), bf16[16,136,128]{2,1,0:T(8,128)(2,1)S(1)}, u32[]{:S(2)}, u32[]{:S(2)}) async-start(bf16[16,136,128]{2,1,0:T(8,128)(2,1)} %broadcast_in_dim.19), calls=%async_computation.1 | async-start | bytes 1114112 | tf_op jit(solution)/shard_map/all_to_all | solution.py:20
  28.1 0.8 copy.56
  29.2 16.3 %all-to-all-done.1 = bf16[16,136,128]{2,1,0:T(8,128)(2,1)S(1)} async-done(((bf16[16,136,128]{2,1,0:T(8,128)(2,1)}), bf16[16,136,128]{2,1,0:T(8,128)(2,1)S(1)}, u32[]{:S(2)}, u32[]{:S(2)}) %all-to-all-start.1) | async-done | bytes 557088 | tf_op jit(solution)/shard_map/all_to_all | solution.py:20
  45.4 0.8 slice_reduce_fusion
  46.3 1.3 fusion.2
  47.6 0.6 broadcast_in_dim.22
  48.2 5.9 %all-to-all-start.2 = ((f32[16,1,128]{2,1,0:T(1,128)}), f32[16,1,128]{2,1,0:T(1,128)S(1)}, u32[]{:S(2)}, u32[]{:S(2)}) async-start(f32[16,1,128]{2,1,0:T(1,128)} %broadcast_in_dim.22), calls=%async_computation.2 | async-start | bytes 16384 | tf_op jit(solution)/shard_map/all_to_all | solution.py:20
  54.1 0.9 broadcast_select_fusion
  55.0 1.9 %collective-permute-start.4 = (bf16[128,2048]{1,0:T(8,128)(2,1)}, bf16[128,2048]{1,0:T(8,128)(2,1)}, u32[]{:S(2)}, u32[]{:S(2)}) collective-permute-start(bf16[128,2048]{1,0:T(8,128)(2,1)} %broadcast_select_fusion), channel_id=1, source_target_pairs={{0,32},{32,0},{1,33},{33,1},{2,34},{34,2},{3,35},{35,3},{4,36},{36... | collective-permute-start | bytes 1572872 | tf_op jit(solution)/shard_map/ppermute | solution.py:99
  56.9 0.8 copy.60.a_ref
  57.8 5.1 %all-to-all-done.2 = f32[16,1,128]{2,1,0:T(1,128)S(1)} async-done(((f32[16,1,128]{2,1,0:T(1,128)}), f32[16,1,128]{2,1,0:T(1,128)S(1)}, u32[]{:S(2)}, u32[]{:S(2)}) %all-to-all-start.2) | async-done | bytes 8224 | tf_op jit(solution)/shard_map/all_to_all | solution.py:20
  62.9 0.6 broadcast_in_dim.23
  63.5 9.2 %all-to-all-start.3 = ((f32[32,1,128]{2,1,0:T(1,128)}), f32[32,1,128]{2,1,0:T(1,128)S(1)}, u32[]{:S(2)}, u32[]{:S(2)}) async-start(f32[32,1,128]{2,1,0:T(1,128)} %broadcast_in_dim.23), calls=%async_computation.3 | async-start | bytes 32768 | tf_op jit(solution)/shard_map/all_to_all | solution.py:20
  72.7 1.9 %maximum_select_fusion.1.x_ref = bf16[256,896]{1,0:T(8,128)(2,1)} fusion(bf16[128,896]{1,0:T(8,128)(2,1)} %collective-permute-done, bf16[128,896]{1,0:T(8,128)(2,1)S(1)} %copy-done.1, pred[]{:T(512)S(6)} %eq.20), kind=kLoop, calls=%fused_computation.15 | loop fusion | flops 2064384 | bytes 917505 | tf_op jit(solution)/shard_map/jit(_where)/select_n | solution.py:115
  74.6 2.1 %collective-permute-start.2 = (bf16[16,64,128]{2,1,0:T(8,128)(2,1)}, bf16[16,64,128]{2,1,0:T(8,128)(2,1)S(1)}, u32[]{:S(2)}, u32[]{:S(2)}) collective-permute-start(bf16[16,64,128]{2,1,0:T(8,128)(2,1)} %get-tuple-element.73), channel_id=1, source_target_pairs={{0,16},{16,0},{1,17},{17,1},{2,18},{18,2},{3,19},{19,3},{4,20},{20... | collective-permute-start | bytes 786440 | tf_op jit(solution)/shard_map/ppermute | solution.py:99
  76.8 3.4 %collective-permute-start.1 = (bf16[64,128]{1,0:T(8,128)(2,1)S(1)}, bf16[64,128]{1,0:T(8,128)(2,1)S(1)}, u32[]{:S(2)}, u32[]{:S(2)}) collective-permute-start(bf16[64,128]{1,0:T(8,128)(2,1)S(1)} %get-tuple-element.71), channel_id=1, source_target_pairs={{0,32},{32,0},{1,33},{33,1},{2,34},{34,2},{3,35},{35,3},{4,36},{36... | collective-permute-start | bytes 49160 | tf_op jit(solution)/shard_map/ppermute | solution.py:99
  80.2 0.2 all-to-all-done.3
  80.6 0.2 multiply_convert_fusion
  80.8 0.2 convolution_convert_fusion.1
  81.2 0.9 broadcast_select_fusion.1.g_ref
  82.1 0.1 fusion.27
  82.2 0.5 copy.58
  82.7 0.4 reshape.180
  83.1 0.4 convolution_convert_fusion.2.r_ref
  83.6 0.2 fusion.3
  83.8 0.1 fusion.17
  83.9 0.1 pad_maximum_fusion.1
  84.0 0.1 copy.62
  84.1 0.7 convert_element_type.71
  84.8 7.0 %all-to-all-start.4 = ((bf16[32,18,128]{2,1,0:T(8,128)(2,1)}), bf16[32,18,128]{2,1,0:T(8,128)(2,1)S(1)}, u32[]{:S(2)}, u32[]{:S(2)}) async-start(bf16[32,18,128]{2,1,0:T(8,128)(2,1)} %convert_element_type.71), calls=%async_computation.4 | async-start | bytes 393216 | tf_op jit(solution)/shard_map/all_to_all | solution.py:182
  91.9 0.1 constant_dynamic-update-slice_fusion.35
  92.0 10.2 %all-to-all-done.4 = bf16[32,18,128]{2,1,0:T(8,128)(2,1)S(1)} async-done(((bf16[32,18,128]{2,1,0:T(8,128)(2,1)}), bf16[32,18,128]{2,1,0:T(8,128)(2,1)S(1)}, u32[]{:S(2)}, u32[]{:S(2)}) %all-to-all-start.4) | async-done | bytes 147488 | tf_op jit(solution)/shard_map/all_to_all | solution.py:182
  102.3 0.7 broadcast_in_dim.48
  103.0 4.2 %all-to-all-start.5 = ((bf16[32,18,128]{2,1,0:T(8,128)(2,1)}), bf16[32,18,128]{2,1,0:T(8,128)(2,1)S(1)}, u32[]{:S(2)}, u32[]{:S(2)}) async-start(bf16[32,18,128]{2,1,0:T(8,128)(2,1)} %broadcast_in_dim.48), calls=%async_computation.5 | async-start | bytes 393216 | tf_op jit(solution)/shard_map/all_to_all | solution.py:20
  107.2 4.8 %forward.1 = bf16[16,128,256]{2,1,0:T(8,128)(2,1)} custom-call(bf16[256,896]{1,0:T(8,128)(2,1)} %maximum_select_fusion.1.x_ref, bf16[16,896,128]{2,1,0:T(8,128)(2,1)} %bitcast.44), custom_call_target="tpu_custom_call" | custom-call | flops 939524096 | bytes 3670016 | tf_op jit(solution)/shard_map/forward/pallas_call | solution.py:35
  112.1 5.5 %all-to-all-done.5 = bf16[32,18,128]{2,1,0:T(8,128)(2,1)S(1)} async-done(((bf16[32,18,128]{2,1,0:T(8,128)(2,1)}), bf16[32,18,128]{2,1,0:T(8,128)(2,1)S(1)}, u32[]{:S(2)}, u32[]{:S(2)}) %all-to-all-start.5) | async-done | bytes 147488 | tf_op jit(solution)/shard_map/all_to_all | solution.py:20
  117.6 4.6 %all-to-all-start = ((bf16[16,128,256]{2,1,0:T(8,128)(2,1)}), bf16[16,128,256]{2,1,0:T(8,128)(2,1)S(1)}, u32[]{:S(2)}, u32[]{:S(2)}) async-start(bf16[16,128,256]{2,1,0:T(8,128)(2,1)} %forward.1), calls=%async_computation | async-start | bytes 2097152 | tf_op jit(solution)/shard_map/all_to_all | solution.py:195
  122.1 1.9 %multiply_convert_fusion.1.h_ref = bf16[128,2048]{1,0:T(8,128)(2,1)} fusion(bf16[128,2048]{1,0:T(8,128)(2,1)} %collective-permute-done.4, f32[2048]{0:T(1024)S(1)} %broadcast_select_fusion.5), kind=kLoop, calls=%fused_computation.11 | loop fusion | flops 786432 | bytes 1056768 | tf_op jit(solution)/shard_map/convert_element_type | solution.py:189
  124.1 0.1 maximum_select_fusion
  124.2 0.2 fusion.7
  124.4 0.2 fusion.6
  124.6 0.1 fusion.16
  124.8 0.9 copy.65
  125.7 0.6 pad_maximum_fusion.2
  126.3 5.4 %backward.1 = (f32[128,896]{1,0:T(8,128)}, bf16[128,896]{1,0:T(8,128)(2,1)}) custom-call(bf16[128,2048]{1,0:T(8,128)(2,1)} %broadcast_select_fusion.1.g_ref, bf16[128,2048]{1,0:T(8,128)(2,1)} %multiply_convert_fusion.1.h_ref, bf16[16,896,128]{2,1,0:T(8,128)(2,1)} %bitcast.45, bf16[128,64]{1,0:T(8,128)(2,1)} %copy-done.6, bf16[896,64]{1,0:T(8,128)(2,1)} %copy.60.a_ref), custom_call_target="tpu_custom_call" | custom-call | flops 939524096 | bytes 3670016 | tf_op jit(solution)/shard_map/backward/pallas_call | solution.py:75
  131.7 3.0 %collective-permute-start.5 = (bf16[128,896]{1,0:T(8,128)(2,1)}, bf16[128,896]{1,0:T(8,128)(2,1)S(1)}, u32[]{:S(2)}, u32[]{:S(2)}) collective-permute-start(bf16[128,896]{1,0:T(8,128)(2,1)} %get-tuple-element.8), channel_id=1, source_target_pairs={{0,32},{32,0},{1,33},{33,1},{2,34},{34,2},{3,35},{35,3},{4,36},{36... | collective-permute-start | bytes 688136 | tf_op jit(solution)/shard_map/ppermute | solution.py:99
  134.6 10.2 %all-to-all-done = bf16[16,128,256]{2,1,0:T(8,128)(2,1)S(1)} async-done(((bf16[16,128,256]{2,1,0:T(8,128)(2,1)}), bf16[16,128,256]{2,1,0:T(8,128)(2,1)S(1)}, u32[]{:S(2)}, u32[]{:S(2)}) %all-to-all-start) | async-done | bytes 1048608 | tf_op jit(solution)/shard_map/all_to_all | solution.py:195
  144.9 0.1 convert_reduce_fusion
  145.0 0.9 multiply_reduce_fusion
  145.9 0.1 fusion.14
  146.0 0.7 broadcast_in_dim.50
  146.7 13.2 %all-to-all-start.6 = ((f32[64,2,128]{2,1,0:T(2,128)}), f32[64,2,128]{2,1,0:T(2,128)S(1)}, u32[]{:S(2)}, u32[]{:S(2)}) async-start(f32[64,2,128]{2,1,0:T(2,128)} %broadcast_in_dim.50), calls=%async_computation.6 | async-start | bytes 131072 | tf_op jit(solution)/shard_map/all_to_all | solution.py:20
  159.9 0.7 collective-permute-start.3
  160.6 0.7 add_convert_fusion
  161.3 8.0 %all-to-all-done.6 = f32[64,2,128]{2,1,0:T(2,128)S(1)} async-done(((f32[64,2,128]{2,1,0:T(2,128)}), f32[64,2,128]{2,1,0:T(2,128)S(1)}, u32[]{:S(2)}, u32[]{:S(2)}) %all-to-all-start.6) | async-done | bytes 65568 | tf_op jit(solution)/shard_map/all_to_all | solution.py:20
  169.3 0.6 multiply_bitcast_fusion
  169.9 0.6 copy.116
  (61 shorter events, 0.6 us)
Async XLA Ops:
  7.2 21.0 %copy-start.2 = (bf16[896,128]{1,0:T(8,128)(2,1)S(1)}, bf16[896,128]{1,0:T(8,128)(2,1)}, u32[]{:S(2)}) copy-start(bf16[896,128]{1,0:T(8,128)(2,1)} %param.7) | copy-start | bytes 688132
  7.2 21.8 %copy-start = (bf16[128,4096]{1,0:T(8,128)(2,1)S(1)}, bf16[128,4096]{1,0:T(8,128)(2,1)}, u32[]{:S(2)}) copy-start(bf16[128,4096]{1,0:T(8,128)(2,1)} %param.11) | copy-start | bytes 3145732
  7.2 100.0 %all-gather.3.cloned.1.call-start = ((), (), s32[]{:S(2)}) async-start(), calls=%async_computation.7 | async-start | bytes 3899392 | tf_op jit(solution)/shard_map/all_gather | solution.py:129
  7.9 64.8 %collective-permute-start = (bf16[128,896]{1,0:T(8,128)(2,1)}, bf16[128,896]{1,0:T(8,128)(2,1)}, u32[]{:S(2)}, u32[]{:S(2)}) collective-permute-start(bf16[128,896]{1,0:T(8,128)(2,1)} %param.6), channel_id=1, source_target_pairs={{0,32},{32,0},{1,33},{33,1},{2,34},{34,2},{3,35},{35,3},{4,36},{36... | collective-permute-start | bytes 688136 | tf_op jit(solution)/shard_map/ppermute | solution.py:99
  16.4 29.0 %all-to-all-start.1 = ((bf16[16,136,128]{2,1,0:T(8,128)(2,1)}), bf16[16,136,128]{2,1,0:T(8,128)(2,1)S(1)}, u32[]{:S(2)}, u32[]{:S(2)}) async-start(bf16[16,136,128]{2,1,0:T(8,128)(2,1)} %broadcast_in_dim.19), calls=%async_computation.1 | async-start | bytes 1114112 | tf_op jit(solution)/shard_map/all_to_all | solution.py:20
  28.1 18.1 %copy-start.5 = (bf16[896,64]{0,1:T(8,128)(2,1)S(1)}, bf16[896,64]{0,1:T(8,128)(2,1)}, u32[]{:S(2)}) copy-start(bf16[896,64]{0,1:T(8,128)(2,1)} %param.8) | copy-start | bytes 344068
  29.1 43.6 %copy-start.1 = (bf16[128,896]{1,0:T(8,128)(2,1)S(1)}, bf16[128,896]{1,0:T(8,128)(2,1)}, u32[]{:S(2)}) copy-start(bf16[128,896]{1,0:T(8,128)(2,1)} %param.6) | copy-start | bytes 688132
  29.1 51.4 %copy-start.3 = (bf16[128,2048]{1,0:T(8,128)(2,1)}, bf16[128,2048]{1,0:T(8,128)(2,1)S(1)}, u32[]{:S(2)}) copy-start(bf16[128,2048]{1,0:T(8,128)(2,1)S(1)} %get-tuple-element.40) | copy-start | bytes 1572868
  48.2 14.7 %all-to-all-start.2 = ((f32[16,1,128]{2,1,0:T(1,128)}), f32[16,1,128]{2,1,0:T(1,128)S(1)}, u32[]{:S(2)}, u32[]{:S(2)}) async-start(f32[16,1,128]{2,1,0:T(1,128)} %broadcast_in_dim.22), calls=%async_computation.2 | async-start | bytes 16384 | tf_op jit(solution)/shard_map/all_to_all | solution.py:20
  55.0 67.2 %collective-permute-start.4 = (bf16[128,2048]{1,0:T(8,128)(2,1)}, bf16[128,2048]{1,0:T(8,128)(2,1)}, u32[]{:S(2)}, u32[]{:S(2)}) collective-permute-start(bf16[128,2048]{1,0:T(8,128)(2,1)} %broadcast_select_fusion), channel_id=1, source_target_pairs={{0,32},{32,0},{1,33},{33,1},{2,34},{34,2},{3,35},{35,3},{4,36},{36... | collective-permute-start | bytes 1572872 | tf_op jit(solution)/shard_map/ppermute | solution.py:99
  63.5 17.0 %all-to-all-start.3 = ((f32[32,1,128]{2,1,0:T(1,128)}), f32[32,1,128]{2,1,0:T(1,128)S(1)}, u32[]{:S(2)}, u32[]{:S(2)}) async-start(f32[32,1,128]{2,1,0:T(1,128)} %broadcast_in_dim.23), calls=%async_computation.3 | async-start | bytes 32768 | tf_op jit(solution)/shard_map/all_to_all | solution.py:20
  74.6 7.5 %collective-permute-start.2 = (bf16[16,64,128]{2,1,0:T(8,128)(2,1)}, bf16[16,64,128]{2,1,0:T(8,128)(2,1)S(1)}, u32[]{:S(2)}, u32[]{:S(2)}) collective-permute-start(bf16[16,64,128]{2,1,0:T(8,128)(2,1)} %get-tuple-element.73), channel_id=1, source_target_pairs={{0,16},{16,0},{1,17},{17,1},{2,18},{18,2},{3,19},{19,3},{4,20},{20... | collective-permute-start | bytes 786440 | tf_op jit(solution)/shard_map/ppermute | solution.py:99
  76.8 47.4 %collective-permute-start.1 = (bf16[64,128]{1,0:T(8,128)(2,1)S(1)}, bf16[64,128]{1,0:T(8,128)(2,1)S(1)}, u32[]{:S(2)}, u32[]{:S(2)}) collective-permute-start(bf16[64,128]{1,0:T(8,128)(2,1)S(1)} %get-tuple-element.71), channel_id=1, source_target_pairs={{0,32},{32,0},{1,33},{33,1},{2,34},{34,2},{3,35},{35,3},{4,36},{36... | collective-permute-start | bytes 49160 | tf_op jit(solution)/shard_map/ppermute | solution.py:99
  83.5 28.5 %copy-start.6 = (bf16[128,64]{1,0:T(8,128)(2,1)}, bf16[128,64]{1,0:T(8,128)(2,1)S(1)}, u32[]{:S(2)}) copy-start(bf16[128,64]{1,0:T(8,128)(2,1)S(1)} %convolution_convert_fusion.2.r_ref) | copy-start | bytes 49156
  84.8 17.4 %all-to-all-start.4 = ((bf16[32,18,128]{2,1,0:T(8,128)(2,1)}), bf16[32,18,128]{2,1,0:T(8,128)(2,1)S(1)}, u32[]{:S(2)}, u32[]{:S(2)}) async-start(bf16[32,18,128]{2,1,0:T(8,128)(2,1)} %convert_element_type.71), calls=%async_computation.4 | async-start | bytes 393216 | tf_op jit(solution)/shard_map/all_to_all | solution.py:182
  103.0 14.6 %all-to-all-start.5 = ((bf16[32,18,128]{2,1,0:T(8,128)(2,1)}), bf16[32,18,128]{2,1,0:T(8,128)(2,1)S(1)}, u32[]{:S(2)}, u32[]{:S(2)}) async-start(bf16[32,18,128]{2,1,0:T(8,128)(2,1)} %broadcast_in_dim.48), calls=%async_computation.5 | async-start | bytes 393216 | tf_op jit(solution)/shard_map/all_to_all | solution.py:20
  117.6 27.3 %all-to-all-start = ((bf16[16,128,256]{2,1,0:T(8,128)(2,1)}), bf16[16,128,256]{2,1,0:T(8,128)(2,1)S(1)}, u32[]{:S(2)}, u32[]{:S(2)}) async-start(bf16[16,128,256]{2,1,0:T(8,128)(2,1)} %forward.1), calls=%async_computation | async-start | bytes 2097152 | tf_op jit(solution)/shard_map/all_to_all | solution.py:195
  131.7 28.9 %copy-start.4 = (f32[128,896]{1,0:T(8,128)S(1)}, f32[128,896]{1,0:T(8,128)}, u32[]{:S(2)}) copy-start(f32[128,896]{1,0:T(8,128)} %get-tuple-element.7) | copy-start | bytes 1376260
  131.7 28.9 %collective-permute-start.5 = (bf16[128,896]{1,0:T(8,128)(2,1)}, bf16[128,896]{1,0:T(8,128)(2,1)S(1)}, u32[]{:S(2)}, u32[]{:S(2)}) collective-permute-start(bf16[128,896]{1,0:T(8,128)(2,1)} %get-tuple-element.8), channel_id=1, source_target_pairs={{0,32},{32,0},{1,33},{33,1},{2,34},{34,2},{3,35},{35,3},{4,36},{36... | collective-permute-start | bytes 688136 | tf_op jit(solution)/shard_map/ppermute | solution.py:99
  146.7 22.6 %all-to-all-start.6 = ((f32[64,2,128]{2,1,0:T(2,128)}), f32[64,2,128]{2,1,0:T(2,128)S(1)}, u32[]{:S(2)}, u32[]{:S(2)}) async-start(f32[64,2,128]{2,1,0:T(2,128)} %broadcast_in_dim.50), calls=%async_computation.6 | async-start | bytes 131072 | tf_op jit(solution)/shard_map/all_to_all | solution.py:20
  159.9 1.4 collective-permute-start.3
Sparse Core Ops, SparseCore 0:
  10.1 49.9 all-gather.2

commit v3 on v2

v3 whole, which is shorter than its diff:
```python
import math

import jax
import jax.numpy as jnp
from jax import lax
from jax.experimental import pallas as pl
from jax.experimental.pallas import tpu as pltpu
from jax.sharding import Mesh
from jax.sharding import PartitionSpec as P

epsilon = 1e-06
F32 = jnp.float32
BF16 = jnp.bfloat16
DP = ("y", "w", "c")
TP = ("z", "u", "v")


def spread(block, axis):
    n = lax.axis_size(axis)
    return lax.all_to_all(jnp.broadcast_to(block[None], (n,) + block.shape), axis, 0, 0)


def forward_kernel(i_ref, x_ref, o_ref, a_ref, b_ref, c_ref, w_ref, *rest):
    u, v, w, c = (i_ref[k] for k in (0, 1, 3, 4))
    out, (x, r) = rest[:4], rest[4:]
    t = x_ref.shape[0]

    @pl.when(pl.program_id(0) == 0)
    def _():
        same = v == w
        x[:t] = jnp.where(same, x_ref[...], o_ref[...])
        x[t:] = jnp.where(same, o_ref[...], x_ref[...])
        r[...] = lax.dot_general(
            x[...], a_ref[...], (((1,), (1,)), ((), ())), preferred_element_type=F32
        ).astype(BF16)

    for k in range(2):
        at = (u + k) % 2
        b, d = b_ref[2 * at + w], c_ref[2 * at + w]
        up = jnp.concatenate([jnp.where(c == 0, b, d), jnp.where(c == 0, d, b)], axis=1)
        wide = jnp.concatenate([w_ref[2 * at], w_ref[2 * at + 1]], axis=1)
        y = jnp.dot(x[...], wide, preferred_element_type=F32)
        y = (y + jnp.dot(r[...], up, preferred_element_type=F32)).astype(BF16)
        out[2 * k][0] = y[:t]
        out[2 * k + 1][0] = y[t:]


def forward(place, x, other_x, down_t, up, other_up, gathered):
    t, f = x.shape
    n, rank = gathered.shape[0], down_t.shape[0]
    n_z = n // 4
    whole = lambda i, s: (0, 0)
    part = lambda i, s: (i, 0, 0)
    return pl.pallas_call(
        forward_kernel,
        grid_spec=pltpu.PrefetchScalarGridSpec(
            num_scalar_prefetch=1,
            grid=(n_z,),
            in_specs=[
                pl.BlockSpec((t, f), whole),
                pl.BlockSpec((t, f), whole),
                pl.BlockSpec((rank, f), whole),
                pl.BlockSpec((4, rank, 128), part),
                pl.BlockSpec((4, rank, 128), part),
                pl.BlockSpec((4, f, 128), part),
            ],
            out_specs=[pl.BlockSpec((1, t, 256), lambda i, s: ((i + n_z - s[2]) % n_z, 0, 0))] * 4,
            scratch_shapes=[pltpu.VMEM((2 * t, f), BF16), pltpu.VMEM((2 * t, rank), BF16)],
        ),
        out_shape=[jax.ShapeDtypeStruct((n_z, t, 256), BF16)] * 4,
        cost_estimate=pl.CostEstimate(
            flops=4 * t * f * n * 128, bytes_accessed=2 * f * n * 128, transcendentals=0
        ),
        name="forward",
    )(place, x, other_x, down_t, up, other_up, gathered)


def backward_kernel(i_ref, g_ref, h_ref, s_ref, w_ref, r_ref, a_ref, own_ref, other_ref, acc):
    i = pl.program_id(0)
    t = g_ref.shape[0]

    @pl.when(i == 0)
    def _():
        acc[:t] = jnp.dot(r_ref[...], a_ref[...], preferred_element_type=F32)
        acc[t:] = jnp.zeros_like(acc[t:])

    wide = jnp.concatenate([w_ref[0], w_ref[1]], axis=1)
    g = jnp.concatenate([g_ref[...], h_ref[...]], axis=0)
    g = (g.astype(F32) * s_ref[...]).astype(BF16)
    acc[...] += lax.dot_general(
        g, wide, (((1,), (1,)), ((), ())), preferred_element_type=F32
    )

    @pl.when(i == pl.num_programs(0) - 1)
    def _():
        own_ref[...] = acc[:t]
        other_ref[...] = acc[t:].astype(BF16)


def backward(place, cotangent, other_cotangent, scale, gathered, r, down_t):
    t = cotangent.shape[0]
    n, f, _ = gathered.shape
    whole = lambda i, s: (0, 0)
    mine = lambda i, s: (0, 2 * i + s[3])
    return pl.pallas_call(
        backward_kernel,
        grid_spec=pltpu.PrefetchScalarGridSpec(
            num_scalar_prefetch=1,
            grid=(n // 2,),
            in_specs=[
                pl.BlockSpec((t, 256), mine),
                pl.BlockSpec((t, 256), lambda i, s: (0, i)),
                pl.BlockSpec((1, 256), mine),
                pl.BlockSpec((2, f, 128), lambda i, s: (i, 0, 0)),
                pl.BlockSpec(r.shape, whole),
                pl.BlockSpec(down_t.shape, whole),
            ],
            out_specs=[pl.BlockSpec((t, f), whole)] * 2,
            scratch_shapes=[pltpu.VMEM((2 * t, f), F32)],
        ),
        out_shape=[
            jax.ShapeDtypeStruct((t, f), F32),
            jax.ShapeDtypeStruct((t, f), BF16),
        ],
        cost_estimate=pl.CostEstimate(
            flops=4 * t * f * n * 128, bytes_accessed=2 * f * n * 128, transcendentals=0
        ),
        name="backward",
    )(place, cotangent, other_cotangent, scale, gathered, r, down_t)


def swap(x, axis):
    return lax.ppermute(x, axis, [(0, 1), (1, 0)])


def cross(x):
    return lax.ppermute(x, ("w", "v"), [(0, 0), (1, 2), (2, 1), (3, 3)])


def every_other(x, which):
    n = x.shape[-1] // 256
    pick = lambda s: jnp.concatenate(
        [x[..., i * 256 : (i + 1) * 256] for i in range(s, n, 2)], axis=-1
    )
    return jnp.where(which == 0, pick(0), pick(1))


def in_order(which, own, other, axis):
    return jnp.where(
        which == 0,
        jnp.concatenate([own, other], axis=axis),
        jnp.concatenate([other, own], axis=axis),
    )


def second_kernel(i_ref, w_ref, a_ref, b_ref, x_ref, o_ref):
    rank = a_ref.shape[0]
    whole = w_ref[...].astype(F32) + lax.dot_general(
        a_ref[...], b_ref[0, :rank], (((0,), (0,)), ((), ())), preferred_element_type=F32
    )
    left = jnp.sum(whole * whole, axis=0, keepdims=True)
    pieces = []
    for _ in range(3):
        pieces.append(left.astype(BF16))
        left = left - pieces[-1].astype(F32)
    pieces.append(jnp.zeros((5, 128), BF16))
    r = lax.dot_general(
        a_ref[...], x_ref[...], (((1,), (1,)), ((), ())), preferred_element_type=F32
    )
    o_ref[...] = jnp.concatenate([r.astype(BF16)] + pieces, axis=0)


def second_block(index, w, down_t, first, tokens):
    rows, (rank, f) = first.shape[1], down_t.shape
    whole = lambda i, s: (0, 0)
    return pl.pallas_call(
        second_kernel,
        grid_spec=pltpu.PrefetchScalarGridSpec(
            num_scalar_prefetch=1,
            grid=(1,),
            in_specs=[
                pl.BlockSpec(w.shape, whole),
                pl.BlockSpec(down_t.shape, whole),
                pl.BlockSpec((1, rows, 128), lambda i, s: (s[0], 0, 0)),
                pl.BlockSpec(tokens.shape, whole),
            ],
            out_specs=pl.BlockSpec((rank + 8, 128), whole),
        ),
        out_shape=jax.ShapeDtypeStruct((rank + 8, 128), BF16),
        name="second_block",
    )(index.reshape(1), w, down_t, first, tokens)


def on_device(tokens, frozen_matrix, adapter_down_factor, adapter_up_factor, magnitude, cotangent):
    t, f = tokens.shape
    n_dp, n_tp = lax.axis_size(DP), lax.axis_size(TP)
    y, w, c, z, u, v = (lax.axis_index(a) for a in DP + TP)
    rank, own = adapter_up_factor.shape
    down_t = adapter_down_factor.T
    place = jnp.stack([u, v, z, w, c])
    tie = lax.optimization_barrier

    gathered = lax.all_gather(frozen_matrix, ("y", "c"), axis=0)

    first = jnp.concatenate(
        [
            jnp.where(c == 0, adapter_up_factor[:, :128], adapter_up_factor[:, 128:]),
            magnitude.reshape(2, 128),
            jnp.zeros((6, 128), BF16),
        ],
        axis=0,
    )
    first = spread(first, TP)
    cotangent_out = every_other(cotangent, 1 - w)
    cotangent_out, tokens_out = tie((cotangent_out, tokens))
    other_tokens = swap(tokens_out, "w")

    second = second_block(2 * y + w, frozen_matrix, down_t, first, tokens)
    second, cotangent_out, first = tie((second, cotangent_out, first))
    second = spread(second, TP).astype(F32)
    rank_activation = jnp.sum(second[:, :rank], axis=0).astype(BF16)
    squares = jnp.sum(second[:, rank : rank + 3], axis=(0, 1)).reshape(1, 128)
    own_half = first[:, :rank]
    other_half = swap(own_half, "c")
    full_magnitude = first[:, rank : rank + 2].reshape(-1)
    up_blocks = in_order(c, own_half[:, None], other_half[:, None], 1)
    full_up = jnp.moveaxis(up_blocks, 2, 0).reshape(rank, -1)

    squares = spread(squares, DP)
    other_cotangent = swap(cotangent_out, "w")
    outgoing = forward(place, tokens, other_tokens, down_t, own_half, other_half, gathered)
    squares, outgoing = tie((squares, outgoing))
    received = [
        lax.ppermute(outgoing[k], ("u", "v"), [(i, i ^ k) for i in range(4)]) for k in (1, 2, 3)
    ]
    along_x = sum((r.astype(F32) for r in received), outgoing[0].astype(F32))
    n_z = lax.axis_size("z")
    along_z = [along_x[0]] + [
        lax.ppermute(
            along_x[k].astype(BF16), "z", [(i, (i + k) % n_z) for i in range(n_z)]
        ).astype(F32)
        for k in range(1, n_z)
    ]

    norm = jnp.sqrt(squares.reshape(-1) + epsilon)
    scale = full_magnitude.astype(F32) / norm
    scaled = (cotangent.astype(F32) * scale).astype(BF16)
    rank_back = lax.dot_general(
        scaled, full_up, (((1,), (1,)), ((), ())), preferred_element_type=F32
    ).astype(BF16)
    down = lax.dot_general(
        rank_back, tokens, (((0,), (0,)), ((), ())), preferred_element_type=F32
    )
    q = (2 * z + u) * 2 + v
    up = jnp.dot(
        rank_activation,
        lax.dynamic_slice_in_dim(scaled, q * own, own, 1),
        preferred_element_type=F32,
    )
    columns = [down[:, i : i + 128] for i in range(0, f, 128)]
    columns += [up[:, i : i + 128] for i in range(0, own, 128)]
    shares = jnp.concatenate(columns, axis=0).astype(BF16)
    shares = lax.all_to_all(shares.reshape(n_dp, -1, 128), DP, 0, 0)
    shares = jnp.sum(shares.astype(F32), axis=0).astype(BF16)

    block = 2 * z + u
    here = 2 * block + w
    at = lambda x: lax.dynamic_slice_in_dim(x, here * own, own, 0)
    merged = sum(along_z[1:], along_z[0])
    here_cotangent = jnp.where(
        v == w,
        lax.dynamic_slice_in_dim(cotangent, here * own, own, 1),
        lax.dynamic_slice_in_dim(other_cotangent, block * own, own, 1),
    ).astype(F32)
    mag_part = jnp.sum(here_cotangent * merged, axis=0) / at(norm)

    rows = shares.shape[0]
    high = lax.reduce_precision(mag_part, 8, 7)
    last = jnp.concatenate(
        [
            shares,
            high.astype(BF16).reshape(2, 128),
            (mag_part - high).astype(BF16).reshape(2, 128),
        ],
        axis=0,
    )
    last, merged, rank_back = tie((last, merged, rank_back))
    last = spread(last, DP + ("v",)).reshape(n_dp // 4, 2, 2, 2, rows + 4, 128)
    factor = 1.0 / math.sqrt(t * n_dp)
    sums = jnp.where(v == 0, last[:, :, :, 0, :rows], last[:, :, :, 1, :rows])
    sums = sums.astype(F32).reshape(-1, rank, 128) * factor
    grad_down = jnp.concatenate([sums[i] for i in range(f // 128)], axis=1).T
    grad_up = jnp.concatenate([sums[i] for i in range(f // 128, sums.shape[0])], axis=1)
    mags = jnp.where(v == 0, last[:, 0, :, :, rows:], last[:, 1, :, :, rows:]).astype(F32)
    mags = jnp.sum(mags, axis=(0, 1, 2))
    grad_magnitude = (mags[:2] + mags[2:]).reshape(-1) * factor

    output = cross((merged * at(scale)).astype(BF16))
    own_part, other_part = backward(
        place, cotangent, other_cotangent, scale.reshape(1, -1), gathered, rank_back, down_t
    )
    input_gradient = (own_part + swap(other_part, "w").astype(F32)).astype(BF16)
    return (output, input_gradient, grad_down, grad_up, grad_magnitude)


def solution(mesh):
    fine = Mesh(mesh.devices.reshape(8, 2, 2, 4, 2, 2), DP + TP)
    return jax.shard_map(
        on_device,
        mesh=fine,
        in_specs=(P(DP, TP), P(TP, DP), P(TP, None), P(None, TP), P(TP), P(DP, None)),
        out_specs=(P(DP, TP), P(DP, TP), P(TP, None), P(None, TP), P(TP)),
        check_vma=False,
    )
```

time: 178 us -> 159 us (0.89)
  waiting for transfers between devices: 56.3 us -> 18.1 us
  starting transfers between devices: 71.8 us -> 85.9 us
  Pallas kernels: 10.2 us -> 16.2 us
  local copies, waits for them, and re-layouts: 9.14 us -> 12.8 us
  other arithmetic: 11.7 us -> 8.46 us
  matrix products: 3.72 us -> 0.77 us
    all_to_all x5 -> x4, waiting for transfers between devices: 35.1 us -> 7.82 us  [spread(): lax.all_to_all(jnp.broadcast_to(block[None], (n,) + block.shape), axis, 0...]
    ppermute x0 -> x6, starting transfers between devices: none -> 24 us  [the longest x3 14.4 us: on_device(): lax.ppermute(along_x[k].astype(BF16), 'z', [(i, (i + k) % n_z) for i in r...]
    all_to_all x2 -> x1, waiting for transfers between devices: 20.5 us -> 0.01 us  [on_device(): shares = lax.all_to_all(shares.reshape(n_dp, -1, 128), DP, 0, 0)]
    pallas_call x2 -> x3, Pallas kernels: 10.2 us -> 16.2 us  [the longest x1 8.11 us: backward(): pl.pallas_call(backward_kernel, grid_spec=pltpu.PrefetchScalarGridSpec(nu...]
    ppermute x5 -> x4, waiting for transfers between devices: 0.01 us -> 5.08 us  [swap(): return lax.ppermute(x, axis, [(0, 1), (1, 0)])]
    ppermute x0 -> x6, waiting for transfers between devices: none -> 4.51 us  [the longest x3 2.58 us: on_device(): lax.ppermute(outgoing[k], ('u', 'v'), [(i, i ^ k) for i in range(4)])]
    all_to_all x5 -> x4, starting transfers between devices: 44.2 us -> 40.3 us  [spread(): lax.all_to_all(jnp.broadcast_to(block[None], (n,) + block.shape), axis, 0...]
    all_to_all x2 -> x1, starting transfers between devices: 11.6 us -> 8.3 us  [on_device(): shares = lax.all_to_all(shares.reshape(n_dp, -1, 128), DP, 0, 0)]
  transfers between devices with their start and end apart: 14 -> 17, of which waited for: 7 -> 5; matrix products, arithmetic and copies ran while one was open for 13% -> 10% of each run, Pallas kernels for 6% -> 10%
where the time goes in v3:
time: 159 us; the launch traced here: 157 us
  starting transfers between devices  85.9 us (54%)
  waiting for transfers between devices  18.1 us (11%)
  Pallas kernels  16.2 us (10%)
  between operations  14.7 us (9%)
  local copies, waits for them, and re-layouts  12.8 us (8%)
  other arithmetic  8.46 us (5%)
    all_to_all x4, starting transfers between devices, spread(): lax.all_to_all(jnp.broadcast_to(block[None], (n,) + block.shape), axis, 0...  40.3 us
    ppermute x3, starting transfers between devices, on_device(): lax.ppermute(along_x[k].astype(BF16), 'z', [(i, (i + k) % n_z) for i in r...  14.4 us
    ppermute x4, starting transfers between devices, swap(): return lax.ppermute(x, axis, [(0, 1), (1, 0)])  12.7 us
    ppermute x3, starting transfers between devices, on_device(): lax.ppermute(outgoing[k], ('u', 'v'), [(i, i ^ k) for i in range(4)])  9.58 us
    all_to_all x1, starting transfers between devices, on_device(): shares = lax.all_to_all(shares.reshape(n_dp, -1, 128), DP, 0, 0)  8.3 us
    pallas_call x1, Pallas kernels, backward(): pl.pallas_call(backward_kernel, grid_spec=pltpu.PrefetchScalarGridSpec(nu...  8.11 us
    all_to_all x4, waiting for transfers between devices, spread(): lax.all_to_all(jnp.broadcast_to(block[None], (n,) + block.shape), axis, 0...  7.82 us
    pallas_call x1, Pallas kernels, forward(): pl.pallas_call(forward_kernel, grid_spec=pltpu.PrefetchScalarGridSpec(num...  6.06 us
  transfers between devices with their start and end apart: 17, of which 5 were waited for; matrix products, arithmetic and copies ran while one was open for 10% of the time, Pallas kernels for 10%

profile of v3, /device:TPU:1, one launch (start us, length us, event | category | flops | bytes accessed | tf_op | source)
XLA Modules:
  0.0 156.9 jit_solution(261389204971367159)
XLA Ops:
  7.2 0.0 all-gather.3.cloned.1.call-start
  7.2 0.7 all-gather.3.cloned.1.call-update
  7.9 0.1 pad.11.clone
  8.0 0.7 slice_select_fusion
  8.7 0.7 maximum_maximum_fusion
  9.5 0.8 broadcast_in_dim.15
  10.3 13.4 %all-to-all-start = ((bf16[16,72,128]{2,1,0:T(8,128)(2,1)}), bf16[16,72,128]{2,1,0:T(8,128)(2,1)S(1)}, u32[]{:S(2)}, u32[]{:S(2)}) async-start(bf16[16,72,128]{2,1,0:T(8,128)(2,1)} %broadcast_in_dim.15), calls=%async_computation | async-start | bytes 589824 | tf_op jit(solution)/shard_map/all_to_all | solution.py:20
  23.7 0.9 constant_dynamic-update-slice_fusion.15
  24.6 0.9 constant_dynamic-update-slice_fusion.14
  25.5 0.9 constant_dynamic-update-slice_fusion.13
  26.5 0.9 broadcast_select_fusion
  27.3 6.9 %all-to-all-done.b_ref = bf16[16,72,128]{2,1,0:T(8,128)(2,1)S(1)} async-done(((bf16[16,72,128]{2,1,0:T(8,128)(2,1)}), bf16[16,72,128]{2,1,0:T(8,128)(2,1)S(1)}, u32[]{:S(2)}, u32[]{:S(2)}) %all-to-all-start) | async-done | bytes 294944 | tf_op jit(solution)/shard_map/all_to_all | solution.py:20
  34.2 0.7 copy-done.1
  34.9 2.1 %second_block.1 = bf16[72,128]{1,0:T(8,128)(2,1)} custom-call(s32[1]{0:T(128)} %bitcast.i_ref, bf16[896,128]{1,0:T(8,128)(2,1)} %w_ref.1, bf16[64,896]{1,0:T(8,128)(2,1)} %bitcast.87, bf16[16,72,128]{2,1,0:T(8,128)(2,1)} %copy-done.1, bf16[128,896]{1,0:T(8,128)(2,1)} %x_ref.3), custom_call_target="tpu_custom_call" | custom-call | tf_op jit(solution)/shard_map/second_block/pallas_call | solution.py:176
  37.0 1.5 broadcast_in_dim.16
  38.5 5.4 %all-to-all-start.1 = ((bf16[16,72,128]{2,1,0:T(8,128)(2,1)}), bf16[16,72,128]{2,1,0:T(8,128)(2,1)S(1)}, u32[]{:S(2)}, u32[]{:S(2)}) async-start(bf16[16,72,128]{2,1,0:T(8,128)(2,1)} %broadcast_in_dim.16), calls=%async_computation.1 | async-start | bytes 589824 | tf_op jit(solution)/shard_map/all_to_all | solution.py:20
  43.9 1.1 slice_bitcast_fusion.13
  45.0 4.1 %collective-permute-start.1 = (bf16[16,64,128]{2,1,0:T(8,128)(2,1)S(1)}, bf16[16,64,128]{2,1,0:T(8,128)(2,1)S(1)}, u32[]{:S(2)}, u32[]{:S(2)}) collective-permute-start(bf16[16,64,128]{2,1,0:T(8,128)(2,1)S(1)} %get-tuple-element.70.b_ref), channel_id=1, source_target_pairs={{0,16},{16,0},{1,17},{17,1},{2,18},{18,2},{3,19},{19,3},{4,20},{20... | collective-permute-start | bytes 786440 | tf_op jit(solution)/shard_map/ppermute | solution.py:133
  49.1 3.0 %collective-permute-start = (bf16[128,896]{1,0:T(8,128)(2,1)S(1)}, bf16[128,896]{1,0:T(8,128)(2,1)S(1)}, u32[]{:S(2)}, u32[]{:S(2)}) collective-permute-start(bf16[128,896]{1,0:T(8,128)(2,1)S(1)} %copy-done.2), channel_id=1, source_target_pairs={{0,32},{32,0},{1,33},{33,1},{2,34},{34,2},{3,35},{35,3},{4,36},{36... | collective-permute-start | bytes 688136 | tf_op jit(solution)/shard_map/ppermute | solution.py:133
  52.1 0.6 stack.23.i_ref
  52.7 2.3 %collective-permute-start.2 = (bf16[128,2048]{1,0:T(8,128)(2,1)}, bf16[128,2048]{1,0:T(8,128)(2,1)}, u32[]{:S(2)}, u32[]{:S(2)}) collective-permute-start(bf16[128,2048]{1,0:T(8,128)(2,1)} %broadcast_select_fusion), channel_id=1, source_target_pairs={{0,32},{32,0},{1,33},{33,1},{2,34},{34,2},{3,35},{35,3},{4,36},{36... | collective-permute-start | bytes 1572872 | tf_op jit(solution)/shard_map/ppermute | solution.py:133
  55.0 0.8 slice_convert_fusion
  55.8 0.1 fusion
  55.9 0.5 copy.25
  56.4 0.4 reshape.99
  56.9 0.6 broadcast_in_dim.17
  57.5 10.2 %all-to-all-start.2 = ((f32[32,1,128]{2,1,0:T(1,128)}), f32[32,1,128]{2,1,0:T(1,128)S(1)}, u32[]{:S(2)}, u32[]{:S(2)}) async-start(f32[32,1,128]{2,1,0:T(1,128)} %broadcast_in_dim.17), calls=%async_computation.2 | async-start | bytes 32768 | tf_op jit(solution)/shard_map/all_to_all | solution.py:20
  67.8 0.0 all-gather.3.cloned.1.call-done
  67.9 0.7 copy-done.8
  68.5 6.1 %forward.1 = (bf16[4,128,256]{2,1,0:T(8,128)(2,1)}, bf16[4,128,256]{2,1,0:T(8,128)(2,1)}, bf16[4,128,256]{2,1,0:T(8,128)(2,1)}, bf16[4,128,256]{2,1,0:T(8,128)(2,1)}) custom-call(s32[5]{0:T(128)} %stack.23.i_ref, bf16[128,896]{1,0:T(8,128)(2,1)} %x_ref.3, bf16[128,896]{1,0:T(8,128)(2,1)} %copy-done.8, bf16[64,896]{1,0:T(8,128)(2,1)} %bitcast.88, ...), custom_call_target="tpu_custom_call" | custom-call | flops 939524096 | bytes 3670016 | tf_op jit(solution)/shard_map/forward/pallas_call | solution.py:54
  74.6 0.9 all-to-all-done.2
  75.6 2.0 %collective-permute-start.3 = (bf16[4,128,256]{2,1,0:T(8,128)(2,1)}, bf16[4,128,256]{2,1,0:T(8,128)(2,1)S(1)}, u32[]{:S(2)}, u32[]{:S(2)}) collective-permute-start(bf16[4,128,256]{2,1,0:T(8,128)(2,1)} %get-tuple-element.35), channel_id=1, source_target_pairs={{0,1},{1,0},{2,3},{3,2},{4,5},{5,4},{6,7},{7,6},{8,9},{9,8},{10,11... | collective-permute-start | bytes 786440 | tf_op jit(solution)/shard_map/ppermute | solution.py:234
  77.6 4.3 %collective-permute-start.4 = (bf16[4,128,256]{2,1,0:T(8,128)(2,1)}, bf16[4,128,256]{2,1,0:T(8,128)(2,1)S(1)}, u32[]{:S(2)}, u32[]{:S(2)}) collective-permute-start(bf16[4,128,256]{2,1,0:T(8,128)(2,1)} %get-tuple-element.36), channel_id=1, source_target_pairs={{0,2},{1,3},{2,0},{3,1},{4,6},{5,7},{6,4},{7,5},{8,10},{9,11},{10,... | collective-permute-start | bytes 786440 | tf_op jit(solution)/shard_map/ppermute | solution.py:234
  81.9 3.3 %collective-permute-start.5 = (bf16[4,128,256]{2,1,0:T(8,128)(2,1)}, bf16[4,128,256]{2,1,0:T(8,128)(2,1)S(1)}, u32[]{:S(2)}, u32[]{:S(2)}) collective-permute-start(bf16[4,128,256]{2,1,0:T(8,128)(2,1)} %get-tuple-element.37), channel_id=1, source_target_pairs={{0,3},{1,2},{2,1},{3,0},{4,7},{5,6},{6,5},{7,4},{8,11},{9,10},{10,... | collective-permute-start | bytes 786440 | tf_op jit(solution)/shard_map/ppermute | solution.py:234
  85.2 0.2 multiply_convert_fusion
  85.4 0.4 convolution_convert_fusion.1.r_ref
  85.9 0.2 convolution_convert_fusion
  86.2 0.1 convolution_convert_fusion.2
  86.3 0.7 convert_element_type.108
  87.1 8.3 %all-to-all-start.3 = ((bf16[32,18,128]{2,1,0:T(8,128)(2,1)}), bf16[32,18,128]{2,1,0:T(8,128)(2,1)S(1)}, u32[]{:S(2)}, u32[]{:S(2)}) async-start(bf16[32,18,128]{2,1,0:T(8,128)(2,1)} %convert_element_type.108), calls=%async_computation.3 | async-start | bytes 393216 | tf_op jit(solution)/shard_map/all_to_all | solution.py:263
  95.4 2.6 %collective-permute-done.5 = bf16[4,128,256]{2,1,0:T(8,128)(2,1)S(1)} collective-permute-done((bf16[4,128,256]{2,1,0:T(8,128)(2,1)}, bf16[4,128,256]{2,1,0:T(8,128)(2,1)S(1)}, u32[]{:S(2)}, u32[]{:S(2)}) %collective-permute-start.5) | collective-permute-done | bytes 262176 | tf_op jit(solution)/shard_map/ppermute | solution.py:234
  98.0 0.1 fusion.11
  98.1 4.0 %collective-permute-start.6 = (bf16[128,256]{1,0:T(8,128)(2,1)S(1)}, bf16[128,256]{1,0:T(8,128)(2,1)S(1)}, u32[]{:S(2)}, u32[]{:S(2)}) collective-permute-start(bf16[128,256]{1,0:T(8,128)(2,1)S(1)} %get-tuple-element.71), channel_id=1, source_target_pairs={{0,4},{4,8},{8,12},{12,0},{1,5},{5,9},{9,13},{13,1},{2,6},{6,10},{... | collective-permute-start | bytes 196616 | tf_op jit(solution)/shard_map/ppermute | solution.py:239
  102.1 3.4 %collective-permute-start.8 = (bf16[128,256]{1,0:T(8,128)(2,1)S(1)}, bf16[128,256]{1,0:T(8,128)(2,1)S(1)}, u32[]{:S(2)}, u32[]{:S(2)}) collective-permute-start(bf16[128,256]{1,0:T(8,128)(2,1)S(1)} %get-tuple-element.72), channel_id=1, source_target_pairs={{0,12},{4,0},{8,4},{12,8},{1,13},{5,1},{9,5},{13,9},{2,14},{6,2},{... | collective-permute-start | bytes 196616 | tf_op jit(solution)/shard_map/ppermute | solution.py:239
  105.5 7.0 %collective-permute-start.7 = (bf16[128,256]{1,0:T(8,128)(2,1)S(1)}, bf16[128,256]{1,0:T(8,128)(2,1)S(1)}, u32[]{:S(2)}, u32[]{:S(2)}) collective-permute-start(bf16[128,256]{1,0:T(8,128)(2,1)S(1)} %get-tuple-element.73), channel_id=1, source_target_pairs={{0,8},{4,12},{8,0},{12,4},{1,9},{5,13},{9,1},{13,5},{2,10},{6,14},... | collective-permute-start | bytes 196616 | tf_op jit(solution)/shard_map/ppermute | solution.py:239
  112.6 0.1 reduce_sum.50
  112.6 1.9 %collective-permute-done.7 = bf16[128,256]{1,0:T(8,128)(2,1)S(1)} collective-permute-done((bf16[128,256]{1,0:T(8,128)(2,1)S(1)}, bf16[128,256]{1,0:T(8,128)(2,1)S(1)}, u32[]{:S(2)}, u32[]{:S(2)}) %collective-permute-start.7) | collective-permute-done | bytes 65568 | tf_op jit(solution)/shard_map/ppermute | solution.py:239
  114.6 0.9 multiply_reduce_fusion
  115.5 0.1 fusion.9
  115.6 0.8 broadcast_in_dim.40
  116.4 11.2 %all-to-all-start.4 = ((bf16[64,22,128]{2,1,0:T(8,128)(2,1)}), bf16[64,22,128]{2,1,0:T(8,128)(2,1)S(1)}, u32[]{:S(2)}, u32[]{:S(2)}) async-start(bf16[64,22,128]{2,1,0:T(8,128)(2,1)} %broadcast_in_dim.40), calls=%async_computation.4 | async-start | bytes 786432 | tf_op jit(solution)/shard_map/all_to_all | solution.py:20
  127.6 0.6 bitcast_multiply_fusion.s_ref
  128.2 8.1 %backward.1 = (f32[128,896]{1,0:T(8,128)}, bf16[128,896]{1,0:T(8,128)(2,1)}) custom-call(s32[5]{0:T(128)} %stack.23.i_ref, bf16[128,4096]{1,0:T(8,128)(2,1)} %g_ref.1, bf16[128,2048]{1,0:T(8,128)(2,1)} %collective-permute-done.2.h_ref, f32[1,4096]{1,0:T(1,128)} %bitcast_multiply_fusion.s_ref, bf16[16,896,128]{2,1,0:T(8,128)(2,1)} %bitcast.83, ...), custom_call_target="tpu_custom_call" | custom-call | flops 939524096 | bytes 3670016 | tf_op jit(solution)/shard_map/backward/pallas_call | solution.py:105
  136.3 3.3 %collective-permute-start.10 = (bf16[128,896]{1,0:T(8,128)(2,1)}, bf16[128,896]{1,0:T(8,128)(2,1)S(1)}, u32[]{:S(2)}, u32[]{:S(2)}) collective-permute-start(bf16[128,896]{1,0:T(8,128)(2,1)} %get-tuple-element.41), channel_id=1, source_target_pairs={{0,32},{32,0},{1,33},{33,1},{2,34},{34,2},{3,35},{35,3},{4,36},{36... | collective-permute-start | bytes 688136 | tf_op jit(solution)/shard_map/ppermute | solution.py:133
  139.6 0.7 collective-permute-start.9
  140.3 5.1 %collective-permute-done.10 = bf16[128,896]{1,0:T(8,128)(2,1)S(1)} collective-permute-done((bf16[128,896]{1,0:T(8,128)(2,1)}, bf16[128,896]{1,0:T(8,128)(2,1)S(1)}, u32[]{:S(2)}, u32[]{:S(2)}) %collective-permute-start.10) | collective-permute-done | bytes 229408 | tf_op jit(solution)/shard_map/ppermute | solution.py:133
  145.4 1.7 %add_convert_fusion = bf16[128,896]{1,0:T(8,128)(2,1)} fusion(f32[128,896]{1,0:T(8,128)} %get-tuple-element.40, bf16[128,896]{1,0:T(8,128)(2,1)S(1)} %collective-permute-done.10), kind=kLoop, calls=%fused_computation.9 | loop fusion | flops 344064 | bytes 917504 | tf_op jit(solution)/shard_map/convert_element_type | solution.py:302
  147.2 0.1 copy.27
  147.2 0.6 fusion.12
  147.9 0.1 convert_reduce_fusion
  148.0 0.1 copy.30
  148.1 0.6 multiply_bitcast_fusion
  148.8 0.7 pad_maximum_fusion
  149.4 0.6 copy.68
  (63 shorter events, 0.5 us)
Async XLA Ops:
  7.2 19.2 %copy-start = (bf16[128,4096]{1,0:T(8,128)(2,1)S(1)}, bf16[128,4096]{1,0:T(8,128)(2,1)}, u32[]{:S(2)}) copy-start(bf16[128,4096]{1,0:T(8,128)(2,1)} %g_ref.1) | copy-start | bytes 3145732
  7.2 60.7 %all-gather.3.cloned.1.call-start = ((), (), s32[]{:S(2)}) async-start(), calls=%async_computation.5 | async-start | bytes 3899392 | tf_op jit(solution)/shard_map/all_gather | solution.py:203
  10.3 24.0 %all-to-all-start = ((bf16[16,72,128]{2,1,0:T(8,128)(2,1)}), bf16[16,72,128]{2,1,0:T(8,128)(2,1)S(1)}, u32[]{:S(2)}, u32[]{:S(2)}) async-start(bf16[16,72,128]{2,1,0:T(8,128)(2,1)} %broadcast_in_dim.15), calls=%async_computation | async-start | bytes 589824 | tf_op jit(solution)/shard_map/all_to_all | solution.py:20
  26.5 22.6 %copy-start.2 = (bf16[128,896]{1,0:T(8,128)(2,1)S(1)}, bf16[128,896]{1,0:T(8,128)(2,1)}, u32[]{:S(2)}) copy-start(bf16[128,896]{1,0:T(8,128)(2,1)} %x_ref.3) | copy-start | bytes 688132
  34.2 0.7 copy-start.1
  38.5 18.4 %all-to-all-start.1 = ((bf16[16,72,128]{2,1,0:T(8,128)(2,1)}), bf16[16,72,128]{2,1,0:T(8,128)(2,1)S(1)}, u32[]{:S(2)}, u32[]{:S(2)}) async-start(bf16[16,72,128]{2,1,0:T(8,128)(2,1)} %broadcast_in_dim.16), calls=%async_computation.1 | async-start | bytes 589824 | tf_op jit(solution)/shard_map/all_to_all | solution.py:20
  45.0 22.8 %copy-start.4 = (bf16[16,64,128]{2,1,0:T(8,128)(2,1)}, bf16[16,64,128]{2,1,0:T(8,128)(2,1)S(1)}, u32[]{:S(2)}) copy-start(bf16[16,64,128]{2,1,0:T(8,128)(2,1)S(1)} %get-tuple-element.70.b_ref) | copy-start | bytes 786436
  45.0 10.8 %collective-permute-start.1 = (bf16[16,64,128]{2,1,0:T(8,128)(2,1)S(1)}, bf16[16,64,128]{2,1,0:T(8,128)(2,1)S(1)}, u32[]{:S(2)}, u32[]{:S(2)}) collective-permute-start(bf16[16,64,128]{2,1,0:T(8,128)(2,1)S(1)} %get-tuple-element.70.b_ref), channel_id=1, source_target_pairs={{0,16},{16,0},{1,17},{17,1},{2,18},{18,2},{3,19},{19,3},{4,20},{20... | collective-permute-start | bytes 786440 | tf_op jit(solution)/shard_map/ppermute | solution.py:133
  49.1 18.7 %collective-permute-start = (bf16[128,896]{1,0:T(8,128)(2,1)S(1)}, bf16[128,896]{1,0:T(8,128)(2,1)S(1)}, u32[]{:S(2)}, u32[]{:S(2)}) collective-permute-start(bf16[128,896]{1,0:T(8,128)(2,1)S(1)} %copy-done.2), channel_id=1, source_target_pairs={{0,32},{32,0},{1,33},{33,1},{2,34},{34,2},{3,35},{35,3},{4,36},{36... | collective-permute-start | bytes 688136 | tf_op jit(solution)/shard_map/ppermute | solution.py:133
  52.7 59.9 %collective-permute-start.2 = (bf16[128,2048]{1,0:T(8,128)(2,1)}, bf16[128,2048]{1,0:T(8,128)(2,1)}, u32[]{:S(2)}, u32[]{:S(2)}) collective-permute-start(bf16[128,2048]{1,0:T(8,128)(2,1)} %broadcast_select_fusion), channel_id=1, source_target_pairs={{0,32},{32,0},{1,33},{33,1},{2,34},{34,2},{3,35},{35,3},{4,36},{36... | collective-permute-start | bytes 1572872 | tf_op jit(solution)/shard_map/ppermute | solution.py:133
  55.8 12.0 %copy-start.5 = (bf16[16,64,128]{2,1,0:T(8,128)(2,1)}, bf16[16,64,128]{2,1,0:T(8,128)(2,1)S(1)}, u32[]{:S(2)}) copy-start(bf16[16,64,128]{2,1,0:T(8,128)(2,1)S(1)} %collective-permute-done.1.c_ref) | copy-start | bytes 786436
  57.5 18.0 %all-to-all-start.2 = ((f32[32,1,128]{2,1,0:T(1,128)}), f32[32,1,128]{2,1,0:T(1,128)S(1)}, u32[]{:S(2)}, u32[]{:S(2)}) async-start(f32[32,1,128]{2,1,0:T(1,128)} %broadcast_in_dim.17), calls=%async_computation.2 | async-start | bytes 32768 | tf_op jit(solution)/shard_map/all_to_all | solution.py:20
  67.8 0.7 copy-start.8
  74.6 11.3 %copy-start.3 = (bf16[128,896]{1,0:T(8,128)(2,1)S(1)}, bf16[128,896]{1,0:T(8,128)(2,1)}, u32[]{:S(2)}) copy-start(bf16[128,896]{1,0:T(8,128)(2,1)} %x_ref.3) | copy-start | bytes 688132
  75.6 19.8 %collective-permute-start.3 = (bf16[4,128,256]{2,1,0:T(8,128)(2,1)}, bf16[4,128,256]{2,1,0:T(8,128)(2,1)S(1)}, u32[]{:S(2)}, u32[]{:S(2)}) collective-permute-start(bf16[4,128,256]{2,1,0:T(8,128)(2,1)} %get-tuple-element.35), channel_id=1, source_target_pairs={{0,1},{1,0},{2,3},{3,2},{4,5},{5,4},{6,7},{7,6},{8,9},{9,8},{10,11... | collective-permute-start | bytes 786440 | tf_op jit(solution)/shard_map/ppermute | solution.py:234
  77.6 17.8 %collective-permute-start.4 = (bf16[4,128,256]{2,1,0:T(8,128)(2,1)}, bf16[4,128,256]{2,1,0:T(8,128)(2,1)S(1)}, u32[]{:S(2)}, u32[]{:S(2)}) collective-permute-start(bf16[4,128,256]{2,1,0:T(8,128)(2,1)} %get-tuple-element.36), channel_id=1, source_target_pairs={{0,2},{1,3},{2,0},{3,1},{4,6},{5,7},{6,4},{7,5},{8,10},{9,11},{10,... | collective-permute-start | bytes 786440 | tf_op jit(solution)/shard_map/ppermute | solution.py:234
  81.9 16.1 %collective-permute-start.5 = (bf16[4,128,256]{2,1,0:T(8,128)(2,1)}, bf16[4,128,256]{2,1,0:T(8,128)(2,1)S(1)}, u32[]{:S(2)}, u32[]{:S(2)}) collective-permute-start(bf16[4,128,256]{2,1,0:T(8,128)(2,1)} %get-tuple-element.37), channel_id=1, source_target_pairs={{0,3},{1,2},{2,1},{3,0},{4,7},{5,6},{6,5},{7,4},{8,11},{9,10},{10,... | collective-permute-start | bytes 786440 | tf_op jit(solution)/shard_map/ppermute | solution.py:234
  85.2 12.8 %copy-start.7 = (bf16[4,128,256]{2,1,0:T(8,128)(2,1)S(1)}, bf16[4,128,256]{2,1,0:T(8,128)(2,1)}, u32[]{:S(2)}) copy-start(bf16[4,128,256]{2,1,0:T(8,128)(2,1)} %get-tuple-element.34) | copy-start | bytes 786436
  85.9 29.6 %copy-start.6 = (bf16[128,64]{1,0:T(8,128)(2,1)}, bf16[128,64]{1,0:T(8,128)(2,1)S(1)}, u32[]{:S(2)}) copy-start(bf16[128,64]{1,0:T(8,128)(2,1)S(1)} %convolution_convert_fusion.1.r_ref) | copy-start | bytes 49156
  87.1 25.5 %all-to-all-start.3 = ((bf16[32,18,128]{2,1,0:T(8,128)(2,1)}), bf16[32,18,128]{2,1,0:T(8,128)(2,1)S(1)}, u32[]{:S(2)}, u32[]{:S(2)}) async-start(bf16[32,18,128]{2,1,0:T(8,128)(2,1)} %convert_element_type.108), calls=%async_computation.3 | async-start | bytes 393216 | tf_op jit(solution)/shard_map/all_to_all | solution.py:263
  98.1 14.5 %collective-permute-start.6 = (bf16[128,256]{1,0:T(8,128)(2,1)S(1)}, bf16[128,256]{1,0:T(8,128)(2,1)S(1)}, u32[]{:S(2)}, u32[]{:S(2)}) collective-permute-start(bf16[128,256]{1,0:T(8,128)(2,1)S(1)} %get-tuple-element.71), channel_id=1, source_target_pairs={{0,4},{4,8},{8,12},{12,0},{1,5},{5,9},{9,13},{13,1},{2,6},{6,10},{... | collective-permute-start | bytes 196616 | tf_op jit(solution)/shard_map/ppermute | solution.py:239
  102.1 10.5 %collective-permute-start.8 = (bf16[128,256]{1,0:T(8,128)(2,1)S(1)}, bf16[128,256]{1,0:T(8,128)(2,1)S(1)}, u32[]{:S(2)}, u32[]{:S(2)}) collective-permute-start(bf16[128,256]{1,0:T(8,128)(2,1)S(1)} %get-tuple-element.72), channel_id=1, source_target_pairs={{0,12},{4,0},{8,4},{12,8},{1,13},{5,1},{9,5},{13,9},{2,14},{6,2},{... | collective-permute-start | bytes 196616 | tf_op jit(solution)/shard_map/ppermute | solution.py:239
  105.5 9.0 %collective-permute-start.7 = (bf16[128,256]{1,0:T(8,128)(2,1)S(1)}, bf16[128,256]{1,0:T(8,128)(2,1)S(1)}, u32[]{:S(2)}, u32[]{:S(2)}) collective-permute-start(bf16[128,256]{1,0:T(8,128)(2,1)S(1)} %get-tuple-element.73), channel_id=1, source_target_pairs={{0,8},{4,12},{8,0},{12,4},{1,9},{5,13},{9,1},{13,5},{2,10},{6,14},... | collective-permute-start | bytes 196616 | tf_op jit(solution)/shard_map/ppermute | solution.py:239
  116.4 30.8 %all-to-all-start.4 = ((bf16[64,22,128]{2,1,0:T(8,128)(2,1)}), bf16[64,22,128]{2,1,0:T(8,128)(2,1)S(1)}, u32[]{:S(2)}, u32[]{:S(2)}) async-start(bf16[64,22,128]{2,1,0:T(8,128)(2,1)} %broadcast_in_dim.40), calls=%async_computation.4 | async-start | bytes 786432 | tf_op jit(solution)/shard_map/all_to_all | solution.py:20
  136.3 9.1 %collective-permute-start.10 = (bf16[128,896]{1,0:T(8,128)(2,1)}, bf16[128,896]{1,0:T(8,128)(2,1)S(1)}, u32[]{:S(2)}, u32[]{:S(2)}) collective-permute-start(bf16[128,896]{1,0:T(8,128)(2,1)} %get-tuple-element.41), channel_id=1, source_target_pairs={{0,32},{32,0},{1,33},{33,1},{2,34},{34,2},{3,35},{35,3},{4,36},{36... | collective-permute-start | bytes 688136 | tf_op jit(solution)/shard_map/ppermute | solution.py:133
  139.6 0.7 collective-permute-start.9
  148.8 1.3 copy-start.9
Sparse Core Ops, SparseCore 0:
  10.1 49.9 all-gather.2

commit v4 on v3

v4 whole, which is shorter than its diff:
```python
import math

import jax
import jax.numpy as jnp
from jax import lax
from jax.experimental import pallas as pl
from jax.experimental.pallas import tpu as pltpu
from jax.sharding import Mesh
from jax.sharding import PartitionSpec as P

epsilon = 1e-06
F32 = jnp.float32
BF16 = jnp.bfloat16
DP = ("g", "h", "w", "c")
TP = ("z", "u", "v")


def spread(block, axis):
    n = lax.axis_size(axis)
    return lax.all_to_all(jnp.broadcast_to(block[None], (n,) + block.shape), axis, 0, 0)


def forward_kernel(i_ref, x_ref, o_ref, a_ref, b_ref, c_ref, w_ref, *rest):
    w, c = i_ref[0], i_ref[1]
    out, x, r = rest
    t = x_ref.shape[0]

    @pl.when(pl.program_id(0) == 0)
    def _():
        x[:t] = jnp.where(w == 0, x_ref[...], o_ref[...])
        x[t:] = jnp.where(w == 0, o_ref[...], x_ref[...])
        r[...] = lax.dot_general(
            x[...], a_ref[...], (((1,), (1,)), ((), ())), preferred_element_type=F32
        ).astype(BF16)

    for k in range(2):
        b, d = b_ref[2 * k + w], c_ref[2 * k + w]
        up = jnp.concatenate([jnp.where(c == 0, b, d), jnp.where(c == 0, d, b)], axis=1)
        wide = jnp.concatenate([w_ref[2 * k], w_ref[2 * k + 1]], axis=1)
        y = jnp.dot(x[...], wide, preferred_element_type=F32)
        y = (y + jnp.dot(r[...], up, preferred_element_type=F32)).astype(BF16)
        out[2 * k] = y[:t]
        out[2 * k + 1] = y[t:]


def forward(place, x, other_x, down_t, up, other_up, gathered):
    t, f = x.shape
    n, rank = gathered.shape[0], down_t.shape[0]
    whole = lambda i, s: (0, 0)
    part = lambda i, s: (i, 0, 0)
    return pl.pallas_call(
        forward_kernel,
        grid_spec=pltpu.PrefetchScalarGridSpec(
            num_scalar_prefetch=1,
            grid=(n // 4,),
            in_specs=[
                pl.BlockSpec((t, f), whole),
                pl.BlockSpec((t, f), whole),
                pl.BlockSpec((rank, f), whole),
                pl.BlockSpec((4, rank, 128), part),
                pl.BlockSpec((4, rank, 128), part),
                pl.BlockSpec((4, f, 128), part),
            ],
            out_specs=pl.BlockSpec((4, t, 256), part),
            scratch_shapes=[pltpu.VMEM((2 * t, f), BF16), pltpu.VMEM((2 * t, rank), BF16)],
        ),
        out_shape=jax.ShapeDtypeStruct((n, t, 256), BF16),
        cost_estimate=pl.CostEstimate(
            flops=4 * t * f * n * 128, bytes_accessed=2 * f * n * 128, transcendentals=0
        ),
        name="forward",
    )(place, x, other_x, down_t, up, other_up, gathered)


def backward_kernel(
    i_ref, g_ref, k_ref, h_ref, s_ref, q_ref, w_ref, r_ref, a_ref, own_ref, other_ref, acc
):
    i = pl.program_id(0)
    t = g_ref.shape[0]

    @pl.when(i == 0)
    def _():
        acc[:t] = jnp.dot(r_ref[...], a_ref[...], preferred_element_type=F32)
        acc[t:] = jnp.zeros_like(acc[t:])

    wide = jnp.concatenate([w_ref[k] for k in range(4)], axis=1)
    g = jnp.concatenate([g_ref[...], k_ref[...]], axis=1)
    g = jnp.concatenate([g, h_ref[...]], axis=0).astype(F32)
    g = (g * jnp.concatenate([s_ref[...], q_ref[...]], axis=1)).astype(BF16)
    acc[...] += lax.dot_general(
        g, wide, (((1,), (1,)), ((), ())), preferred_element_type=F32
    )

    @pl.when(i == pl.num_programs(0) - 1)
    def _():
        own_ref[...] = acc[:t]
        other_ref[...] = acc[t:].astype(BF16)


def backward(place, cotangent, other_cotangent, scale, gathered, r, down_t):
    t = cotangent.shape[0]
    n, f, _ = gathered.shape
    whole = lambda i, s: (0, 0)
    mine = lambda i, s: (0, 4 * i + s[0])
    next_mine = lambda i, s: (0, 4 * i + 2 + s[0])
    return pl.pallas_call(
        backward_kernel,
        grid_spec=pltpu.PrefetchScalarGridSpec(
            num_scalar_prefetch=1,
            grid=(n // 4,),
            in_specs=[
                pl.BlockSpec((t, 256), mine),
                pl.BlockSpec((t, 256), next_mine),
                pl.BlockSpec((t, 512), lambda i, s: (0, i)),
                pl.BlockSpec((1, 256), mine),
                pl.BlockSpec((1, 256), next_mine),
                pl.BlockSpec((4, f, 128), lambda i, s: (i, 0, 0)),
                pl.BlockSpec(r.shape, whole),
                pl.BlockSpec(down_t.shape, whole),
            ],
            out_specs=[pl.BlockSpec((t, f), whole)] * 2,
            scratch_shapes=[pltpu.VMEM((2 * t, f), F32)],
        ),
        out_shape=[
            jax.ShapeDtypeStruct((t, f), F32),
            jax.ShapeDtypeStruct((t, f), BF16),
        ],
        cost_estimate=pl.CostEstimate(flops=4 * t * f * n * 128, bytes_accessed=2 * f * n * 128, transcendentals=0),
        name="backward",
    )(place, cotangent, cotangent, other_cotangent, scale, scale, gathered, r, down_t)


def swap(x, axis):
    return lax.ppermute(x, axis, [(0, 1), (1, 0)])


def cross(x):
    return lax.ppermute(x, ("w", "v"), [(0, 0), (1, 2), (2, 1), (3, 3)])


def every_other(x, which):
    n = x.shape[-1] // 256
    pick = lambda s: jnp.concatenate(
        [x[..., i * 256 : (i + 1) * 256] for i in range(s, n, 2)], axis=-1
    )
    return jnp.where(which == 0, pick(0), pick(1))


def in_order(which, own, other, axis):
    return jnp.where(
        which == 0,
        jnp.concatenate([own, other], axis=axis),
        jnp.concatenate([other, own], axis=axis),
    )


def fold(x, axis, where):
    n = x.shape[0] // 2
    sent = swap(jnp.where(where == 0, x[n:], x[:n]), axis)
    return jnp.where(where == 0, x[:n], x[n:]) + sent


def scatter(x, axis, where):
    n = lax.axis_size(axis)
    x = x.reshape(n, x.shape[0] // n, x.shape[1])
    block = lambda k: lax.dynamic_index_in_dim(x, (where + k) % n, 0, keepdims=False)
    total = block(0)
    for k in range(1, n):
        total += lax.ppermute(block(k), axis, [(i, (i + k) % n) for i in range(n)])
    return total


def second_kernel(i_ref, w_ref, a_ref, b_ref, x_ref, m_ref, o_ref):
    rank = a_ref.shape[0]
    whole = w_ref[...].astype(F32) + lax.dot_general(
        a_ref[...], b_ref[0], (((0,), (0,)), ((), ())), preferred_element_type=F32
    )
    left = jnp.sum(whole * whole, axis=0, keepdims=True)
    pieces = []
    for _ in range(3):
        pieces.append(left.astype(BF16))
        left = left - pieces[-1].astype(F32)
    r = lax.dot_general(
        a_ref[...], x_ref[...], (((1,), (1,)), ((), ())), preferred_element_type=F32
    )
    tail = jnp.concatenate(pieces + [m_ref[...], jnp.zeros((11, 128), BF16)], axis=0)
    for i in range(o_ref.shape[0]):
        o_ref[i, :rank] = r.astype(BF16)
        o_ref[i, rank:] = tail


def second_blocks(index, w, down_t, up, tokens, magnitude):
    (n, rank, _), f = up.shape, down_t.shape[1]
    whole = lambda i, s: (0, 0)
    return pl.pallas_call(
        second_kernel,
        grid_spec=pltpu.PrefetchScalarGridSpec(
            num_scalar_prefetch=1,
            grid=(1,),
            in_specs=[
                pl.BlockSpec(w.shape, whole),
                pl.BlockSpec(down_t.shape, whole),
                pl.BlockSpec((1, rank, 128), lambda i, s: (s[0], 0, 0)),
                pl.BlockSpec(tokens.shape, whole),
                pl.BlockSpec((2, 128), whole),
            ],
            out_specs=pl.BlockSpec((n, rank + 16, 128), lambda i, s: (0, 0, 0)),
        ),
        out_shape=jax.ShapeDtypeStruct((n, rank + 16, 128), BF16),
        name="second_blocks",
    )(index.reshape(1), w, down_t, up, tokens, magnitude.reshape(2, 128))


def on_device(tokens, frozen_matrix, adapter_down_factor, adapter_up_factor, magnitude, cotangent):
    t, f = tokens.shape
    n_dp, n_tp = lax.axis_size(DP), lax.axis_size(TP)
    g, h, w, c, z, u, v = (lax.axis_index(a) for a in DP + TP)
    rank, own = adapter_up_factor.shape
    down_t = adapter_down_factor.T
    place = jnp.stack([w, c])
    tie = lax.optimization_barrier

    gathered = lax.all_gather(frozen_matrix, ("g", "h", "c"), axis=0)

    own_half = jnp.where(c == 0, adapter_up_factor[:, :128], adapter_up_factor[:, 128:])
    own_half = spread(own_half, TP)
    cotangent_out = every_other(cotangent, 1 - w)
    cotangent_out, tokens_out = tie((cotangent_out, tokens))
    other_tokens = swap(tokens_out, "w")

    index = (2 * g + h) * 2 + w
    second = second_blocks(index, frozen_matrix, down_t, own_half, tokens, magnitude)
    second, cotangent_out, own_half = tie((second, cotangent_out, own_half))
    second = lax.all_to_all(second, TP, 0, 0)
    squares = second[:, rank : rank + 3].astype(F32)
    squares = jnp.sum(squares, axis=(0, 1)).reshape(1, 128)
    other_half = swap(own_half, "c")
    up_blocks = in_order(c, own_half[:, None], other_half[:, None], 1)
    full_up = jnp.moveaxis(up_blocks, 2, 0).reshape(rank, -1)

    squares = spread(squares, DP)
    rank_activation = jnp.sum(second[:, :rank].astype(F32), axis=0).astype(BF16)
    full_magnitude = second[:, rank + 3 : rank + 5].reshape(-1)
    other_cotangent = swap(cotangent_out, "w")
    outgoing = forward(place, tokens, other_tokens, down_t, own_half, other_half, gathered)
    squares, outgoing, other_cotangent = tie((squares, outgoing, other_cotangent))

    parts = lax.all_to_all(outgoing, TP, 0, 0)

    norm = jnp.sqrt(squares.reshape(-1) + epsilon)
    scale = full_magnitude.astype(F32) / norm
    scaled = (cotangent.astype(F32) * scale).astype(BF16)
    rank_back = lax.dot_general(
        scaled, full_up, (((1,), (1,)), ((), ())), preferred_element_type=F32
    ).astype(BF16)
    down = lax.dot_general(
        rank_back, tokens, (((0,), (0,)), ((), ())), preferred_element_type=F32
    )
    q = (2 * z + u) * 2 + v
    up = jnp.dot(
        rank_activation,
        lax.dynamic_slice_in_dim(scaled, q * own, own, 1),
        preferred_element_type=F32,
    )
    shares = jnp.concatenate([down, up], axis=1)
    shares = fold(fold(shares, "c", c), "h", h)
    shares = scatter(shares, "g", g)

    shares, rank_back = tie((shares, rank_back))
    own_part, other_part = backward(
        place, cotangent, other_cotangent, scale.reshape(1, -1), gathered, rank_back, down_t
    )
    shares = fold(shares, "w", w)
    parts, other_part = tie((parts, other_part))

    block = 2 * z + u
    here = 2 * block + w
    at = lambda x: lax.dynamic_slice_in_dim(x, here * own, own, 0)
    merged = jnp.sum(parts.astype(F32), axis=0)
    here_cotangent = jnp.where(
        v == w,
        lax.dynamic_slice_in_dim(cotangent, here * own, own, 1),
        lax.dynamic_slice_in_dim(other_cotangent, block * own, own, 1),
    ).astype(F32)
    mag_part = jnp.sum(here_cotangent * merged, axis=0) / at(norm)

    high = lax.reduce_precision(mag_part, 8, 7)
    mag_part = jnp.stack([high, mag_part - high]).astype(BF16)
    last = jnp.concatenate([shares.astype(BF16), mag_part], axis=1)
    last, merged, other_part = tie((last, merged, other_part))
    last = spread(last, ("c", "h", "g", "w", "v")).reshape(n_dp // 2, 2, 2, 2, f + 2 * own)
    factor = 1.0 / math.sqrt(t * n_dp)
    sums = last[..., : f + own]
    sums = jnp.where(v == 0, sums[:, :, 0], sums[:, :, 1]).astype(F32)
    sums = sums.reshape(rank, f + own) * factor
    grad_down = sums[:, :f].T
    grad_up = sums[:, f:]
    mags = last[..., f + own :]
    mags = jnp.where(v == 0, mags[:, 0], mags[:, 1]).astype(F32)
    grad_magnitude = jnp.sum(mags, axis=(0, 1, 2)) * factor

    output = cross((merged * at(scale)).astype(BF16))
    input_gradient = (own_part + swap(other_part, "w").astype(F32)).astype(BF16)
    return (output, input_gradient, grad_down, grad_up, grad_magnitude)


def solution(mesh):
    fine = Mesh(mesh.devices.reshape(4, 2, 2, 2, 4, 2, 2), DP + TP)
    return jax.shard_map(
        on_device,
        mesh=fine,
        in_specs=(P(DP, TP), P(TP, DP), P(TP, None), P(None, TP), P(TP), P(DP, None)),
        out_specs=(P(DP, TP), P(DP, TP), P(TP, None), P(None, TP), P(TP)),
        check_vma=False,
    )
```

time: 159 us -> 152 us (0.956)
  local copies, waits for them, and re-layouts: 12.8 us -> 9.79 us
  starting transfers between devices: 85.9 us -> 83.9 us
  Pallas kernels: 16.2 us -> 14.4 us
  waiting for transfers between devices: 18.1 us -> 19.7 us
    ppermute x6 -> x3, starting transfers between devices: 24 us -> 13.1 us  [scatter(): total += lax.ppermute(block(k), axis, [(i, (i + k) % n) for i in range(n)])]
    ppermute x4 -> x7, starting transfers between devices: 12.7 us -> 20 us  [swap(): return lax.ppermute(x, axis, [(0, 1), (1, 0)])]
    all_to_all x1 -> x2, starting transfers between devices: 8.3 us -> 11.8 us  [the longest x1 6.48 us: on_device(): parts = lax.all_to_all(outgoing, TP, 0, 0)]
    ppermute x4 -> x7, waiting for transfers between devices: 5.08 us -> 8.55 us  [swap(): return lax.ppermute(x, axis, [(0, 1), (1, 0)])]
    ppermute x6 -> x3, waiting for transfers between devices: 4.51 us -> 2.34 us  [scatter(): total += lax.ppermute(block(k), axis, [(i, (i + k) % n) for i in range(n)])]
    pallas_call x1, Pallas kernels: 8.11 us -> 6.09 us  [backward(): pl.pallas_call(backward_kernel, grid_spec=pltpu.PrefetchScalarGridSpec(nu...]
    all_to_all x4 -> x3, starting transfers between devices: 40.3 us -> 38.3 us  [spread(): lax.all_to_all(jnp.broadcast_to(block[None], (n,) + block.shape), axis, 0...]
    broadcast_in_dim x4 -> x3, local copies, waits for them, and re-layouts: 3.66 us -> 2.29 us  [spread(): jnp.broadcast_to(block[None], (n,) + block.shape)]
  transfers between devices with their start and end apart: 17 -> 17, of which waited for: 5 -> 6; matrix products, arithmetic and copies ran while one was open for 10% -> 7% of each run, Pallas kernels for 10% -> 10%
where the time goes in v4:
time: 152 us; the launch traced here: 150 us
  starting transfers between devices  83.9 us (55%)
  waiting for transfers between devices  19.7 us (13%)
  between operations  14.6 us (10%)
  Pallas kernels  14.4 us (9%)
  local copies, waits for them, and re-layouts  9.79 us (6%)
  other arithmetic  7.25 us (5%)
    all_to_all x3, starting transfers between devices, spread(): lax.all_to_all(jnp.broadcast_to(block[None], (n,) + block.shape), axis, 0...  38.3 us
    ppermute x7, starting transfers between devices, swap(): return lax.ppermute(x, axis, [(0, 1), (1, 0)])  20 us
    ppermute x3, starting transfers between devices, scatter(): total += lax.ppermute(block(k), axis, [(i, (i + k) % n) for i in range(n)])  13.1 us
    ppermute x7, waiting for transfers between devices, swap(): return lax.ppermute(x, axis, [(0, 1), (1, 0)])  8.55 us
    all_to_all x3, waiting for transfers between devices, spread(): lax.all_to_all(jnp.broadcast_to(block[None], (n,) + block.shape), axis, 0...  8.06 us
    all_to_all x1, starting transfers between devices, on_device(): parts = lax.all_to_all(outgoing, TP, 0, 0)  6.48 us
    pallas_call x1, Pallas kernels, backward(): pl.pallas_call(backward_kernel, grid_spec=pltpu.PrefetchScalarGridSpec(nu...  6.09 us
    pallas_call x1, Pallas kernels, forward(): pl.pallas_call(forward_kernel, grid_spec=pltpu.PrefetchScalarGridSpec(num...  6.07 us
  transfers between devices with their start and end apart: 17, of which 6 were waited for; matrix products, arithmetic and copies ran while one was open for 7% of the time, Pallas kernels for 10%

profile of v4, /device:TPU:1, one launch (start us, length us, event | category | flops | bytes accessed | tf_op | source)
XLA Modules:
  0.0 150.4 jit_solution(218574229467908769)
XLA Ops:
  7.2 0.0 copy-start
  7.2 0.0 all-gather.3.cloned.1.call-start
  7.2 0.7 all-gather.3.cloned.1.call-update
  7.9 0.7 slice_select_fusion.1
  8.7 0.7 broadcast_in_dim.10
  9.4 13.4 %all-to-all-start = ((bf16[16,64,128]{2,1,0:T(8,128)(2,1)}), bf16[16,64,128]{2,1,0:T(8,128)(2,1)S(1)}, u32[]{:S(2)}, u32[]{:S(2)}) async-start(bf16[16,64,128]{2,1,0:T(8,128)(2,1)} %broadcast_in_dim.10), calls=%async_computation | async-start | bytes 524288 | tf_op jit(solution)/shard_map/all_to_all | solution.py:20
  22.8 0.9 slice_dynamic-update-slice_fusion.7
  23.7 0.9 slice_dynamic-update-slice_fusion.6
  24.6 0.9 slice_dynamic-update-slice_fusion.5
  25.5 0.9 slice_dynamic-update-slice_fusion.4
  26.4 0.0 copy-start.2
  26.5 0.9 broadcast_select_fusion
  27.4 5.5 %all-to-all-done.b_ref = bf16[16,64,128]{2,1,0:T(8,128)(2,1)S(1)} async-done(((bf16[16,64,128]{2,1,0:T(8,128)(2,1)}), bf16[16,64,128]{2,1,0:T(8,128)(2,1)S(1)}, u32[]{:S(2)}, u32[]{:S(2)}) %all-to-all-start) | async-done | bytes 262176 | tf_op jit(solution)/shard_map/all_to_all | solution.py:20
  32.9 0.7 copy-done.1
  33.6 2.2 %second_blocks.1 = bf16[16,80,128]{2,1,0:T(8,128)(2,1)} custom-call(s32[1]{0:T(128)} %bitcast.i_ref, bf16[896,128]{1,0:T(8,128)(2,1)} %w_ref.1, bf16[64,896]{1,0:T(8,128)(2,1)} %bitcast.42, bf16[16,64,128]{2,1,0:T(8,128)(2,1)} %copy-done.1, bf16[128,896]{1,0:T(8,128)(2,1)} %x_ref.3, bf16[2,128]{1,0:T(2,128)(2,1)} %bitcast.50), custom_call_target="tpu_custom_call" | custom-call | tf_op jit(solution)/shard_map/second_blocks/pallas_call | solution.py:195
  35.8 5.3 %all-to-all-start.1 = ((bf16[16,80,128]{2,1,0:T(8,128)(2,1)}), bf16[16,80,128]{2,1,0:T(8,128)(2,1)S(1)}, u32[]{:S(2)}, u32[]{:S(2)}) async-start(bf16[16,80,128]{2,1,0:T(8,128)(2,1)} %second_blocks.1), calls=%async_computation.1 | async-start | bytes 655360 | tf_op jit(solution)/shard_map/all_to_all | solution.py:234
  41.1 4.0 %collective-permute-start.1 = (bf16[16,64,128]{2,1,0:T(8,128)(2,1)}, bf16[16,64,128]{2,1,0:T(8,128)(2,1)S(1)}, u32[]{:S(2)}, u32[]{:S(2)}) collective-permute-start(bf16[16,64,128]{2,1,0:T(8,128)(2,1)} %copy-done.1), channel_id=1, source_target_pairs={{0,16},{16,0},{1,17},{17,1},{2,18},{18,2},{3,19},{19,3},{4,20},{20... | collective-permute-start | bytes 786440 | tf_op jit(solution)/shard_map/ppermute | solution.py:134
  45.2 2.9 %collective-permute-start = (bf16[128,896]{1,0:T(8,128)(2,1)S(1)}, bf16[128,896]{1,0:T(8,128)(2,1)}, u32[]{:S(2)}, u32[]{:S(2)}) collective-permute-start(bf16[128,896]{1,0:T(8,128)(2,1)S(1)} %copy-done.2), channel_id=1, source_target_pairs={{0,32},{32,0},{1,33},{33,1},{2,34},{34,2},{3,35},{35,3},{4,36},{36... | collective-permute-start | bytes 688136 | tf_op jit(solution)/shard_map/ppermute | solution.py:134
  48.0 0.6 pad_add_fusion.i_ref
  48.6 2.4 %collective-permute-start.2 = (bf16[128,2048]{1,0:T(8,128)(2,1)}, bf16[128,2048]{1,0:T(8,128)(2,1)S(1)}, u32[]{:S(2)}, u32[]{:S(2)}) collective-permute-start(bf16[128,2048]{1,0:T(8,128)(2,1)} %broadcast_select_fusion), channel_id=1, source_target_pairs={{0,32},{32,0},{1,33},{33,1},{2,34},{34,2},{3,35},{35,3},{4,36},{36... | collective-permute-start | bytes 1572872 | tf_op jit(solution)/shard_map/ppermute | solution.py:134
  51.0 0.0 collective-permute-done.1.c_ref
  51.1 1.2 fusion
  52.3 0.5 copy.14
  52.8 0.4 reshape.86
  53.2 0.0 all-to-all-done.1
  53.3 0.6 broadcast_in_dim.11
  53.9 11.4 %all-to-all-start.2 = ((f32[32,1,128]{2,1,0:T(1,128)}), f32[32,1,128]{2,1,0:T(1,128)S(1)}, u32[]{:S(2)}, u32[]{:S(2)}) async-start(f32[32,1,128]{2,1,0:T(1,128)} %broadcast_in_dim.11), calls=%async_computation.2 | async-start | bytes 32768 | tf_op jit(solution)/shard_map/all_to_all | solution.py:20
  65.3 0.0 collective-permute-done.o_ref
  65.3 0.0 all-gather.3.cloned.1.call-done
  65.4 6.1 %forward.1 = bf16[16,128,256]{2,1,0:T(8,128)(2,1)} custom-call(s32[2]{0:T(128)} %pad_add_fusion.i_ref, bf16[128,896]{1,0:T(8,128)(2,1)} %x_ref.3, bf16[128,896]{1,0:T(8,128)(2,1)} %collective-permute-done.o_ref, bf16[64,896]{1,0:T(8,128)(2,1)} %bitcast.43, bf16[16,64,128]{2,1,0:T(8,128)(2,1)} %copy-done.1, bf16[16,64,128]{2,1,0:T(8,128)(2,1)} %copy-done.4, ...), custom_call_target="tpu_custom_call" | custom-call | flops 939524096 | bytes 3670016 | tf_op jit(solution)/shard_map/forward/pallas_call | solution.py:51
  71.5 1.6 %all-to-all-done.2 = f32[32,1,128]{2,1,0:T(1,128)S(1)} async-done(((f32[32,1,128]{2,1,0:T(1,128)}), f32[32,1,128]{2,1,0:T(1,128)S(1)}, u32[]{:S(2)}, u32[]{:S(2)}) %all-to-all-start.2) | async-done | bytes 16416 | tf_op jit(solution)/shard_map/all_to_all | solution.py:20
  73.1 0.2 multiply_convert_fusion
  73.3 0.4 convolution_convert_fusion.r_ref
  73.7 0.0 copy-start.7
  73.7 0.2 fusion.8
  74.0 0.1 fusion.2
  74.1 2.5 %collective-permute-start.3 = (f32[32,1152]{1,0:T(8,128)S(1)}, f32[32,1152]{1,0:T(8,128)S(1)}, u32[]{:S(2)}, u32[]{:S(2)}) collective-permute-start(f32[32,1152]{1,0:T(8,128)S(1)} %broadcast_select_fusion.2), channel_id=1, source_target_pairs={{0,16},{16,0},{1,17},{17,1},{2,18},{18,2},{3,19},{19,3},{4,20},{20... | collective-permute-start | bytes 442376 | tf_op jit(solution)/shard_map/ppermute | solution.py:134
  76.7 1.0 collective-permute-done.3
  77.7 2.3 %collective-permute-start.4 = (f32[16,1152]{1,0:T(8,128)S(1)}, f32[16,1152]{1,0:T(8,128)S(1)}, u32[]{:S(2)}, u32[]{:S(2)}) collective-permute-start(f32[16,1152]{1,0:T(8,128)S(1)} %slice_select_fusion), channel_id=1, source_target_pairs={{0,64},{64,0},{1,65},{65,1},{2,66},{66,2},{3,67},{67,3},{4,68},{68... | collective-permute-start | bytes 221192 | tf_op jit(solution)/shard_map/ppermute | solution.py:134
  80.0 6.5 %all-to-all-start.3 = ((bf16[16,128,256]{2,1,0:T(8,128)(2,1)}), bf16[16,128,256]{2,1,0:T(8,128)(2,1)S(1)}, u32[]{:S(2)}, u32[]{:S(2)}) async-start(bf16[16,128,256]{2,1,0:T(8,128)(2,1)} %forward.1), calls=%async_computation.3 | async-start | bytes 2097152 | tf_op jit(solution)/shard_map/all_to_all | solution.py:248
  86.6 3.6 %collective-permute-start.5 = (f32[4,1152]{1,0:T(4,128)S(1)}, f32[4,1152]{1,0:T(4,128)S(1)}, u32[]{:S(2)}, u32[]{:S(2)}) collective-permute-start(f32[4,1152]{1,0:T(4,128)S(1)} %get-tuple-element.57), channel_id=1, source_target_pairs={{0,128},{128,256},{256,384},{384,0},{1,129},{129,257},{257,385},{3... | collective-permute-start | bytes 55304 | tf_op jit(solution)/shard_map/ppermute | solution.py:169
  90.2 3.8 %collective-permute-start.7 = (f32[4,1152]{1,0:T(4,128)S(1)}, f32[4,1152]{1,0:T(4,128)S(1)}, u32[]{:S(2)}, u32[]{:S(2)}) collective-permute-start(f32[4,1152]{1,0:T(4,128)S(1)} %get-tuple-element.58), channel_id=1, source_target_pairs={{0,384},{128,0},{256,128},{384,256},{1,385},{129,1},{257,129},{385... | collective-permute-start | bytes 55304 | tf_op jit(solution)/shard_map/ppermute | solution.py:169
  94.0 5.7 %collective-permute-start.6 = (f32[4,1152]{1,0:T(4,128)S(1)}, f32[4,1152]{1,0:T(4,128)S(1)}, u32[]{:S(2)}, u32[]{:S(2)}) collective-permute-start(f32[4,1152]{1,0:T(4,128)S(1)} %get-tuple-element.59), channel_id=1, source_target_pairs={{0,256},{128,384},{256,0},{384,128},{1,257},{129,385},{257,1},{385... | collective-permute-start | bytes 55304 | tf_op jit(solution)/shard_map/ppermute | solution.py:169
  99.8 0.6 bitcast_multiply_fusion.s_ref.q_ref
  100.4 2.3 %collective-permute-done.6 = f32[4,1152]{1,0:T(4,128)S(1)} collective-permute-done((f32[4,1152]{1,0:T(4,128)S(1)}, f32[4,1152]{1,0:T(4,128)S(1)}, u32[]{:S(2)}, u32[]{:S(2)}) %collective-permute-start.6) | collective-permute-done | bytes 18464 | tf_op jit(solution)/shard_map/ppermute | solution.py:169
  102.8 2.7 %collective-permute-start.8 = (f32[2,1152]{1,0:T(2,128)S(1)}, f32[2,1152]{1,0:T(2,128)S(1)}, u32[]{:S(2)}, u32[]{:S(2)}) collective-permute-start(f32[2,1152]{1,0:T(2,128)S(1)} %broadcast_select_fusion.4), channel_id=1, source_target_pairs={{0,32},{32,0},{1,33},{33,1},{2,34},{34,2},{3,35},{35,3},{4,36},{36... | collective-permute-start | bytes 27656 | tf_op jit(solution)/shard_map/ppermute | solution.py:134
  105.5 6.1 %backward.1 = (f32[128,896]{1,0:T(8,128)}, bf16[128,896]{1,0:T(8,128)(2,1)}) custom-call(s32[2]{0:T(128)} %pad_add_fusion.i_ref, bf16[128,4096]{1,0:T(8,128)(2,1)} %k_ref.1, bf16[128,4096]{1,0:T(8,128)(2,1)} %k_ref.1, bf16[128,2048]{1,0:T(8,128)(2,1)} %copy-done.5, f32[1,4096]{1,0:T(1,128)} %bitcast_multiply_fusion.s_ref.q_ref, ...), custom_call_target="tpu_custom_call" | custom-call | flops 939524096 | bytes 3670016 | tf_op jit(solution)/shard_map/backward/pallas_call | solution.py:106
  111.6 0.1 convert_reduce_fusion
  111.8 1.0 multiply_reduce_fusion
  112.7 0.1 reduce-precision_convert_fusion
  112.8 0.9 broadcast_in_dim.14
  113.8 13.5 %all-to-all-start.4 = ((bf16[64,2,1408]{2,1,0:T(2,128)(2,1)}), bf16[64,2,1408]{2,1,0:T(2,128)(2,1)S(1)}, u32[]{:S(2)}, u32[]{:S(2)}) async-start(bf16[64,2,1408]{2,1,0:T(2,128)(2,1)} %broadcast_in_dim.14), calls=%async_computation.4 | async-start | bytes 720896 | tf_op jit(solution)/shard_map/all_to_all | solution.py:20
  127.3 3.3 %collective-permute-start.10 = (bf16[128,896]{1,0:T(8,128)(2,1)S(1)}, bf16[128,896]{1,0:T(8,128)(2,1)S(1)}, u32[]{:S(2)}, u32[]{:S(2)}) collective-permute-start(bf16[128,896]{1,0:T(8,128)(2,1)S(1)} %copy-done.8), channel_id=1, source_target_pairs={{0,32},{32,0},{1,33},{33,1},{2,34},{34,2},{3,35},{35,3},{4,36},{36... | collective-permute-start | bytes 688136 | tf_op jit(solution)/shard_map/ppermute | solution.py:134
  130.6 0.7 collective-permute-start.9
  131.3 7.6 %collective-permute-done.10 = bf16[128,896]{1,0:T(8,128)(2,1)S(1)} collective-permute-done((bf16[128,896]{1,0:T(8,128)(2,1)S(1)}, bf16[128,896]{1,0:T(8,128)(2,1)S(1)}, u32[]{:S(2)}, u32[]{:S(2)}) %collective-permute-start.10) | collective-permute-done | bytes 229408 | tf_op jit(solution)/shard_map/ppermute | solution.py:134
  138.8 0.7 add_convert_fusion
  139.5 1.0 all-to-all-done.4
  140.5 0.1 convert_reduce_fusion.1
  140.6 0.2 convert_multiply_fusion
  140.8 0.2 mul.73
  141.0 0.6 slice.154
  141.6 0.7 slice_bitcast_fusion
  142.3 0.6 broadcast_multiply_fusion
  142.9 0.6 copy.32
  (44 shorter events, 0.4 us)
Async XLA Ops:
  7.2 19.2 %copy-start = (bf16[128,4096]{1,0:T(8,128)(2,1)S(1)}, bf16[128,4096]{1,0:T(8,128)(2,1)}, u32[]{:S(2)}) copy-start(bf16[128,4096]{1,0:T(8,128)(2,1)} %k_ref.1) | copy-start | bytes 3145732
  7.2 58.2 %all-gather.3.cloned.1.call-start = ((), (), s32[]{:S(2)}) async-start(), calls=%async_computation.5 | async-start | bytes 3899392 | tf_op jit(solution)/shard_map/all_gather | solution.py:223
  9.4 23.5 %all-to-all-start = ((bf16[16,64,128]{2,1,0:T(8,128)(2,1)}), bf16[16,64,128]{2,1,0:T(8,128)(2,1)S(1)}, u32[]{:S(2)}, u32[]{:S(2)}) async-start(bf16[16,64,128]{2,1,0:T(8,128)(2,1)} %broadcast_in_dim.10), calls=%async_computation | async-start | bytes 524288 | tf_op jit(solution)/shard_map/all_to_all | solution.py:20
  26.4 18.7 %copy-start.2 = (bf16[128,896]{1,0:T(8,128)(2,1)S(1)}, bf16[128,896]{1,0:T(8,128)(2,1)}, u32[]{:S(2)}) copy-start(bf16[128,896]{1,0:T(8,128)(2,1)} %x_ref.3) | copy-start | bytes 688132
  32.9 0.7 copy-start.1
  35.8 17.4 %all-to-all-start.1 = ((bf16[16,80,128]{2,1,0:T(8,128)(2,1)}), bf16[16,80,128]{2,1,0:T(8,128)(2,1)S(1)}, u32[]{:S(2)}, u32[]{:S(2)}) async-start(bf16[16,80,128]{2,1,0:T(8,128)(2,1)} %second_blocks.1), calls=%async_computation.1 | async-start | bytes 655360 | tf_op jit(solution)/shard_map/all_to_all | solution.py:234
  41.1 9.9 %collective-permute-start.1 = (bf16[16,64,128]{2,1,0:T(8,128)(2,1)}, bf16[16,64,128]{2,1,0:T(8,128)(2,1)S(1)}, u32[]{:S(2)}, u32[]{:S(2)}) collective-permute-start(bf16[16,64,128]{2,1,0:T(8,128)(2,1)} %copy-done.1), channel_id=1, source_target_pairs={{0,16},{16,0},{1,17},{17,1},{2,18},{18,2},{3,19},{19,3},{4,20},{20... | collective-permute-start | bytes 786440 | tf_op jit(solution)/shard_map/ppermute | solution.py:134
  45.2 20.2 %collective-permute-start = (bf16[128,896]{1,0:T(8,128)(2,1)S(1)}, bf16[128,896]{1,0:T(8,128)(2,1)}, u32[]{:S(2)}, u32[]{:S(2)}) collective-permute-start(bf16[128,896]{1,0:T(8,128)(2,1)S(1)} %copy-done.2), channel_id=1, source_target_pairs={{0,32},{32,0},{1,33},{33,1},{2,34},{34,2},{3,35},{35,3},{4,36},{36... | collective-permute-start | bytes 688136 | tf_op jit(solution)/shard_map/ppermute | solution.py:134
  48.6 22.8 %collective-permute-start.2 = (bf16[128,2048]{1,0:T(8,128)(2,1)}, bf16[128,2048]{1,0:T(8,128)(2,1)S(1)}, u32[]{:S(2)}, u32[]{:S(2)}) collective-permute-start(bf16[128,2048]{1,0:T(8,128)(2,1)} %broadcast_select_fusion), channel_id=1, source_target_pairs={{0,32},{32,0},{1,33},{33,1},{2,34},{34,2},{3,35},{35,3},{4,36},{36... | collective-permute-start | bytes 1572872 | tf_op jit(solution)/shard_map/ppermute | solution.py:134
  51.1 14.3 %copy-start.4 = (bf16[16,64,128]{2,1,0:T(8,128)(2,1)}, bf16[16,64,128]{2,1,0:T(8,128)(2,1)S(1)}, u32[]{:S(2)}) copy-start(bf16[16,64,128]{2,1,0:T(8,128)(2,1)S(1)} %collective-permute-done.1.c_ref) | copy-start | bytes 786436
  53.9 19.2 %all-to-all-start.2 = ((f32[32,1,128]{2,1,0:T(1,128)}), f32[32,1,128]{2,1,0:T(1,128)S(1)}, u32[]{:S(2)}, u32[]{:S(2)}) async-start(f32[32,1,128]{2,1,0:T(1,128)} %broadcast_in_dim.11), calls=%async_computation.2 | async-start | bytes 32768 | tf_op jit(solution)/shard_map/all_to_all | solution.py:20
  71.4 2.3 %copy-start.3 = (bf16[128,896]{1,0:T(8,128)(2,1)S(1)}, bf16[128,896]{1,0:T(8,128)(2,1)}, u32[]{:S(2)}) copy-start(bf16[128,896]{1,0:T(8,128)(2,1)} %x_ref.3) | copy-start | bytes 688132
  71.4 2.5 %copy-start.5 = (bf16[128,2048]{1,0:T(8,128)(2,1)}, bf16[128,2048]{1,0:T(8,128)(2,1)S(1)}, u32[]{:S(2)}) copy-start(bf16[128,2048]{1,0:T(8,128)(2,1)S(1)} %collective-permute-done.2.h_ref) | copy-start | bytes 1572868
  73.7 12.8 %copy-start.7 = (bf16[128,64]{1,0:T(8,128)(2,1)}, bf16[128,64]{1,0:T(8,128)(2,1)S(1)}, u32[]{:S(2)}) copy-start(bf16[128,64]{1,0:T(8,128)(2,1)S(1)} %convolution_convert_fusion.r_ref) | copy-start | bytes 49156
  74.1 3.5 %collective-permute-start.3 = (f32[32,1152]{1,0:T(8,128)S(1)}, f32[32,1152]{1,0:T(8,128)S(1)}, u32[]{:S(2)}, u32[]{:S(2)}) collective-permute-start(f32[32,1152]{1,0:T(8,128)S(1)} %broadcast_select_fusion.2), channel_id=1, source_target_pairs={{0,16},{16,0},{1,17},{17,1},{2,18},{18,2},{3,19},{19,3},{4,20},{20... | collective-permute-start | bytes 442376 | tf_op jit(solution)/shard_map/ppermute | solution.py:134
  77.7 8.8 %collective-permute-start.4 = (f32[16,1152]{1,0:T(8,128)S(1)}, f32[16,1152]{1,0:T(8,128)S(1)}, u32[]{:S(2)}, u32[]{:S(2)}) collective-permute-start(f32[16,1152]{1,0:T(8,128)S(1)} %slice_select_fusion), channel_id=1, source_target_pairs={{0,64},{64,0},{1,65},{65,1},{2,66},{66,2},{3,67},{67,3},{4,68},{68... | collective-permute-start | bytes 221192 | tf_op jit(solution)/shard_map/ppermute | solution.py:134
  80.0 31.6 %all-to-all-start.3 = ((bf16[16,128,256]{2,1,0:T(8,128)(2,1)}), bf16[16,128,256]{2,1,0:T(8,128)(2,1)S(1)}, u32[]{:S(2)}, u32[]{:S(2)}) async-start(bf16[16,128,256]{2,1,0:T(8,128)(2,1)} %forward.1), calls=%async_computation.3 | async-start | bytes 2097152 | tf_op jit(solution)/shard_map/all_to_all | solution.py:248
  86.6 13.8 %collective-permute-start.5 = (f32[4,1152]{1,0:T(4,128)S(1)}, f32[4,1152]{1,0:T(4,128)S(1)}, u32[]{:S(2)}, u32[]{:S(2)}) collective-permute-start(f32[4,1152]{1,0:T(4,128)S(1)} %get-tuple-element.57), channel_id=1, source_target_pairs={{0,128},{128,256},{256,384},{384,0},{1,129},{129,257},{257,385},{3... | collective-permute-start | bytes 55304 | tf_op jit(solution)/shard_map/ppermute | solution.py:169
  90.2 10.2 %collective-permute-start.7 = (f32[4,1152]{1,0:T(4,128)S(1)}, f32[4,1152]{1,0:T(4,128)S(1)}, u32[]{:S(2)}, u32[]{:S(2)}) collective-permute-start(f32[4,1152]{1,0:T(4,128)S(1)} %get-tuple-element.58), channel_id=1, source_target_pairs={{0,384},{128,0},{256,128},{384,256},{1,385},{129,1},{257,129},{385... | collective-permute-start | bytes 55304 | tf_op jit(solution)/shard_map/ppermute | solution.py:169
  94.0 8.7 %collective-permute-start.6 = (f32[4,1152]{1,0:T(4,128)S(1)}, f32[4,1152]{1,0:T(4,128)S(1)}, u32[]{:S(2)}, u32[]{:S(2)}) collective-permute-start(f32[4,1152]{1,0:T(4,128)S(1)} %get-tuple-element.59), channel_id=1, source_target_pairs={{0,256},{128,384},{256,0},{384,128},{1,257},{129,385},{257,1},{385... | collective-permute-start | bytes 55304 | tf_op jit(solution)/shard_map/ppermute | solution.py:169
  102.8 8.8 %collective-permute-start.8 = (f32[2,1152]{1,0:T(2,128)S(1)}, f32[2,1152]{1,0:T(2,128)S(1)}, u32[]{:S(2)}, u32[]{:S(2)}) collective-permute-start(f32[2,1152]{1,0:T(2,128)S(1)} %broadcast_select_fusion.4), channel_id=1, source_target_pairs={{0,32},{32,0},{1,33},{33,1},{2,34},{34,2},{3,35},{35,3},{4,36},{36... | collective-permute-start | bytes 27656 | tf_op jit(solution)/shard_map/ppermute | solution.py:134
  111.6 15.7 %copy-start.8 = (bf16[128,896]{1,0:T(8,128)(2,1)S(1)}, bf16[128,896]{1,0:T(8,128)(2,1)}, u32[]{:S(2)}) copy-start(bf16[128,896]{1,0:T(8,128)(2,1)} %get-tuple-element.37) | copy-start | bytes 688132
  111.6 27.2 %copy-start.6 = (f32[128,896]{1,0:T(8,128)S(1)}, f32[128,896]{1,0:T(8,128)}, u32[]{:S(2)}) copy-start(f32[128,896]{1,0:T(8,128)} %get-tuple-element.36) | copy-start | bytes 1376260
  113.8 26.7 %all-to-all-start.4 = ((bf16[64,2,1408]{2,1,0:T(2,128)(2,1)}), bf16[64,2,1408]{2,1,0:T(2,128)(2,1)S(1)}, u32[]{:S(2)}, u32[]{:S(2)}) async-start(bf16[64,2,1408]{2,1,0:T(2,128)(2,1)} %broadcast_in_dim.14), calls=%async_computation.4 | async-start | bytes 720896 | tf_op jit(solution)/shard_map/all_to_all | solution.py:20
  127.3 11.5 %collective-permute-start.10 = (bf16[128,896]{1,0:T(8,128)(2,1)S(1)}, bf16[128,896]{1,0:T(8,128)(2,1)S(1)}, u32[]{:S(2)}, u32[]{:S(2)}) collective-permute-start(bf16[128,896]{1,0:T(8,128)(2,1)S(1)} %copy-done.8), channel_id=1, source_target_pairs={{0,32},{32,0},{1,33},{33,1},{2,34},{34,2},{3,35},{35,3},{4,36},{36... | collective-permute-start | bytes 688136 | tf_op jit(solution)/shard_map/ppermute | solution.py:134
  130.6 0.7 collective-permute-start.9
Sparse Core Ops, SparseCore 0:
  10.1 49.9 all-gather.2

commit v5 on v4

--- a/solution.py
+++ b/solution.py
@@ -72,49 +72,45 @@
     )(place, x, other_x, down_t, up, other_up, gathered)
 
 
-def backward_kernel(
-    i_ref, g_ref, k_ref, h_ref, s_ref, q_ref, w_ref, r_ref, a_ref, own_ref, other_ref, acc
-):
-    i = pl.program_id(0)
-    t = g_ref.shape[0]
+def backward_kernel(i_ref, g_ref, h_ref, s_ref, w_ref, r_ref, a_ref, own_ref, other_ref, acc):
+    i, last = pl.program_id(0), pl.num_programs(0) - 1
+    t, n = g_ref.shape[0], w_ref.shape[0]
+    wide = jnp.concatenate([w_ref[k] for k in range(n)], axis=1)
+    rows, scales = [], []
+    for k in range(n // 2):
+        mine = pl.ds(pl.multiple_of((n * i + 2 * k + i_ref[0]) * 256, 256), 256)
+        rows.append(g_ref[:, mine])
+        scales.append(s_ref[:, mine])
+    g = jnp.concatenate([jnp.concatenate(rows, axis=1), h_ref[...]], axis=0)
+    g = (g.astype(F32) * jnp.concatenate(scales, axis=1)).astype(BF16)
+    total = lax.dot_general(g, wide, (((1,), (1,)), ((), ())), preferred_element_type=F32)
 
     @pl.when(i == 0)
     def _():
-        acc[:t] = jnp.dot(r_ref[...], a_ref[...], preferred_element_type=F32)
-        acc[t:] = jnp.zeros_like(acc[t:])
-
-    wide = jnp.concatenate([w_ref[k] for k in range(4)], axis=1)
-    g = jnp.concatenate([g_ref[...], k_ref[...]], axis=1)
-    g = jnp.concatenate([g, h_ref[...]], axis=0).astype(F32)
-    g = (g * jnp.concatenate([s_ref[...], q_ref[...]], axis=1)).astype(BF16)
-    acc[...] += lax.dot_general(
-        g, wide, (((1,), (1,)), ((), ())), preferred_element_type=F32
-    )
-
-    @pl.when(i == pl.num_programs(0) - 1)
+        acc[...] = total
+
+    @pl.when(i == last)
     def _():
-        own_ref[...] = acc[:t]
-        other_ref[...] = acc[t:].astype(BF16)
+        whole = acc[...] + total
+        own_ref[...] = whole[:t] + jnp.dot(r_ref[...], a_ref[...], preferred_element_type=F32)
+        other_ref[...] = whole[t:].astype(BF16)
 
 
 def backward(place, cotangent, other_cotangent, scale, gathered, r, down_t):
     t = cotangent.shape[0]
     n, f, _ = gathered.shape
     whole = lambda i, s: (0, 0)
-    mine = lambda i, s: (0, 4 * i + s[0])
-    next_mine = lambda i, s: (0, 4 * i + 2 + s[0])
+    step = n // 2
     return pl.pallas_call(
         backward_kernel,
         grid_spec=pltpu.PrefetchScalarGridSpec(
             num_scalar_prefetch=1,
-            grid=(n // 4,),
+            grid=(2,),
             in_specs=[
-                pl.BlockSpec((t, 256), mine),
-                pl.BlockSpec((t, 256), next_mine),
-                pl.BlockSpec((t, 512), lambda i, s: (0, i)),
-                pl.BlockSpec((1, 256), mine),
-                pl.BlockSpec((1, 256), next_mine),
-                pl.BlockSpec((4, f, 128), lambda i, s: (i, 0, 0)),
+                pl.BlockSpec(cotangent.shape, whole),
+                pl.BlockSpec((t, step * 128), lambda i, s: (0, i)),
+                pl.BlockSpec(scale.shape, whole),
+                pl.BlockSpec((step, f, 128), lambda i, s: (i, 0, 0)),
                 pl.BlockSpec(r.shape, whole),
                 pl.BlockSpec(down_t.shape, whole),
             ],
@@ -125,9 +121,12 @@
             jax.ShapeDtypeStruct((t, f), F32),
             jax.ShapeDtypeStruct((t, f), BF16),
         ],
-        cost_estimate=pl.CostEstimate(flops=4 * t * f * n * 128, bytes_accessed=2 * f * n * 128, transcendentals=0),
+        compiler_params=pltpu.CompilerParams(vmem_limit_bytes=40 * 1024 * 1024),
+        cost_estimate=pl.CostEstimate(
+            flops=4 * t * f * n * 128, bytes_accessed=2 * f * n * 128, transcendentals=0
+        ),
         name="backward",
-    )(place, cotangent, cotangent, other_cotangent, scale, scale, gathered, r, down_t)
+    )(place, cotangent, other_cotangent, scale, gathered, r, down_t)
 
 
 def swap(x, axis):
@@ -183,10 +182,11 @@
     r = lax.dot_general(
         a_ref[...], x_ref[...], (((1,), (1,)), ((), ())), preferred_element_type=F32
     )
-    tail = jnp.concatenate(pieces + [m_ref[...], jnp.zeros((11, 128), BF16)], axis=0)
+    block = jnp.concatenate(
+        [r.astype(BF16)] + pieces + [m_ref[...], jnp.zeros((3, 128), BF16)], axis=0
+    )
     for i in range(o_ref.shape[0]):
-        o_ref[i, :rank] = r.astype(BF16)
-        o_ref[i, rank:] = tail
+        o_ref[i] = block
 
 
 def second_blocks(index, w, down_t, up, tokens, magnitude):
@@ -204,9 +204,9 @@
                 pl.BlockSpec(tokens.shape, whole),
                 pl.BlockSpec((2, 128), whole),
             ],
-            out_specs=pl.BlockSpec((n, rank + 16, 128), lambda i, s: (0, 0, 0)),
-        ),
-        out_shape=jax.ShapeDtypeStruct((n, rank + 16, 128), BF16),
+            out_specs=pl.BlockSpec((n, rank + 8, 128), lambda i, s: (0, 0, 0)),
+        ),
+        out_shape=jax.ShapeDtypeStruct((n, rank + 8, 128), BF16),
         name="second_blocks",
     )(index.reshape(1), w, down_t, up, tokens, magnitude.reshape(2, 128))
 
@@ -299,7 +299,8 @@
     mags = jnp.where(v == 0, mags[:, 0], mags[:, 1]).astype(F32)
     grad_magnitude = jnp.sum(mags, axis=(0, 1, 2)) * factor
 
-    output = cross((merged * at(scale)).astype(BF16))
+    here_output = (merged * at(scale)).astype(BF16)
+    output = jnp.where(v == w, here_output, cross(here_output))
     input_gradient = (own_part + swap(other_part, "w").astype(F32)).astype(BF16)
     return (output, input_gradient, grad_down, grad_up, grad_magnitude)
 

time: 152 us -> 152 us (level)
  waiting for transfers between devices: 19.7 us -> 23.6 us
  Pallas kernels: 14.4 us -> 10.6 us
    all_to_all x1, waiting for transfers between devices: 0.01 us -> 4.27 us  [on_device(): parts = lax.all_to_all(outgoing, TP, 0, 0)]
    pallas_call x1, Pallas kernels: 6.09 us -> 2.37 us  [backward(): pl.pallas_call(backward_kernel, grid_spec=pltpu.PrefetchScalarGridSpec(nu...]
    all_to_all x3, starting transfers between devices: 38.3 us -> 35.2 us  [spread(): lax.all_to_all(jnp.broadcast_to(block[None], (n,) + block.shape), axis, 0...]
    ppermute x7, starting transfers between devices: 20 us -> 22.4 us  [swap(): return lax.ppermute(x, axis, [(0, 1), (1, 0)])]
    unnamed x26 -> x23, local copies, waits for them, and re-layouts: 4.96 us -> 6.35 us
  transfers between devices with their start and end apart: 17 -> 17, of which waited for: 6 -> 6; matrix products, arithmetic and copies ran while one was open for 7% -> 7% of each run, Pallas kernels for 10% -> 7%
where the time goes in v5:
time: 152 us; the launch traced here: 151 us
  starting transfers between devices  83.5 us (55%)
  waiting for transfers between devices  23.6 us (16%)
  between operations  14.6 us (10%)
  local copies, waits for them, and re-layouts  11.2 us (7%)
  Pallas kernels  10.6 us (7%)
  other arithmetic  6.38 us (4%)
    all_to_all x3, starting transfers between devices, spread(): lax.all_to_all(jnp.broadcast_to(block[None], (n,) + block.shape), axis, 0...  35.2 us
    ppermute x7, starting transfers between devices, swap(): return lax.ppermute(x, axis, [(0, 1), (1, 0)])  22.4 us
    ppermute x3, starting transfers between devices, scatter(): total += lax.ppermute(block(k), axis, [(i, (i + k) % n) for i in range(n)])  12.9 us
    ppermute x7, waiting for transfers between devices, swap(): return lax.ppermute(x, axis, [(0, 1), (1, 0)])  8.37 us
    all_to_all x3, waiting for transfers between devices, spread(): lax.all_to_all(jnp.broadcast_to(block[None], (n,) + block.shape), axis, 0...  7.14 us
    all_to_all x1, starting transfers between devices, on_device(): parts = lax.all_to_all(outgoing, TP, 0, 0)  6.95 us
    unnamed x23, local copies, waits for them, and re-layouts  6.35 us
    pallas_call x1, Pallas kernels, forward(): pl.pallas_call(forward_kernel, grid_spec=pltpu.PrefetchScalarGridSpec(num...  6.06 us
  transfers between devices with their start and end apart: 17, of which 6 were waited for; matrix products, arithmetic and copies ran while one was open for 7% of the time, Pallas kernels for 7%

profile of v5, /device:TPU:1, one launch (start us, length us, event | category | flops | bytes accessed | tf_op | source)
XLA Modules:
  0.0 150.7 jit_solution(14642734370145848715)
XLA Ops:
  7.2 0.0 copy-start.1
  7.2 0.0 all-gather.3.cloned.1.call-start
  7.2 0.7 all-gather.3.cloned.1.call-update
  7.9 0.7 slice_select_fusion.1
  8.7 0.7 broadcast_in_dim.10
  9.4 13.4 %all-to-all-start = ((bf16[16,64,128]{2,1,0:T(8,128)(2,1)}), bf16[16,64,128]{2,1,0:T(8,128)(2,1)S(1)}, u32[]{:S(2)}, u32[]{:S(2)}) async-start(bf16[16,64,128]{2,1,0:T(8,128)(2,1)} %broadcast_in_dim.10), calls=%async_computation | async-start | bytes 524288 | tf_op jit(solution)/shard_map/all_to_all | solution.py:20
  22.8 0.9 slice_dynamic-update-slice_fusion.7
  23.7 0.9 slice_dynamic-update-slice_fusion.6
  24.6 0.9 slice_dynamic-update-slice_fusion.5
  25.5 0.9 slice_dynamic-update-slice_fusion.4
  26.4 0.0 copy-start.5
  26.5 0.9 broadcast_select_fusion
  27.4 5.5 %all-to-all-done.b_ref = bf16[16,64,128]{2,1,0:T(8,128)(2,1)S(1)} async-done(((bf16[16,64,128]{2,1,0:T(8,128)(2,1)}), bf16[16,64,128]{2,1,0:T(8,128)(2,1)S(1)}, u32[]{:S(2)}, u32[]{:S(2)}) %all-to-all-start) | async-done | bytes 262176 | tf_op jit(solution)/shard_map/all_to_all | solution.py:20
  32.9 0.7 copy-done.4
  33.6 2.2 %second_blocks.1 = bf16[16,72,128]{2,1,0:T(8,128)(2,1)} custom-call(s32[1]{0:T(128)} %bitcast.i_ref, bf16[896,128]{1,0:T(8,128)(2,1)} %w_ref.1, bf16[64,896]{1,0:T(8,128)(2,1)} %bitcast.38, bf16[16,64,128]{2,1,0:T(8,128)(2,1)} %copy-done.4, bf16[128,896]{1,0:T(8,128)(2,1)} %x_ref.3, bf16[2,128]{1,0:T(2,128)(2,1)} %bitcast.50), custom_call_target="tpu_custom_call" | custom-call | tf_op jit(solution)/shard_map/second_blocks/pallas_call | solution.py:195
  35.8 5.3 %all-to-all-start.1 = ((bf16[16,72,128]{2,1,0:T(8,128)(2,1)}), bf16[16,72,128]{2,1,0:T(8,128)(2,1)S(1)}, u32[]{:S(2)}, u32[]{:S(2)}) async-start(bf16[16,72,128]{2,1,0:T(8,128)(2,1)} %second_blocks.1), calls=%async_computation.1 | async-start | bytes 589824 | tf_op jit(solution)/shard_map/all_to_all | solution.py:234
  41.1 4.0 %collective-permute-start.1 = (bf16[16,64,128]{2,1,0:T(8,128)(2,1)}, bf16[16,64,128]{2,1,0:T(8,128)(2,1)S(1)}, u32[]{:S(2)}, u32[]{:S(2)}) collective-permute-start(bf16[16,64,128]{2,1,0:T(8,128)(2,1)} %copy-done.4), channel_id=1, source_target_pairs={{0,16},{16,0},{1,17},{17,1},{2,18},{18,2},{3,19},{19,3},{4,20},{20... | collective-permute-start | bytes 786440 | tf_op jit(solution)/shard_map/ppermute | solution.py:133
  45.1 2.9 %collective-permute-start = (bf16[128,896]{1,0:T(8,128)(2,1)S(1)}, bf16[128,896]{1,0:T(8,128)(2,1)}, u32[]{:S(2)}, u32[]{:S(2)}) collective-permute-start(bf16[128,896]{1,0:T(8,128)(2,1)S(1)} %copy-done.5), channel_id=1, source_target_pairs={{0,32},{32,0},{1,33},{33,1},{2,34},{34,2},{3,35},{35,3},{4,36},{36... | collective-permute-start | bytes 688136 | tf_op jit(solution)/shard_map/ppermute | solution.py:133
  48.0 0.6 pad_add_fusion.i_ref
  48.6 2.4 %collective-permute-start.2 = (bf16[128,2048]{1,0:T(8,128)(2,1)}, bf16[128,2048]{1,0:T(8,128)(2,1)S(1)}, u32[]{:S(2)}, u32[]{:S(2)}) collective-permute-start(bf16[128,2048]{1,0:T(8,128)(2,1)} %broadcast_select_fusion), channel_id=1, source_target_pairs={{0,32},{32,0},{1,33},{33,1},{2,34},{34,2},{3,35},{35,3},{4,36},{36... | collective-permute-start | bytes 1572872 | tf_op jit(solution)/shard_map/ppermute | solution.py:133
  51.0 0.0 collective-permute-done.1.c_ref
  51.0 1.2 fusion
  52.2 0.5 copy.14
  52.8 0.4 reshape.86
  53.2 0.6 broadcast_in_dim.11
  53.8 10.9 %all-to-all-start.2 = ((f32[32,1,128]{2,1,0:T(1,128)}), f32[32,1,128]{2,1,0:T(1,128)S(1)}, u32[]{:S(2)}, u32[]{:S(2)}) async-start(f32[32,1,128]{2,1,0:T(1,128)} %broadcast_in_dim.11), calls=%async_computation.2 | async-start | bytes 32768 | tf_op jit(solution)/shard_map/all_to_all | solution.py:20
  64.8 0.0 collective-permute-done.o_ref
  64.8 0.0 all-gather.3.cloned.1.call-done
  64.9 6.1 %forward.1 = bf16[16,128,256]{2,1,0:T(8,128)(2,1)} custom-call(s32[2]{0:T(128)} %pad_add_fusion.i_ref, bf16[128,896]{1,0:T(8,128)(2,1)} %x_ref.3, bf16[128,896]{1,0:T(8,128)(2,1)} %collective-permute-done.o_ref, bf16[64,896]{1,0:T(8,128)(2,1)} %bitcast.39, bf16[16,64,128]{2,1,0:T(8,128)(2,1)} %copy-done.4, bf16[16,64,128]{2,1,0:T(8,128)(2,1)} %copy-done.7, ...), custom_call_target="tpu_custom_call" | custom-call | flops 939524096 | bytes 3670016 | tf_op jit(solution)/shard_map/forward/pallas_call | solution.py:51
  70.9 1.6 %all-to-all-done.2 = f32[32,1,128]{2,1,0:T(1,128)S(1)} async-done(((f32[32,1,128]{2,1,0:T(1,128)}), f32[32,1,128]{2,1,0:T(1,128)S(1)}, u32[]{:S(2)}, u32[]{:S(2)}) %all-to-all-start.2) | async-done | bytes 16416 | tf_op jit(solution)/shard_map/all_to_all | solution.py:20
  72.6 0.2 multiply_convert_fusion
  72.8 0.4 convolution_convert_fusion.r_ref
  73.2 0.2 fusion.8
  73.4 0.1 fusion.2
  73.6 2.7 %collective-permute-start.3 = (f32[32,1152]{1,0:T(8,128)S(1)}, f32[32,1152]{1,0:T(8,128)S(1)}, u32[]{:S(2)}, u32[]{:S(2)}) collective-permute-start(f32[32,1152]{1,0:T(8,128)S(1)} %broadcast_select_fusion.2), channel_id=1, source_target_pairs={{0,16},{16,0},{1,17},{17,1},{2,18},{18,2},{3,19},{19,3},{4,20},{20... | collective-permute-start | bytes 442376 | tf_op jit(solution)/shard_map/ppermute | solution.py:133
  76.3 1.0 collective-permute-done.3
  77.3 2.3 %collective-permute-start.4 = (f32[16,1152]{1,0:T(8,128)S(1)}, f32[16,1152]{1,0:T(8,128)S(1)}, u32[]{:S(2)}, u32[]{:S(2)}) collective-permute-start(f32[16,1152]{1,0:T(8,128)S(1)} %slice_select_fusion), channel_id=1, source_target_pairs={{0,64},{64,0},{1,65},{65,1},{2,66},{66,2},{3,67},{67,3},{4,68},{68... | collective-permute-start | bytes 221192 | tf_op jit(solution)/shard_map/ppermute | solution.py:133
  79.6 7.0 %all-to-all-start.3 = ((bf16[16,128,256]{2,1,0:T(8,128)(2,1)}), bf16[16,128,256]{2,1,0:T(8,128)(2,1)S(1)}, u32[]{:S(2)}, u32[]{:S(2)}) async-start(bf16[16,128,256]{2,1,0:T(8,128)(2,1)} %forward.1), calls=%async_computation.3 | async-start | bytes 2097152 | tf_op jit(solution)/shard_map/all_to_all | solution.py:248
  86.7 3.4 %collective-permute-start.5 = (f32[4,1152]{1,0:T(4,128)S(1)}, f32[4,1152]{1,0:T(4,128)S(1)}, u32[]{:S(2)}, u32[]{:S(2)}) collective-permute-start(f32[4,1152]{1,0:T(4,128)S(1)} %get-tuple-element.57), channel_id=1, source_target_pairs={{0,128},{128,256},{256,384},{384,0},{1,129},{129,257},{257,385},{3... | collective-permute-start | bytes 55304 | tf_op jit(solution)/shard_map/ppermute | solution.py:168
  90.1 4.0 %collective-permute-start.7 = (f32[4,1152]{1,0:T(4,128)S(1)}, f32[4,1152]{1,0:T(4,128)S(1)}, u32[]{:S(2)}, u32[]{:S(2)}) collective-permute-start(f32[4,1152]{1,0:T(4,128)S(1)} %get-tuple-element.58), channel_id=1, source_target_pairs={{0,384},{128,0},{256,128},{384,256},{1,385},{129,1},{257,129},{385... | collective-permute-start | bytes 55304 | tf_op jit(solution)/shard_map/ppermute | solution.py:168
  94.1 5.5 %collective-permute-start.6 = (f32[4,1152]{1,0:T(4,128)S(1)}, f32[4,1152]{1,0:T(4,128)S(1)}, u32[]{:S(2)}, u32[]{:S(2)}) collective-permute-start(f32[4,1152]{1,0:T(4,128)S(1)} %get-tuple-element.59), channel_id=1, source_target_pairs={{0,256},{128,384},{256,0},{384,128},{1,257},{129,385},{257,1},{385... | collective-permute-start | bytes 55304 | tf_op jit(solution)/shard_map/ppermute | solution.py:168
  99.7 0.0 collective-permute-done.5
  99.7 3.1 %collective-permute-done.6 = f32[4,1152]{1,0:T(4,128)S(1)} collective-permute-done((f32[4,1152]{1,0:T(4,128)S(1)}, f32[4,1152]{1,0:T(4,128)S(1)}, u32[]{:S(2)}, u32[]{:S(2)}) %collective-permute-start.6) | collective-permute-done | bytes 18464 | tf_op jit(solution)/shard_map/ppermute | solution.py:168
  102.8 2.5 %collective-permute-start.8 = (f32[2,1152]{1,0:T(2,128)S(1)}, f32[2,1152]{1,0:T(2,128)S(1)}, u32[]{:S(2)}, u32[]{:S(2)}) collective-permute-start(f32[2,1152]{1,0:T(2,128)S(1)} %broadcast_select_fusion.5), channel_id=1, source_target_pairs={{0,32},{32,0},{1,33},{33,1},{2,34},{34,2},{3,35},{35,3},{4,36},{36... | collective-permute-start | bytes 27656 | tf_op jit(solution)/shard_map/ppermute | solution.py:133
  105.4 2.0 %copy-done = bf16[14336,128]{1,0:T(8,128)(2,1)S(1)} copy-done((bf16[14336,128]{1,0:T(8,128)(2,1)S(1)}, bf16[14336,128]{1,0:T(8,128)(2,1)}, u32[]{:S(2)}) %copy-start) | copy-done | bytes 3670040
  107.4 2.4 %backward.1 = (f32[128,896]{1,0:T(8,128)S(1)}, bf16[128,896]{1,0:T(8,128)(2,1)S(1)}) custom-call(s32[2]{0:T(128)S(1)} %copy-done.3, bf16[128,4096]{1,0:T(8,128)(2,1)S(1)} %copy-done.1, bf16[128,2048]{1,0:T(8,128)(2,1)S(1)} %collective-permute-done.2.h_ref, f32[1,4096]{1,0:T(1,128)S(1)} %bitcast_multiply_fusion.s_ref, bf16[16,896,128]{2,1,0:T(8,128)(2,1)S(1)} %bitcast.37, ...), custom_call_target="tpu_custom_call" | custom-call | flops 939524096 | bytes 3670016 | tf_op jit(solution)/shard_map/backward/pallas_call | solution.py:104
  109.8 0.0 collective-permute-done.8
  109.8 4.3 %all-to-all-done.3 = bf16[16,128,256]{2,1,0:T(8,128)(2,1)S(1)} async-done(((bf16[16,128,256]{2,1,0:T(8,128)(2,1)}), bf16[16,128,256]{2,1,0:T(8,128)(2,1)S(1)}, u32[]{:S(2)}, u32[]{:S(2)}) %all-to-all-start.3) | async-done | bytes 1048608 | tf_op jit(solution)/shard_map/all_to_all | solution.py:248
  114.1 0.1 convert_reduce_fusion
  114.2 0.1 multiply_reduce_fusion
  114.3 0.1 reduce-precision_convert_fusion
  114.4 0.9 broadcast_in_dim.14
  115.3 10.9 %all-to-all-start.4 = ((bf16[64,2,1408]{2,1,0:T(2,128)(2,1)}), bf16[64,2,1408]{2,1,0:T(2,128)(2,1)S(1)}, u32[]{:S(2)}, u32[]{:S(2)}) async-start(bf16[64,2,1408]{2,1,0:T(2,128)(2,1)} %broadcast_in_dim.14), calls=%async_computation.4 | async-start | bytes 720896 | tf_op jit(solution)/shard_map/all_to_all | solution.py:20
  126.3 0.7 collective-permute-start.9
  127.0 5.7 %collective-permute-start.10 = (bf16[128,896]{1,0:T(8,128)(2,1)S(1)}, bf16[128,896]{1,0:T(8,128)(2,1)S(1)}, u32[]{:S(2)}, u32[]{:S(2)}) collective-permute-start(bf16[128,896]{1,0:T(8,128)(2,1)S(1)} %get-tuple-element.37), channel_id=1, source_target_pairs={{0,32},{32,0},{1,33},{33,1},{2,34},{34,2},{3,35},{35,3},{4,36},{36... | collective-permute-start | bytes 688136 | tf_op jit(solution)/shard_map/ppermute | solution.py:133
  132.7 0.7 broadcast_select_fusion.4
  133.3 7.4 %collective-permute-done.10 = bf16[128,896]{1,0:T(8,128)(2,1)S(1)} collective-permute-done((bf16[128,896]{1,0:T(8,128)(2,1)S(1)}, bf16[128,896]{1,0:T(8,128)(2,1)S(1)}, u32[]{:S(2)}, u32[]{:S(2)}) %collective-permute-start.10) | collective-permute-done | bytes 229408 | tf_op jit(solution)/shard_map/ppermute | solution.py:133
  140.7 0.7 add_convert_fusion
  141.4 0.1 convert_reduce_fusion.1
  141.5 0.2 convert_multiply_fusion
  141.7 0.2 mul.73
  141.9 0.6 slice.154
  142.6 0.7 slice_bitcast_fusion
  143.3 0.6 broadcast_multiply_fusion
  (42 shorter events, 0.4 us)
Async XLA Ops:
  7.2 19.2 %copy-start.1 = (bf16[128,4096]{1,0:T(8,128)(2,1)S(1)}, bf16[128,4096]{1,0:T(8,128)(2,1)}, u32[]{:S(2)}) copy-start(bf16[128,4096]{1,0:T(8,128)(2,1)} %g_ref.1) | copy-start | bytes 3145732
  7.2 57.7 %all-gather.3.cloned.1.call-start = ((), (), s32[]{:S(2)}) async-start(), calls=%async_computation.5 | async-start | bytes 3899392 | tf_op jit(solution)/shard_map/all_gather | solution.py:223
  9.4 23.5 %all-to-all-start = ((bf16[16,64,128]{2,1,0:T(8,128)(2,1)}), bf16[16,64,128]{2,1,0:T(8,128)(2,1)S(1)}, u32[]{:S(2)}, u32[]{:S(2)}) async-start(bf16[16,64,128]{2,1,0:T(8,128)(2,1)} %broadcast_in_dim.10), calls=%async_computation | async-start | bytes 524288 | tf_op jit(solution)/shard_map/all_to_all | solution.py:20
  26.4 18.7 %copy-start.5 = (bf16[128,896]{1,0:T(8,128)(2,1)S(1)}, bf16[128,896]{1,0:T(8,128)(2,1)}, u32[]{:S(2)}) copy-start(bf16[128,896]{1,0:T(8,128)(2,1)} %x_ref.3) | copy-start | bytes 688132
  32.9 0.7 copy-start.4
  35.8 17.4 %all-to-all-start.1 = ((bf16[16,72,128]{2,1,0:T(8,128)(2,1)}), bf16[16,72,128]{2,1,0:T(8,128)(2,1)S(1)}, u32[]{:S(2)}, u32[]{:S(2)}) async-start(bf16[16,72,128]{2,1,0:T(8,128)(2,1)} %second_blocks.1), calls=%async_computation.1 | async-start | bytes 589824 | tf_op jit(solution)/shard_map/all_to_all | solution.py:234
  41.1 9.9 %collective-permute-start.1 = (bf16[16,64,128]{2,1,0:T(8,128)(2,1)}, bf16[16,64,128]{2,1,0:T(8,128)(2,1)S(1)}, u32[]{:S(2)}, u32[]{:S(2)}) collective-permute-start(bf16[16,64,128]{2,1,0:T(8,128)(2,1)} %copy-done.4), channel_id=1, source_target_pairs={{0,16},{16,0},{1,17},{17,1},{2,18},{18,2},{3,19},{19,3},{4,20},{20... | collective-permute-start | bytes 786440 | tf_op jit(solution)/shard_map/ppermute | solution.py:133
  45.1 19.7 %collective-permute-start = (bf16[128,896]{1,0:T(8,128)(2,1)S(1)}, bf16[128,896]{1,0:T(8,128)(2,1)}, u32[]{:S(2)}, u32[]{:S(2)}) collective-permute-start(bf16[128,896]{1,0:T(8,128)(2,1)S(1)} %copy-done.5), channel_id=1, source_target_pairs={{0,32},{32,0},{1,33},{33,1},{2,34},{34,2},{3,35},{35,3},{4,36},{36... | collective-permute-start | bytes 688136 | tf_op jit(solution)/shard_map/ppermute | solution.py:133
  48.6 22.3 %collective-permute-start.2 = (bf16[128,2048]{1,0:T(8,128)(2,1)}, bf16[128,2048]{1,0:T(8,128)(2,1)S(1)}, u32[]{:S(2)}, u32[]{:S(2)}) collective-permute-start(bf16[128,2048]{1,0:T(8,128)(2,1)} %broadcast_select_fusion), channel_id=1, source_target_pairs={{0,32},{32,0},{1,33},{33,1},{2,34},{34,2},{3,35},{35,3},{4,36},{36... | collective-permute-start | bytes 1572872 | tf_op jit(solution)/shard_map/ppermute | solution.py:133
  51.0 13.8 %copy-start.7 = (bf16[16,64,128]{2,1,0:T(8,128)(2,1)}, bf16[16,64,128]{2,1,0:T(8,128)(2,1)S(1)}, u32[]{:S(2)}) copy-start(bf16[16,64,128]{2,1,0:T(8,128)(2,1)S(1)} %collective-permute-done.1.c_ref) | copy-start | bytes 786436
  53.8 18.7 %all-to-all-start.2 = ((f32[32,1,128]{2,1,0:T(1,128)}), f32[32,1,128]{2,1,0:T(1,128)S(1)}, u32[]{:S(2)}, u32[]{:S(2)}) async-start(f32[32,1,128]{2,1,0:T(1,128)} %broadcast_in_dim.11), calls=%async_computation.2 | async-start | bytes 32768 | tf_op jit(solution)/shard_map/all_to_all | solution.py:20
  70.9 2.3 %copy-start.6 = (bf16[128,896]{1,0:T(8,128)(2,1)S(1)}, bf16[128,896]{1,0:T(8,128)(2,1)}, u32[]{:S(2)}) copy-start(bf16[128,896]{1,0:T(8,128)(2,1)} %x_ref.3) | copy-start | bytes 688132
  73.6 31.8 %copy-start.2 = (bf16[896,64]{0,1:T(8,128)(2,1)S(1)}, bf16[896,64]{0,1:T(8,128)(2,1)}, u32[]{:S(2)}) copy-start(bf16[896,64]{0,1:T(8,128)(2,1)} %param.8) | copy-start | bytes 344068
  73.6 31.8 %copy-start.3 = (s32[2]{0:T(128)S(1)}, s32[2]{0:T(128)}, u32[]{:S(2)}) copy-start(s32[2]{0:T(128)} %pad_add_fusion.i_ref) | copy-start | bytes 28
  73.6 3.6 %collective-permute-start.3 = (f32[32,1152]{1,0:T(8,128)S(1)}, f32[32,1152]{1,0:T(8,128)S(1)}, u32[]{:S(2)}, u32[]{:S(2)}) collective-permute-start(f32[32,1152]{1,0:T(8,128)S(1)} %broadcast_select_fusion.2), channel_id=1, source_target_pairs={{0,16},{16,0},{1,17},{17,1},{2,18},{18,2},{3,19},{19,3},{4,20},{20... | collective-permute-start | bytes 442376 | tf_op jit(solution)/shard_map/ppermute | solution.py:133
  77.3 9.3 %collective-permute-start.4 = (f32[16,1152]{1,0:T(8,128)S(1)}, f32[16,1152]{1,0:T(8,128)S(1)}, u32[]{:S(2)}, u32[]{:S(2)}) collective-permute-start(f32[16,1152]{1,0:T(8,128)S(1)} %slice_select_fusion), channel_id=1, source_target_pairs={{0,64},{64,0},{1,65},{65,1},{2,66},{66,2},{3,67},{67,3},{4,68},{68... | collective-permute-start | bytes 221192 | tf_op jit(solution)/shard_map/ppermute | solution.py:133
  79.6 34.4 %all-to-all-start.3 = ((bf16[16,128,256]{2,1,0:T(8,128)(2,1)}), bf16[16,128,256]{2,1,0:T(8,128)(2,1)S(1)}, u32[]{:S(2)}, u32[]{:S(2)}) async-start(bf16[16,128,256]{2,1,0:T(8,128)(2,1)} %forward.1), calls=%async_computation.3 | async-start | bytes 2097152 | tf_op jit(solution)/shard_map/all_to_all | solution.py:248
  86.7 13.0 %collective-permute-start.5 = (f32[4,1152]{1,0:T(4,128)S(1)}, f32[4,1152]{1,0:T(4,128)S(1)}, u32[]{:S(2)}, u32[]{:S(2)}) collective-permute-start(f32[4,1152]{1,0:T(4,128)S(1)} %get-tuple-element.57), channel_id=1, source_target_pairs={{0,128},{128,256},{256,384},{384,0},{1,129},{129,257},{257,385},{3... | collective-permute-start | bytes 55304 | tf_op jit(solution)/shard_map/ppermute | solution.py:168
  90.1 9.6 %collective-permute-start.7 = (f32[4,1152]{1,0:T(4,128)S(1)}, f32[4,1152]{1,0:T(4,128)S(1)}, u32[]{:S(2)}, u32[]{:S(2)}) collective-permute-start(f32[4,1152]{1,0:T(4,128)S(1)} %get-tuple-element.58), channel_id=1, source_target_pairs={{0,384},{128,0},{256,128},{384,256},{1,385},{129,1},{257,129},{385... | collective-permute-start | bytes 55304 | tf_op jit(solution)/shard_map/ppermute | solution.py:168
  94.1 8.7 %collective-permute-start.6 = (f32[4,1152]{1,0:T(4,128)S(1)}, f32[4,1152]{1,0:T(4,128)S(1)}, u32[]{:S(2)}, u32[]{:S(2)}) collective-permute-start(f32[4,1152]{1,0:T(4,128)S(1)} %get-tuple-element.59), channel_id=1, source_target_pairs={{0,256},{128,384},{256,0},{384,128},{1,257},{129,385},{257,1},{385... | collective-permute-start | bytes 55304 | tf_op jit(solution)/shard_map/ppermute | solution.py:168
  102.8 7.0 %collective-permute-start.8 = (f32[2,1152]{1,0:T(2,128)S(1)}, f32[2,1152]{1,0:T(2,128)S(1)}, u32[]{:S(2)}, u32[]{:S(2)}) collective-permute-start(f32[2,1152]{1,0:T(2,128)S(1)} %broadcast_select_fusion.5), channel_id=1, source_target_pairs={{0,32},{32,0},{1,33},{33,1},{2,34},{34,2},{3,35},{35,3},{4,36},{36... | collective-permute-start | bytes 27656 | tf_op jit(solution)/shard_map/ppermute | solution.py:133
  105.4 2.0 %copy-start = (bf16[14336,128]{1,0:T(8,128)(2,1)S(1)}, bf16[14336,128]{1,0:T(8,128)(2,1)}, u32[]{:S(2)}) copy-start(bf16[14336,128]{1,0:T(8,128)(2,1)} %all-gather.3.cloned.1.call-done) | copy-start | bytes 11010052
  115.3 26.1 %all-to-all-start.4 = ((bf16[64,2,1408]{2,1,0:T(2,128)(2,1)}), bf16[64,2,1408]{2,1,0:T(2,128)(2,1)S(1)}, u32[]{:S(2)}, u32[]{:S(2)}) async-start(bf16[64,2,1408]{2,1,0:T(2,128)(2,1)} %broadcast_in_dim.14), calls=%async_computation.4 | async-start | bytes 720896 | tf_op jit(solution)/shard_map/all_to_all | solution.py:20
  126.3 6.4 %collective-permute-start.9 = (bf16[128,256]{1,0:T(8,128)(2,1)S(1)}, bf16[128,256]{1,0:T(8,128)(2,1)S(1)}, u32[]{:S(2)}, u32[]{:S(2)}) collective-permute-start(bf16[128,256]{1,0:T(8,128)(2,1)S(1)} %multiply_convert_fusion.1), channel_id=1, source_target_pairs={{0,0},{1,32},{32,1},{33,33},{2,2},{3,34},{34,3},{35,35},{4,4},{5,3... | collective-permute-start | bytes 196616 | tf_op jit(solution)/shard_map/ppermute | solution.py:137
  127.0 13.7 %collective-permute-start.10 = (bf16[128,896]{1,0:T(8,128)(2,1)S(1)}, bf16[128,896]{1,0:T(8,128)(2,1)S(1)}, u32[]{:S(2)}, u32[]{:S(2)}) collective-permute-start(bf16[128,896]{1,0:T(8,128)(2,1)S(1)} %get-tuple-element.37), channel_id=1, source_target_pairs={{0,32},{32,0},{1,33},{33,1},{2,34},{34,2},{3,35},{35,3},{4,36},{36... | collective-permute-start | bytes 688136 | tf_op jit(solution)/shard_map/ppermute | solution.py:133
Sparse Core Ops, SparseCore 0:
  10.1 49.9 all-gather.2

commit v6 on v5

--- a/solution.py
+++ b/solution.py
@@ -230,7 +230,7 @@
 
     index = (2 * g + h) * 2 + w
     second = second_blocks(index, frozen_matrix, down_t, own_half, tokens, magnitude)
-    second, cotangent_out, own_half = tie((second, cotangent_out, own_half))
+    second, cotangent_out = tie((second, cotangent_out))
     second = lax.all_to_all(second, TP, 0, 0)
     squares = second[:, rank : rank + 3].astype(F32)
     squares = jnp.sum(squares, axis=(0, 1)).reshape(1, 128)
@@ -282,14 +282,14 @@
         lax.dynamic_slice_in_dim(cotangent, here * own, own, 1),
         lax.dynamic_slice_in_dim(other_cotangent, block * own, own, 1),
     ).astype(F32)
-    mag_part = jnp.sum(here_cotangent * merged, axis=0) / at(norm)
+    factor = 1.0 / math.sqrt(t * n_dp)
+    mag_part = jnp.sum(here_cotangent * merged, axis=0) / at(norm) * factor
 
     high = lax.reduce_precision(mag_part, 8, 7)
     mag_part = jnp.stack([high, mag_part - high]).astype(BF16)
     last = jnp.concatenate([shares.astype(BF16), mag_part], axis=1)
     last, merged, other_part = tie((last, merged, other_part))
     last = spread(last, ("c", "h", "g", "w", "v")).reshape(n_dp // 2, 2, 2, 2, f + 2 * own)
-    factor = 1.0 / math.sqrt(t * n_dp)
     sums = last[..., : f + own]
     sums = jnp.where(v == 0, sums[:, :, 0], sums[:, :, 1]).astype(F32)
     sums = sums.reshape(rank, f + own) * factor
@@ -297,7 +297,7 @@
     grad_up = sums[:, f:]
     mags = last[..., f + own :]
     mags = jnp.where(v == 0, mags[:, 0], mags[:, 1]).astype(F32)
-    grad_magnitude = jnp.sum(mags, axis=(0, 1, 2)) * factor
+    grad_magnitude = jnp.sum(mags, axis=(0, 1, 2))
 
     here_output = (merged * at(scale)).astype(BF16)
     output = jnp.where(v == w, here_output, cross(here_output))

time: 152 us -> 152 us (level)
  no operation moved by 1% of the time
where the time goes in v6:
time: 152 us; the launch traced here: 151 us
  starting transfers between devices  83.5 us (55%)
  waiting for transfers between devices  23.6 us (16%)
  between operations  14.6 us (10%)
  local copies, waits for them, and re-layouts  11.2 us (7%)
  Pallas kernels  10.6 us (7%)
  other arithmetic  6.38 us (4%)
    all_to_all x3, starting transfers between devices, spread(): lax.all_to_all(jnp.broadcast_to(block[None], (n,) + block.shape), axis, 0...  35.2 us
    ppermute x7, starting transfers between devices, swap(): return lax.ppermute(x, axis, [(0, 1), (1, 0)])  22.4 us
    ppermute x3, starting transfers between devices, scatter(): total += lax.ppermute(block(k), axis, [(i, (i + k) % n) for i in range(n)])  12.9 us
    ppermute x7, waiting for transfers between devices, swap(): return lax.ppermute(x, axis, [(0, 1), (1, 0)])  8.37 us
    all_to_all x3, waiting for transfers between devices, spread(): lax.all_to_all(jnp.broadcast_to(block[None], (n,) + block.shape), axis, 0...  7.14 us
    all_to_all x1, starting transfers between devices, on_device(): parts = lax.all_to_all(outgoing, TP, 0, 0)  6.95 us
    unnamed x23, local copies, waits for them, and re-layouts  6.35 us
    pallas_call x1, Pallas kernels, forward(): pl.pallas_call(forward_kernel, grid_spec=pltpu.PrefetchScalarGridSpec(num...  6.06 us
  transfers between devices with their start and end apart: 17, of which 6 were waited for; matrix products, arithmetic and copies ran while one was open for 7% of the time, Pallas kernels for 7%

profile of v6, /device:TPU:1, one launch (start us, length us, event | category | flops | bytes accessed | tf_op | source)
XLA Modules:
  0.0 150.7 jit_solution(4374728153369817661)
XLA Ops:
  7.2 0.0 copy-start.1
  7.2 0.0 all-gather.3.cloned.1.call-start
  7.2 0.7 all-gather.3.cloned.1.call-update
  7.9 0.7 slice_select_fusion.1
  8.7 0.7 broadcast_in_dim.10
  9.4 13.4 %all-to-all-start = ((bf16[16,64,128]{2,1,0:T(8,128)(2,1)}), bf16[16,64,128]{2,1,0:T(8,128)(2,1)S(1)}, u32[]{:S(2)}, u32[]{:S(2)}) async-start(bf16[16,64,128]{2,1,0:T(8,128)(2,1)} %broadcast_in_dim.10), calls=%async_computation | async-start | bytes 524288 | tf_op jit(solution)/shard_map/all_to_all | solution.py:20
  22.8 0.9 slice_dynamic-update-slice_fusion.7
  23.7 0.9 slice_dynamic-update-slice_fusion.6
  24.6 0.9 slice_dynamic-update-slice_fusion.5
  25.5 0.9 slice_dynamic-update-slice_fusion.4
  26.4 0.0 copy-start.5
  26.5 0.9 broadcast_select_fusion
  27.4 5.5 %all-to-all-done.b_ref = bf16[16,64,128]{2,1,0:T(8,128)(2,1)S(1)} async-done(((bf16[16,64,128]{2,1,0:T(8,128)(2,1)}), bf16[16,64,128]{2,1,0:T(8,128)(2,1)S(1)}, u32[]{:S(2)}, u32[]{:S(2)}) %all-to-all-start) | async-done | bytes 262176 | tf_op jit(solution)/shard_map/all_to_all | solution.py:20
  32.9 0.7 copy-done.4
  33.6 2.2 %second_blocks.1 = bf16[16,72,128]{2,1,0:T(8,128)(2,1)} custom-call(s32[1]{0:T(128)} %bitcast.i_ref, bf16[896,128]{1,0:T(8,128)(2,1)} %w_ref.1, bf16[64,896]{1,0:T(8,128)(2,1)} %bitcast.38, bf16[16,64,128]{2,1,0:T(8,128)(2,1)} %copy-done.4, bf16[128,896]{1,0:T(8,128)(2,1)} %x_ref.3, bf16[2,128]{1,0:T(2,128)(2,1)} %bitcast.50), custom_call_target="tpu_custom_call" | custom-call | tf_op jit(solution)/shard_map/second_blocks/pallas_call | solution.py:195
  35.8 5.3 %all-to-all-start.1 = ((bf16[16,72,128]{2,1,0:T(8,128)(2,1)}), bf16[16,72,128]{2,1,0:T(8,128)(2,1)S(1)}, u32[]{:S(2)}, u32[]{:S(2)}) async-start(bf16[16,72,128]{2,1,0:T(8,128)(2,1)} %second_blocks.1), calls=%async_computation.1 | async-start | bytes 589824 | tf_op jit(solution)/shard_map/all_to_all | solution.py:234
  41.1 4.0 %collective-permute-start.1 = (bf16[16,64,128]{2,1,0:T(8,128)(2,1)}, bf16[16,64,128]{2,1,0:T(8,128)(2,1)S(1)}, u32[]{:S(2)}, u32[]{:S(2)}) collective-permute-start(bf16[16,64,128]{2,1,0:T(8,128)(2,1)} %copy-done.4), channel_id=1, source_target_pairs={{0,16},{16,0},{1,17},{17,1},{2,18},{18,2},{3,19},{19,3},{4,20},{20... | collective-permute-start | bytes 786440 | tf_op jit(solution)/shard_map/ppermute | solution.py:133
  45.1 2.9 %collective-permute-start = (bf16[128,896]{1,0:T(8,128)(2,1)S(1)}, bf16[128,896]{1,0:T(8,128)(2,1)}, u32[]{:S(2)}, u32[]{:S(2)}) collective-permute-start(bf16[128,896]{1,0:T(8,128)(2,1)S(1)} %copy-done.5), channel_id=1, source_target_pairs={{0,32},{32,0},{1,33},{33,1},{2,34},{34,2},{3,35},{35,3},{4,36},{36... | collective-permute-start | bytes 688136 | tf_op jit(solution)/shard_map/ppermute | solution.py:133
  48.0 0.6 pad_add_fusion.i_ref
  48.6 2.4 %collective-permute-start.2 = (bf16[128,2048]{1,0:T(8,128)(2,1)}, bf16[128,2048]{1,0:T(8,128)(2,1)S(1)}, u32[]{:S(2)}, u32[]{:S(2)}) collective-permute-start(bf16[128,2048]{1,0:T(8,128)(2,1)} %broadcast_select_fusion), channel_id=1, source_target_pairs={{0,32},{32,0},{1,33},{33,1},{2,34},{34,2},{3,35},{35,3},{4,36},{36... | collective-permute-start | bytes 1572872 | tf_op jit(solution)/shard_map/ppermute | solution.py:133
  51.0 0.0 collective-permute-done.1.c_ref
  51.0 1.2 fusion
  52.2 0.5 copy.14
  52.8 0.4 reshape.86
  53.2 0.6 broadcast_in_dim.11
  53.8 10.9 %all-to-all-start.2 = ((f32[32,1,128]{2,1,0:T(1,128)}), f32[32,1,128]{2,1,0:T(1,128)S(1)}, u32[]{:S(2)}, u32[]{:S(2)}) async-start(f32[32,1,128]{2,1,0:T(1,128)} %broadcast_in_dim.11), calls=%async_computation.2 | async-start | bytes 32768 | tf_op jit(solution)/shard_map/all_to_all | solution.py:20
  64.8 0.0 collective-permute-done.o_ref
  64.8 0.0 all-gather.3.cloned.1.call-done
  64.9 6.1 %forward.1 = bf16[16,128,256]{2,1,0:T(8,128)(2,1)} custom-call(s32[2]{0:T(128)} %pad_add_fusion.i_ref, bf16[128,896]{1,0:T(8,128)(2,1)} %x_ref.3, bf16[128,896]{1,0:T(8,128)(2,1)} %collective-permute-done.o_ref, bf16[64,896]{1,0:T(8,128)(2,1)} %bitcast.39, bf16[16,64,128]{2,1,0:T(8,128)(2,1)} %copy-done.4, bf16[16,64,128]{2,1,0:T(8,128)(2,1)} %copy-done.7, ...), custom_call_target="tpu_custom_call" | custom-call | flops 939524096 | bytes 3670016 | tf_op jit(solution)/shard_map/forward/pallas_call | solution.py:51
  70.9 1.6 %all-to-all-done.2 = f32[32,1,128]{2,1,0:T(1,128)S(1)} async-done(((f32[32,1,128]{2,1,0:T(1,128)}), f32[32,1,128]{2,1,0:T(1,128)S(1)}, u32[]{:S(2)}, u32[]{:S(2)}) %all-to-all-start.2) | async-done | bytes 16416 | tf_op jit(solution)/shard_map/all_to_all | solution.py:20
  72.6 0.2 multiply_convert_fusion
  72.8 0.4 convolution_convert_fusion.r_ref
  73.2 0.2 fusion.8
  73.4 0.1 fusion.2
  73.6 2.7 %collective-permute-start.3 = (f32[32,1152]{1,0:T(8,128)S(1)}, f32[32,1152]{1,0:T(8,128)S(1)}, u32[]{:S(2)}, u32[]{:S(2)}) collective-permute-start(f32[32,1152]{1,0:T(8,128)S(1)} %broadcast_select_fusion.2), channel_id=1, source_target_pairs={{0,16},{16,0},{1,17},{17,1},{2,18},{18,2},{3,19},{19,3},{4,20},{20... | collective-permute-start | bytes 442376 | tf_op jit(solution)/shard_map/ppermute | solution.py:133
  76.3 1.0 collective-permute-done.3
  77.3 2.3 %collective-permute-start.4 = (f32[16,1152]{1,0:T(8,128)S(1)}, f32[16,1152]{1,0:T(8,128)S(1)}, u32[]{:S(2)}, u32[]{:S(2)}) collective-permute-start(f32[16,1152]{1,0:T(8,128)S(1)} %slice_select_fusion), channel_id=1, source_target_pairs={{0,64},{64,0},{1,65},{65,1},{2,66},{66,2},{3,67},{67,3},{4,68},{68... | collective-permute-start | bytes 221192 | tf_op jit(solution)/shard_map/ppermute | solution.py:133
  79.6 7.0 %all-to-all-start.3 = ((bf16[16,128,256]{2,1,0:T(8,128)(2,1)}), bf16[16,128,256]{2,1,0:T(8,128)(2,1)S(1)}, u32[]{:S(2)}, u32[]{:S(2)}) async-start(bf16[16,128,256]{2,1,0:T(8,128)(2,1)} %forward.1), calls=%async_computation.3 | async-start | bytes 2097152 | tf_op jit(solution)/shard_map/all_to_all | solution.py:248
  86.7 3.4 %collective-permute-start.5 = (f32[4,1152]{1,0:T(4,128)S(1)}, f32[4,1152]{1,0:T(4,128)S(1)}, u32[]{:S(2)}, u32[]{:S(2)}) collective-permute-start(f32[4,1152]{1,0:T(4,128)S(1)} %get-tuple-element.55), channel_id=1, source_target_pairs={{0,128},{128,256},{256,384},{384,0},{1,129},{129,257},{257,385},{3... | collective-permute-start | bytes 55304 | tf_op jit(solution)/shard_map/ppermute | solution.py:168
  90.1 4.0 %collective-permute-start.7 = (f32[4,1152]{1,0:T(4,128)S(1)}, f32[4,1152]{1,0:T(4,128)S(1)}, u32[]{:S(2)}, u32[]{:S(2)}) collective-permute-start(f32[4,1152]{1,0:T(4,128)S(1)} %get-tuple-element.56), channel_id=1, source_target_pairs={{0,384},{128,0},{256,128},{384,256},{1,385},{129,1},{257,129},{385... | collective-permute-start | bytes 55304 | tf_op jit(solution)/shard_map/ppermute | solution.py:168
  94.1 5.5 %collective-permute-start.6 = (f32[4,1152]{1,0:T(4,128)S(1)}, f32[4,1152]{1,0:T(4,128)S(1)}, u32[]{:S(2)}, u32[]{:S(2)}) collective-permute-start(f32[4,1152]{1,0:T(4,128)S(1)} %get-tuple-element.57), channel_id=1, source_target_pairs={{0,256},{128,384},{256,0},{384,128},{1,257},{129,385},{257,1},{385... | collective-permute-start | bytes 55304 | tf_op jit(solution)/shard_map/ppermute | solution.py:168
  99.7 0.0 collective-permute-done.5
  99.7 3.1 %collective-permute-done.6 = f32[4,1152]{1,0:T(4,128)S(1)} collective-permute-done((f32[4,1152]{1,0:T(4,128)S(1)}, f32[4,1152]{1,0:T(4,128)S(1)}, u32[]{:S(2)}, u32[]{:S(2)}) %collective-permute-start.6) | collective-permute-done | bytes 18464 | tf_op jit(solution)/shard_map/ppermute | solution.py:168
  102.8 2.5 %collective-permute-start.8 = (f32[2,1152]{1,0:T(2,128)S(1)}, f32[2,1152]{1,0:T(2,128)S(1)}, u32[]{:S(2)}, u32[]{:S(2)}) collective-permute-start(f32[2,1152]{1,0:T(2,128)S(1)} %broadcast_select_fusion.5), channel_id=1, source_target_pairs={{0,32},{32,0},{1,33},{33,1},{2,34},{34,2},{3,35},{35,3},{4,36},{36... | collective-permute-start | bytes 27656 | tf_op jit(solution)/shard_map/ppermute | solution.py:133
  105.4 2.0 %copy-done = bf16[14336,128]{1,0:T(8,128)(2,1)S(1)} copy-done((bf16[14336,128]{1,0:T(8,128)(2,1)S(1)}, bf16[14336,128]{1,0:T(8,128)(2,1)}, u32[]{:S(2)}) %copy-start) | copy-done | bytes 3670040
  107.4 2.4 %backward.1 = (f32[128,896]{1,0:T(8,128)S(1)}, bf16[128,896]{1,0:T(8,128)(2,1)S(1)}) custom-call(s32[2]{0:T(128)S(1)} %copy-done.3, bf16[128,4096]{1,0:T(8,128)(2,1)S(1)} %copy-done.1, bf16[128,2048]{1,0:T(8,128)(2,1)S(1)} %collective-permute-done.2.h_ref, f32[1,4096]{1,0:T(1,128)S(1)} %bitcast_multiply_fusion.s_ref, bf16[16,896,128]{2,1,0:T(8,128)(2,1)S(1)} %bitcast.37, ...), custom_call_target="tpu_custom_call" | custom-call | flops 939524096 | bytes 3670016 | tf_op jit(solution)/shard_map/backward/pallas_call | solution.py:104
  109.8 0.0 collective-permute-done.8
  109.8 4.3 %all-to-all-done.3 = bf16[16,128,256]{2,1,0:T(8,128)(2,1)S(1)} async-done(((bf16[16,128,256]{2,1,0:T(8,128)(2,1)}), bf16[16,128,256]{2,1,0:T(8,128)(2,1)S(1)}, u32[]{:S(2)}, u32[]{:S(2)}) %all-to-all-start.3) | async-done | bytes 1048608 | tf_op jit(solution)/shard_map/all_to_all | solution.py:248
  114.1 0.1 convert_reduce_fusion
  114.2 0.1 multiply_reduce_fusion
  114.3 0.1 reduce-precision_convert_fusion
  114.4 0.9 broadcast_in_dim.14
  115.3 10.9 %all-to-all-start.4 = ((bf16[64,2,1408]{2,1,0:T(2,128)(2,1)}), bf16[64,2,1408]{2,1,0:T(2,128)(2,1)S(1)}, u32[]{:S(2)}, u32[]{:S(2)}) async-start(bf16[64,2,1408]{2,1,0:T(2,128)(2,1)} %broadcast_in_dim.14), calls=%async_computation.4 | async-start | bytes 720896 | tf_op jit(solution)/shard_map/all_to_all | solution.py:20
  126.3 0.7 collective-permute-start.9
  127.0 5.7 %collective-permute-start.10 = (bf16[128,896]{1,0:T(8,128)(2,1)S(1)}, bf16[128,896]{1,0:T(8,128)(2,1)S(1)}, u32[]{:S(2)}, u32[]{:S(2)}) collective-permute-start(bf16[128,896]{1,0:T(8,128)(2,1)S(1)} %get-tuple-element.35), channel_id=1, source_target_pairs={{0,32},{32,0},{1,33},{33,1},{2,34},{34,2},{3,35},{35,3},{4,36},{36... | collective-permute-start | bytes 688136 | tf_op jit(solution)/shard_map/ppermute | solution.py:133
  132.7 0.0 collective-permute-done.9
  132.7 0.7 broadcast_select_fusion.4
  133.3 7.4 %collective-permute-done.10 = bf16[128,896]{1,0:T(8,128)(2,1)S(1)} collective-permute-done((bf16[128,896]{1,0:T(8,128)(2,1)S(1)}, bf16[128,896]{1,0:T(8,128)(2,1)S(1)}, u32[]{:S(2)}, u32[]{:S(2)}) %collective-permute-start.10) | collective-permute-done | bytes 229408 | tf_op jit(solution)/shard_map/ppermute | solution.py:133
  140.7 0.7 add_convert_fusion
  141.5 0.6 convert_reduce_fusion.1
  142.1 0.2 convert_multiply_fusion
  142.3 0.2 mul.75
  142.5 0.6 slice.154
  143.1 0.7 slice_bitcast_fusion
  (41 shorter events, 0.4 us)
Async XLA Ops:
  7.2 19.2 %copy-start.1 = (bf16[128,4096]{1,0:T(8,128)(2,1)S(1)}, bf16[128,4096]{1,0:T(8,128)(2,1)}, u32[]{:S(2)}) copy-start(bf16[128,4096]{1,0:T(8,128)(2,1)} %g_ref.1) | copy-start | bytes 3145732
  7.2 57.7 %all-gather.3.cloned.1.call-start = ((), (), s32[]{:S(2)}) async-start(), calls=%async_computation.5 | async-start | bytes 3899392 | tf_op jit(solution)/shard_map/all_gather | solution.py:223
  9.4 23.5 %all-to-all-start = ((bf16[16,64,128]{2,1,0:T(8,128)(2,1)}), bf16[16,64,128]{2,1,0:T(8,128)(2,1)S(1)}, u32[]{:S(2)}, u32[]{:S(2)}) async-start(bf16[16,64,128]{2,1,0:T(8,128)(2,1)} %broadcast_in_dim.10), calls=%async_computation | async-start | bytes 524288 | tf_op jit(solution)/shard_map/all_to_all | solution.py:20
  26.4 18.7 %copy-start.5 = (bf16[128,896]{1,0:T(8,128)(2,1)S(1)}, bf16[128,896]{1,0:T(8,128)(2,1)}, u32[]{:S(2)}) copy-start(bf16[128,896]{1,0:T(8,128)(2,1)} %x_ref.3) | copy-start | bytes 688132
  32.9 0.7 copy-start.4
  35.8 17.4 %all-to-all-start.1 = ((bf16[16,72,128]{2,1,0:T(8,128)(2,1)}), bf16[16,72,128]{2,1,0:T(8,128)(2,1)S(1)}, u32[]{:S(2)}, u32[]{:S(2)}) async-start(bf16[16,72,128]{2,1,0:T(8,128)(2,1)} %second_blocks.1), calls=%async_computation.1 | async-start | bytes 589824 | tf_op jit(solution)/shard_map/all_to_all | solution.py:234
  41.1 9.9 %collective-permute-start.1 = (bf16[16,64,128]{2,1,0:T(8,128)(2,1)}, bf16[16,64,128]{2,1,0:T(8,128)(2,1)S(1)}, u32[]{:S(2)}, u32[]{:S(2)}) collective-permute-start(bf16[16,64,128]{2,1,0:T(8,128)(2,1)} %copy-done.4), channel_id=1, source_target_pairs={{0,16},{16,0},{1,17},{17,1},{2,18},{18,2},{3,19},{19,3},{4,20},{20... | collective-permute-start | bytes 786440 | tf_op jit(solution)/shard_map/ppermute | solution.py:133
  45.1 19.7 %collective-permute-start = (bf16[128,896]{1,0:T(8,128)(2,1)S(1)}, bf16[128,896]{1,0:T(8,128)(2,1)}, u32[]{:S(2)}, u32[]{:S(2)}) collective-permute-start(bf16[128,896]{1,0:T(8,128)(2,1)S(1)} %copy-done.5), channel_id=1, source_target_pairs={{0,32},{32,0},{1,33},{33,1},{2,34},{34,2},{3,35},{35,3},{4,36},{36... | collective-permute-start | bytes 688136 | tf_op jit(solution)/shard_map/ppermute | solution.py:133
  48.6 22.3 %collective-permute-start.2 = (bf16[128,2048]{1,0:T(8,128)(2,1)}, bf16[128,2048]{1,0:T(8,128)(2,1)S(1)}, u32[]{:S(2)}, u32[]{:S(2)}) collective-permute-start(bf16[128,2048]{1,0:T(8,128)(2,1)} %broadcast_select_fusion), channel_id=1, source_target_pairs={{0,32},{32,0},{1,33},{33,1},{2,34},{34,2},{3,35},{35,3},{4,36},{36... | collective-permute-start | bytes 1572872 | tf_op jit(solution)/shard_map/ppermute | solution.py:133
  51.0 13.8 %copy-start.7 = (bf16[16,64,128]{2,1,0:T(8,128)(2,1)}, bf16[16,64,128]{2,1,0:T(8,128)(2,1)S(1)}, u32[]{:S(2)}) copy-start(bf16[16,64,128]{2,1,0:T(8,128)(2,1)S(1)} %collective-permute-done.1.c_ref) | copy-start | bytes 786436
  53.8 18.7 %all-to-all-start.2 = ((f32[32,1,128]{2,1,0:T(1,128)}), f32[32,1,128]{2,1,0:T(1,128)S(1)}, u32[]{:S(2)}, u32[]{:S(2)}) async-start(f32[32,1,128]{2,1,0:T(1,128)} %broadcast_in_dim.11), calls=%async_computation.2 | async-start | bytes 32768 | tf_op jit(solution)/shard_map/all_to_all | solution.py:20
  70.9 2.3 %copy-start.6 = (bf16[128,896]{1,0:T(8,128)(2,1)S(1)}, bf16[128,896]{1,0:T(8,128)(2,1)}, u32[]{:S(2)}) copy-start(bf16[128,896]{1,0:T(8,128)(2,1)} %x_ref.3) | copy-start | bytes 688132
  73.6 31.8 %copy-start.2 = (bf16[896,64]{0,1:T(8,128)(2,1)S(1)}, bf16[896,64]{0,1:T(8,128)(2,1)}, u32[]{:S(2)}) copy-start(bf16[896,64]{0,1:T(8,128)(2,1)} %param.8) | copy-start | bytes 344068
  73.6 31.8 %copy-start.3 = (s32[2]{0:T(128)S(1)}, s32[2]{0:T(128)}, u32[]{:S(2)}) copy-start(s32[2]{0:T(128)} %pad_add_fusion.i_ref) | copy-start | bytes 28
  73.6 3.6 %collective-permute-start.3 = (f32[32,1152]{1,0:T(8,128)S(1)}, f32[32,1152]{1,0:T(8,128)S(1)}, u32[]{:S(2)}, u32[]{:S(2)}) collective-permute-start(f32[32,1152]{1,0:T(8,128)S(1)} %broadcast_select_fusion.2), channel_id=1, source_target_pairs={{0,16},{16,0},{1,17},{17,1},{2,18},{18,2},{3,19},{19,3},{4,20},{20... | collective-permute-start | bytes 442376 | tf_op jit(solution)/shard_map/ppermute | solution.py:133
  77.3 9.3 %collective-permute-start.4 = (f32[16,1152]{1,0:T(8,128)S(1)}, f32[16,1152]{1,0:T(8,128)S(1)}, u32[]{:S(2)}, u32[]{:S(2)}) collective-permute-start(f32[16,1152]{1,0:T(8,128)S(1)} %slice_select_fusion), channel_id=1, source_target_pairs={{0,64},{64,0},{1,65},{65,1},{2,66},{66,2},{3,67},{67,3},{4,68},{68... | collective-permute-start | bytes 221192 | tf_op jit(solution)/shard_map/ppermute | solution.py:133
  79.6 34.4 %all-to-all-start.3 = ((bf16[16,128,256]{2,1,0:T(8,128)(2,1)}), bf16[16,128,256]{2,1,0:T(8,128)(2,1)S(1)}, u32[]{:S(2)}, u32[]{:S(2)}) async-start(bf16[16,128,256]{2,1,0:T(8,128)(2,1)} %forward.1), calls=%async_computation.3 | async-start | bytes 2097152 | tf_op jit(solution)/shard_map/all_to_all | solution.py:248
  86.7 13.0 %collective-permute-start.5 = (f32[4,1152]{1,0:T(4,128)S(1)}, f32[4,1152]{1,0:T(4,128)S(1)}, u32[]{:S(2)}, u32[]{:S(2)}) collective-permute-start(f32[4,1152]{1,0:T(4,128)S(1)} %get-tuple-element.55), channel_id=1, source_target_pairs={{0,128},{128,256},{256,384},{384,0},{1,129},{129,257},{257,385},{3... | collective-permute-start | bytes 55304 | tf_op jit(solution)/shard_map/ppermute | solution.py:168
  90.1 9.6 %collective-permute-start.7 = (f32[4,1152]{1,0:T(4,128)S(1)}, f32[4,1152]{1,0:T(4,128)S(1)}, u32[]{:S(2)}, u32[]{:S(2)}) collective-permute-start(f32[4,1152]{1,0:T(4,128)S(1)} %get-tuple-element.56), channel_id=1, source_target_pairs={{0,384},{128,0},{256,128},{384,256},{1,385},{129,1},{257,129},{385... | collective-permute-start | bytes 55304 | tf_op jit(solution)/shard_map/ppermute | solution.py:168
  94.1 8.7 %collective-permute-start.6 = (f32[4,1152]{1,0:T(4,128)S(1)}, f32[4,1152]{1,0:T(4,128)S(1)}, u32[]{:S(2)}, u32[]{:S(2)}) collective-permute-start(f32[4,1152]{1,0:T(4,128)S(1)} %get-tuple-element.57), channel_id=1, source_target_pairs={{0,256},{128,384},{256,0},{384,128},{1,257},{129,385},{257,1},{385... | collective-permute-start | bytes 55304 | tf_op jit(solution)/shard_map/ppermute | solution.py:168
  102.8 7.0 %collective-permute-start.8 = (f32[2,1152]{1,0:T(2,128)S(1)}, f32[2,1152]{1,0:T(2,128)S(1)}, u32[]{:S(2)}, u32[]{:S(2)}) collective-permute-start(f32[2,1152]{1,0:T(2,128)S(1)} %broadcast_select_fusion.5), channel_id=1, source_target_pairs={{0,32},{32,0},{1,33},{33,1},{2,34},{34,2},{3,35},{35,3},{4,36},{36... | collective-permute-start | bytes 27656 | tf_op jit(solution)/shard_map/ppermute | solution.py:133
  105.4 2.0 %copy-start = (bf16[14336,128]{1,0:T(8,128)(2,1)S(1)}, bf16[14336,128]{1,0:T(8,128)(2,1)}, u32[]{:S(2)}) copy-start(bf16[14336,128]{1,0:T(8,128)(2,1)} %all-gather.3.cloned.1.call-done) | copy-start | bytes 11010052
  115.3 26.1 %all-to-all-start.4 = ((bf16[64,2,1408]{2,1,0:T(2,128)(2,1)}), bf16[64,2,1408]{2,1,0:T(2,128)(2,1)S(1)}, u32[]{:S(2)}, u32[]{:S(2)}) async-start(bf16[64,2,1408]{2,1,0:T(2,128)(2,1)} %broadcast_in_dim.14), calls=%async_computation.4 | async-start | bytes 720896 | tf_op jit(solution)/shard_map/all_to_all | solution.py:20
  126.3 6.4 %collective-permute-start.9 = (bf16[128,256]{1,0:T(8,128)(2,1)S(1)}, bf16[128,256]{1,0:T(8,128)(2,1)S(1)}, u32[]{:S(2)}, u32[]{:S(2)}) collective-permute-start(bf16[128,256]{1,0:T(8,128)(2,1)S(1)} %multiply_convert_fusion.1), channel_id=1, source_target_pairs={{0,0},{1,32},{32,1},{33,33},{2,2},{3,34},{34,3},{35,35},{4,4},{5,3... | collective-permute-start | bytes 196616 | tf_op jit(solution)/shard_map/ppermute | solution.py:137
  127.0 13.7 %collective-permute-start.10 = (bf16[128,896]{1,0:T(8,128)(2,1)S(1)}, bf16[128,896]{1,0:T(8,128)(2,1)S(1)}, u32[]{:S(2)}, u32[]{:S(2)}) collective-permute-start(bf16[128,896]{1,0:T(8,128)(2,1)S(1)} %get-tuple-element.35), channel_id=1, source_target_pairs={{0,32},{32,0},{1,33},{33,1},{2,34},{34,2},{3,35},{35,3},{4,36},{36... | collective-permute-start | bytes 688136 | tf_op jit(solution)/shard_map/ppermute | solution.py:133
Sparse Core Ops, SparseCore 0:
  10.1 49.9 all-gather.2

commit v7 on v6

--- a/solution.py
+++ b/solution.py
@@ -33,14 +33,18 @@
             x[...], a_ref[...], (((1,), (1,)), ((), ())), preferred_element_type=F32
         ).astype(BF16)
 
-    for k in range(2):
+    n = w_ref.shape[0]
+    ups = []
+    for k in range(n // 2):
         b, d = b_ref[2 * k + w], c_ref[2 * k + w]
-        up = jnp.concatenate([jnp.where(c == 0, b, d), jnp.where(c == 0, d, b)], axis=1)
-        wide = jnp.concatenate([w_ref[2 * k], w_ref[2 * k + 1]], axis=1)
-        y = jnp.dot(x[...], wide, preferred_element_type=F32)
-        y = (y + jnp.dot(r[...], up, preferred_element_type=F32)).astype(BF16)
-        out[2 * k] = y[:t]
-        out[2 * k + 1] = y[t:]
+        ups += [jnp.where(c == 0, b, d), jnp.where(c == 0, d, b)]
+    wide = jnp.concatenate([w_ref[k] for k in range(n)], axis=1)
+    y = jnp.dot(x[...], wide, preferred_element_type=F32)
+    y = y + jnp.dot(r[...], jnp.concatenate(ups, axis=1), preferred_element_type=F32)
+    y = y.astype(BF16)
+    for k in range(n // 2):
+        out[2 * k] = y[:t, k * 256 : (k + 1) * 256]
+        out[2 * k + 1] = y[t:, k * 256 : (k + 1) * 256]
 
 
 def forward(place, x, other_x, down_t, up, other_up, gathered):
@@ -52,19 +56,20 @@
         forward_kernel,
         grid_spec=pltpu.PrefetchScalarGridSpec(
             num_scalar_prefetch=1,
-            grid=(n // 4,),
+            grid=(n // 8,),
             in_specs=[
                 pl.BlockSpec((t, f), whole),
                 pl.BlockSpec((t, f), whole),
                 pl.BlockSpec((rank, f), whole),
-                pl.BlockSpec((4, rank, 128), part),
-                pl.BlockSpec((4, rank, 128), part),
-                pl.BlockSpec((4, f, 128), part),
+                pl.BlockSpec((8, rank, 128), part),
+                pl.BlockSpec((8, rank, 128), part),
+                pl.BlockSpec((8, f, 128), part),
             ],
-            out_specs=pl.BlockSpec((4, t, 256), part),
+            out_specs=pl.BlockSpec((8, t, 256), part),
             scratch_shapes=[pltpu.VMEM((2 * t, f), BF16), pltpu.VMEM((2 * t, rank), BF16)],
         ),
         out_shape=jax.ShapeDtypeStruct((n, t, 256), BF16),
+        compiler_params=pltpu.CompilerParams(vmem_limit_bytes=40 * 1024 * 1024),
         cost_estimate=pl.CostEstimate(
             flops=4 * t * f * n * 128, bytes_accessed=2 * f * n * 128, transcendentals=0
         ),

time: 152 us -> 155 us (1.020)
  local copies, waits for them, and re-layouts: 11.2 us -> 15.6 us
  Pallas kernels: 10.6 us -> 7.86 us
    pallas_call x1, Pallas kernels: 6.06 us -> 3.31 us  [forward(): pl.pallas_call(forward_kernel, grid_spec=pltpu.PrefetchScalarGridSpec(num...]
    unnamed x23 -> x27, local copies, waits for them, and re-layouts: 6.35 us -> 8.93 us
    all_to_all x3, starting transfers between devices: 35.2 us -> 33.4 us  [spread(): lax.all_to_all(jnp.broadcast_to(block[None], (n,) + block.shape), axis, 0...]
  transfers between devices with their start and end apart: 17 -> 17, of which waited for: 6 -> 6; matrix products, arithmetic and copies ran while one was open for 7% -> 8% of each run, Pallas kernels for 7% -> 5%
where the time goes in v7:
time: 155 us; the launch traced here: 153 us
  starting transfers between devices  82.2 us (53%)
  waiting for transfers between devices  24.8 us (16%)
  local copies, waits for them, and re-layouts  15.6 us (10%)
  between operations  14.6 us (9%)
  Pallas kernels  7.86 us (5%)
  other arithmetic  7.63 us (5%)
    all_to_all x3, starting transfers between devices, spread(): lax.all_to_all(jnp.broadcast_to(block[None], (n,) + block.shape), axis, 0...  33.4 us
    ppermute x7, starting transfers between devices, swap(): return lax.ppermute(x, axis, [(0, 1), (1, 0)])  21.9 us
    ppermute x3, starting transfers between devices, scatter(): total += lax.ppermute(block(k), axis, [(i, (i + k) % n) for i in range(n)])  12.6 us
    unnamed x27, local copies, waits for them, and re-layouts  8.93 us
    ppermute x7, waiting for transfers between devices, swap(): return lax.ppermute(x, axis, [(0, 1), (1, 0)])  8.37 us
    all_to_all x1, starting transfers between devices, on_device(): parts = lax.all_to_all(outgoing, TP, 0, 0)  8.22 us
    all_to_all x3, waiting for transfers between devices, spread(): lax.all_to_all(jnp.broadcast_to(block[None], (n,) + block.shape), axis, 0...  7.24 us
    all_to_all x1, starting transfers between devices, on_device(): second = lax.all_to_all(second, TP, 0, 0)  5.44 us
  transfers between devices with their start and end apart: 17, of which 6 were waited for; matrix products, arithmetic and copies ran while one was open for 8% of the time, Pallas kernels for 5%

profile of v7, /device:TPU:1, one launch (start us, length us, event | category | flops | bytes accessed | tf_op | source)
XLA Modules:
  0.0 153.5 jit_solution(4517832561523692473)
XLA Ops:
  7.2 0.0 copy-start.2
  7.2 0.0 all-gather.3.cloned.1.call-start
  7.2 0.7 all-gather.3.cloned.1.call-update
  7.9 0.7 slice_select_fusion.1
  8.7 0.7 broadcast_in_dim.10
  9.4 13.4 %all-to-all-start = ((bf16[16,64,128]{2,1,0:T(8,128)(2,1)}), bf16[16,64,128]{2,1,0:T(8,128)(2,1)S(1)}, u32[]{:S(2)}, u32[]{:S(2)}) async-start(bf16[16,64,128]{2,1,0:T(8,128)(2,1)} %broadcast_in_dim.10), calls=%async_computation | async-start | bytes 524288 | tf_op jit(solution)/shard_map/all_to_all | solution.py:20
  22.8 0.9 slice_dynamic-update-slice_fusion.7
  23.7 0.9 slice_dynamic-update-slice_fusion.6
  24.6 0.9 slice_dynamic-update-slice_fusion.5
  25.5 0.9 slice_dynamic-update-slice_fusion.4
  26.4 0.0 copy-start.5
  26.5 0.9 broadcast_select_fusion
  27.4 5.5 %all-to-all-done.b_ref = bf16[16,64,128]{2,1,0:T(8,128)(2,1)S(1)} async-done(((bf16[16,64,128]{2,1,0:T(8,128)(2,1)}), bf16[16,64,128]{2,1,0:T(8,128)(2,1)S(1)}, u32[]{:S(2)}, u32[]{:S(2)}) %all-to-all-start) | async-done | bytes 262176 | tf_op jit(solution)/shard_map/all_to_all | solution.py:20
  32.9 0.7 copy-done.3
  33.6 2.2 %second_blocks.1 = bf16[16,72,128]{2,1,0:T(8,128)(2,1)} custom-call(s32[1]{0:T(128)} %bitcast.i_ref, bf16[896,128]{1,0:T(8,128)(2,1)} %w_ref.1, bf16[64,896]{1,0:T(8,128)(2,1)} %bitcast.40, bf16[16,64,128]{2,1,0:T(8,128)(2,1)} %copy-done.3, bf16[128,896]{1,0:T(8,128)(2,1)} %x_ref.3, bf16[2,128]{1,0:T(2,128)(2,1)} %bitcast.50), custom_call_target="tpu_custom_call" | custom-call | tf_op jit(solution)/shard_map/second_blocks/pallas_call | solution.py:200
  35.8 5.4 %all-to-all-start.1 = ((bf16[16,72,128]{2,1,0:T(8,128)(2,1)}), bf16[16,72,128]{2,1,0:T(8,128)(2,1)S(1)}, u32[]{:S(2)}, u32[]{:S(2)}) async-start(bf16[16,72,128]{2,1,0:T(8,128)(2,1)} %second_blocks.1), calls=%async_computation.1 | async-start | bytes 589824 | tf_op jit(solution)/shard_map/all_to_all | solution.py:239
  41.2 4.0 %collective-permute-start.1 = (bf16[16,64,128]{2,1,0:T(8,128)(2,1)}, bf16[16,64,128]{2,1,0:T(8,128)(2,1)S(1)}, u32[]{:S(2)}, u32[]{:S(2)}) collective-permute-start(bf16[16,64,128]{2,1,0:T(8,128)(2,1)} %copy-done.3), channel_id=1, source_target_pairs={{0,16},{16,0},{1,17},{17,1},{2,18},{18,2},{3,19},{19,3},{4,20},{20... | collective-permute-start | bytes 786440 | tf_op jit(solution)/shard_map/ppermute | solution.py:138
  45.3 2.9 %collective-permute-start = (bf16[128,896]{1,0:T(8,128)(2,1)S(1)}, bf16[128,896]{1,0:T(8,128)(2,1)S(1)}, u32[]{:S(2)}, u32[]{:S(2)}) collective-permute-start(bf16[128,896]{1,0:T(8,128)(2,1)S(1)} %copy-done.5), channel_id=1, source_target_pairs={{0,32},{32,0},{1,33},{33,1},{2,34},{34,2},{3,35},{35,3},{4,36},{36... | collective-permute-start | bytes 688136 | tf_op jit(solution)/shard_map/ppermute | solution.py:138
  48.2 0.1 pad_add_fusion.i_ref
  48.2 2.4 %collective-permute-start.2 = (bf16[128,2048]{1,0:T(8,128)(2,1)}, bf16[128,2048]{1,0:T(8,128)(2,1)S(1)}, u32[]{:S(2)}, u32[]{:S(2)}) collective-permute-start(bf16[128,2048]{1,0:T(8,128)(2,1)} %broadcast_select_fusion), channel_id=1, source_target_pairs={{0,32},{32,0},{1,33},{33,1},{2,34},{34,2},{3,35},{35,3},{4,36},{36... | collective-permute-start | bytes 1572872 | tf_op jit(solution)/shard_map/ppermute | solution.py:138
  50.7 1.1 fusion
  51.8 1.3 copy.14
  53.1 1.4 reshape.86
  54.5 0.0 all-to-all-done.1
  54.6 0.6 broadcast_in_dim.11
  55.2 9.7 %all-to-all-start.2 = ((f32[32,1,128]{2,1,0:T(1,128)}), f32[32,1,128]{2,1,0:T(1,128)S(1)}, u32[]{:S(2)}, u32[]{:S(2)}) async-start(f32[32,1,128]{2,1,0:T(1,128)} %broadcast_in_dim.11), calls=%async_computation.2 | async-start | bytes 32768 | tf_op jit(solution)/shard_map/all_to_all | solution.py:20
  64.9 0.6 slice_reduce_fusion
  65.6 0.0 all-gather.3.cloned.1.call-done
  65.6 2.0 %copy-done = bf16[14336,128]{1,0:T(8,128)(2,1)S(1)} copy-done((bf16[14336,128]{1,0:T(8,128)(2,1)S(1)}, bf16[14336,128]{1,0:T(8,128)(2,1)}, u32[]{:S(2)}) %copy-start) | copy-done | bytes 3670040
  67.7 3.3 %forward.1 = bf16[16,128,256]{2,1,0:T(8,128)(2,1)} custom-call(s32[2]{0:T(128)S(1)} %pad_add_fusion.i_ref, bf16[128,896]{1,0:T(8,128)(2,1)S(1)} %copy-done.5, bf16[128,896]{1,0:T(8,128)(2,1)S(1)} %collective-permute-done.o_ref, bf16[64,896]{1,0:T(8,128)(2,1)S(1)} %bitcast.41, bf16[16,64,128]{2,1,0:T(8,128)(2,1)S(1)} %copy-done.4, ...), custom_call_target="tpu_custom_call" | custom-call | flops 939524096 | bytes 3670016 | tf_op jit(solution)/shard_map/forward/pallas_call | solution.py:55
  71.0 1.7 %all-to-all-done.2 = f32[32,1,128]{2,1,0:T(1,128)S(1)} async-done(((f32[32,1,128]{2,1,0:T(1,128)}), f32[32,1,128]{2,1,0:T(1,128)S(1)}, u32[]{:S(2)}, u32[]{:S(2)}) %all-to-all-start.2) | async-done | bytes 16416 | tf_op jit(solution)/shard_map/all_to_all | solution.py:20
  72.7 0.5 copy-done.7
  73.3 0.2 multiply_convert_fusion
  73.5 0.4 convolution_convert_fusion.r_ref
  73.9 0.2 fusion.8
  74.1 0.0 copy-start.8
  74.2 0.1 fusion.2
  74.3 2.5 %collective-permute-start.3 = (f32[32,1152]{1,0:T(8,128)S(1)}, f32[32,1152]{1,0:T(8,128)S(1)}, u32[]{:S(2)}, u32[]{:S(2)}) collective-permute-start(f32[32,1152]{1,0:T(8,128)S(1)} %broadcast_select_fusion.2), channel_id=1, source_target_pairs={{0,16},{16,0},{1,17},{17,1},{2,18},{18,2},{3,19},{19,3},{4,20},{20... | collective-permute-start | bytes 442376 | tf_op jit(solution)/shard_map/ppermute | solution.py:138
  76.9 1.0 collective-permute-done.3
  77.9 2.3 %collective-permute-start.4 = (f32[16,1152]{1,0:T(8,128)S(1)}, f32[16,1152]{1,0:T(8,128)S(1)}, u32[]{:S(2)}, u32[]{:S(2)}) collective-permute-start(f32[16,1152]{1,0:T(8,128)S(1)} %slice_select_fusion), channel_id=1, source_target_pairs={{0,64},{64,0},{1,65},{65,1},{2,66},{66,2},{3,67},{67,3},{4,68},{68... | collective-permute-start | bytes 221192 | tf_op jit(solution)/shard_map/ppermute | solution.py:138
  80.2 8.2 %all-to-all-start.3 = ((bf16[16,128,256]{2,1,0:T(8,128)(2,1)}), bf16[16,128,256]{2,1,0:T(8,128)(2,1)}, u32[]{:S(2)}, u32[]{:S(2)}) async-start(bf16[16,128,256]{2,1,0:T(8,128)(2,1)} %forward.1), calls=%async_computation.3 | async-start | bytes 2097152 | tf_op jit(solution)/shard_map/all_to_all | solution.py:253
  88.5 3.1 %collective-permute-start.5 = (f32[4,1152]{1,0:T(4,128)S(1)}, f32[4,1152]{1,0:T(4,128)S(1)}, u32[]{:S(2)}, u32[]{:S(2)}) collective-permute-start(f32[4,1152]{1,0:T(4,128)S(1)} %get-tuple-element.55), channel_id=1, source_target_pairs={{0,128},{128,256},{256,384},{384,0},{1,129},{129,257},{257,385},{3... | collective-permute-start | bytes 55304 | tf_op jit(solution)/shard_map/ppermute | solution.py:173
  91.6 4.3 %collective-permute-start.7 = (f32[4,1152]{1,0:T(4,128)S(1)}, f32[4,1152]{1,0:T(4,128)S(1)}, u32[]{:S(2)}, u32[]{:S(2)}) collective-permute-start(f32[4,1152]{1,0:T(4,128)S(1)} %get-tuple-element.56), channel_id=1, source_target_pairs={{0,384},{128,0},{256,128},{384,256},{1,385},{129,1},{257,129},{385... | collective-permute-start | bytes 55304 | tf_op jit(solution)/shard_map/ppermute | solution.py:173
  95.9 5.2 %collective-permute-start.6 = (f32[4,1152]{1,0:T(4,128)S(1)}, f32[4,1152]{1,0:T(4,128)S(1)}, u32[]{:S(2)}, u32[]{:S(2)}) collective-permute-start(f32[4,1152]{1,0:T(4,128)S(1)} %get-tuple-element.57), channel_id=1, source_target_pairs={{0,256},{128,384},{256,0},{384,128},{1,257},{129,385},{257,1},{385... | collective-permute-start | bytes 55304 | tf_op jit(solution)/shard_map/ppermute | solution.py:173
  101.2 3.7 %collective-permute-done.6 = f32[4,1152]{1,0:T(4,128)S(1)} collective-permute-done((f32[4,1152]{1,0:T(4,128)S(1)}, f32[4,1152]{1,0:T(4,128)S(1)}, u32[]{:S(2)}, u32[]{:S(2)}) %collective-permute-start.6) | collective-permute-done | bytes 18464 | tf_op jit(solution)/shard_map/ppermute | solution.py:173
  105.0 2.1 %collective-permute-start.8 = (f32[2,1152]{1,0:T(2,128)S(1)}, f32[2,1152]{1,0:T(2,128)S(1)}, u32[]{:S(2)}, u32[]{:S(2)}) collective-permute-start(f32[2,1152]{1,0:T(2,128)S(1)} %broadcast_select_fusion.5), channel_id=1, source_target_pairs={{0,32},{32,0},{1,33},{33,1},{2,34},{34,2},{3,35},{35,3},{4,36},{36... | collective-permute-start | bytes 27656 | tf_op jit(solution)/shard_map/ppermute | solution.py:138
  107.1 2.0 %copy-done.1 = bf16[14336,128]{1,0:T(8,128)(2,1)S(1)} copy-done((bf16[14336,128]{1,0:T(8,128)(2,1)S(1)}, bf16[14336,128]{1,0:T(8,128)(2,1)}, u32[]{:S(2)}) %copy-start.1) | copy-done | bytes 3670040
  109.1 2.4 %backward.1 = (f32[128,896]{1,0:T(8,128)S(1)}, bf16[128,896]{1,0:T(8,128)(2,1)S(1)}) custom-call(s32[2]{0:T(128)S(1)} %pad_add_fusion.i_ref, bf16[128,4096]{1,0:T(8,128)(2,1)S(1)} %copy-done.2, bf16[128,2048]{1,0:T(8,128)(2,1)S(1)} %collective-permute-done.2.h_ref, f32[1,4096]{1,0:T(1,128)S(1)} %bitcast_multiply_fusion.s_ref, ...), custom_call_target="tpu_custom_call" | custom-call | flops 939524096 | bytes 3670016 | tf_op jit(solution)/shard_map/backward/pallas_call | solution.py:109
  111.5 4.7 %all-to-all-done.3 = bf16[16,128,256]{2,1,0:T(8,128)(2,1)} async-done(((bf16[16,128,256]{2,1,0:T(8,128)(2,1)}), bf16[16,128,256]{2,1,0:T(8,128)(2,1)}, u32[]{:S(2)}, u32[]{:S(2)}) %all-to-all-start.3) | async-done | bytes 1048608 | tf_op jit(solution)/shard_map/all_to_all | solution.py:253
  116.3 1.4 convert_reduce_fusion
  117.6 0.1 multiply_reduce_fusion
  117.7 0.1 reduce-precision_convert_fusion
  117.8 0.9 broadcast_in_dim.14
  118.8 10.3 %all-to-all-start.4 = ((bf16[64,2,1408]{2,1,0:T(2,128)(2,1)}), bf16[64,2,1408]{2,1,0:T(2,128)(2,1)S(1)}, u32[]{:S(2)}, u32[]{:S(2)}) async-start(bf16[64,2,1408]{2,1,0:T(2,128)(2,1)} %broadcast_in_dim.14), calls=%async_computation.4 | async-start | bytes 720896 | tf_op jit(solution)/shard_map/all_to_all | solution.py:20
  129.1 0.7 collective-permute-start.9
  129.8 5.7 %collective-permute-start.10 = (bf16[128,896]{1,0:T(8,128)(2,1)S(1)}, bf16[128,896]{1,0:T(8,128)(2,1)S(1)}, u32[]{:S(2)}, u32[]{:S(2)}) collective-permute-start(bf16[128,896]{1,0:T(8,128)(2,1)S(1)} %get-tuple-element.35), channel_id=1, source_target_pairs={{0,32},{32,0},{1,33},{33,1},{2,34},{34,2},{3,35},{35,3},{4,36},{36... | collective-permute-start | bytes 688136 | tf_op jit(solution)/shard_map/ppermute | solution.py:138
  135.5 0.7 broadcast_select_fusion.4
  136.2 7.4 %collective-permute-done.10 = bf16[128,896]{1,0:T(8,128)(2,1)S(1)} collective-permute-done((bf16[128,896]{1,0:T(8,128)(2,1)S(1)}, bf16[128,896]{1,0:T(8,128)(2,1)S(1)}, u32[]{:S(2)}, u32[]{:S(2)}) %collective-permute-start.10) | collective-permute-done | bytes 229408 | tf_op jit(solution)/shard_map/ppermute | solution.py:138
  143.5 0.7 add_convert_fusion
  144.3 0.6 convert_reduce_fusion.1
  144.9 0.2 convert_multiply_fusion
  145.1 0.2 mul.75
  145.3 0.6 slice.154
  145.9 0.7 slice_bitcast_fusion
  (45 shorter events, 0.4 us)
Async XLA Ops:
  7.2 19.2 %copy-start.2 = (bf16[128,4096]{1,0:T(8,128)(2,1)S(1)}, bf16[128,4096]{1,0:T(8,128)(2,1)}, u32[]{:S(2)}) copy-start(bf16[128,4096]{1,0:T(8,128)(2,1)} %g_ref.1) | copy-start | bytes 3145732
  7.2 58.4 %all-gather.3.cloned.1.call-start = ((), (), s32[]{:S(2)}) async-start(), calls=%async_computation.5 | async-start | bytes 3899392 | tf_op jit(solution)/shard_map/all_gather | solution.py:228
  9.4 23.5 %all-to-all-start = ((bf16[16,64,128]{2,1,0:T(8,128)(2,1)}), bf16[16,64,128]{2,1,0:T(8,128)(2,1)S(1)}, u32[]{:S(2)}, u32[]{:S(2)}) async-start(bf16[16,64,128]{2,1,0:T(8,128)(2,1)} %broadcast_in_dim.10), calls=%async_computation | async-start | bytes 524288 | tf_op jit(solution)/shard_map/all_to_all | solution.py:20
  26.4 18.8 %copy-start.5 = (bf16[128,896]{1,0:T(8,128)(2,1)S(1)}, bf16[128,896]{1,0:T(8,128)(2,1)}, u32[]{:S(2)}) copy-start(bf16[128,896]{1,0:T(8,128)(2,1)} %x_ref.3) | copy-start | bytes 688132
  32.9 0.7 copy-start.3
  35.8 29.8 %copy-start.4 = (bf16[16,64,128]{2,1,0:T(8,128)(2,1)S(1)}, bf16[16,64,128]{2,1,0:T(8,128)(2,1)}, u32[]{:S(2)}) copy-start(bf16[16,64,128]{2,1,0:T(8,128)(2,1)} %copy-done.3) | copy-start | bytes 786436
  35.8 29.8 %copy-start.6 = (bf16[896,64]{0,1:T(8,128)(2,1)S(1)}, bf16[896,64]{0,1:T(8,128)(2,1)}, u32[]{:S(2)}) copy-start(bf16[896,64]{0,1:T(8,128)(2,1)} %param.8) | copy-start | bytes 344068
  35.8 18.7 %all-to-all-start.1 = ((bf16[16,72,128]{2,1,0:T(8,128)(2,1)}), bf16[16,72,128]{2,1,0:T(8,128)(2,1)S(1)}, u32[]{:S(2)}, u32[]{:S(2)}) async-start(bf16[16,72,128]{2,1,0:T(8,128)(2,1)} %second_blocks.1), calls=%async_computation.1 | async-start | bytes 589824 | tf_op jit(solution)/shard_map/all_to_all | solution.py:239
  41.2 9.4 %collective-permute-start.1 = (bf16[16,64,128]{2,1,0:T(8,128)(2,1)}, bf16[16,64,128]{2,1,0:T(8,128)(2,1)S(1)}, u32[]{:S(2)}, u32[]{:S(2)}) collective-permute-start(bf16[16,64,128]{2,1,0:T(8,128)(2,1)} %copy-done.3), channel_id=1, source_target_pairs={{0,16},{16,0},{1,17},{17,1},{2,18},{18,2},{3,19},{19,3},{4,20},{20... | collective-permute-start | bytes 786440 | tf_op jit(solution)/shard_map/ppermute | solution.py:138
  45.3 20.3 %collective-permute-start = (bf16[128,896]{1,0:T(8,128)(2,1)S(1)}, bf16[128,896]{1,0:T(8,128)(2,1)S(1)}, u32[]{:S(2)}, u32[]{:S(2)}) collective-permute-start(bf16[128,896]{1,0:T(8,128)(2,1)S(1)} %copy-done.5), channel_id=1, source_target_pairs={{0,32},{32,0},{1,33},{33,1},{2,34},{34,2},{3,35},{35,3},{4,36},{36... | collective-permute-start | bytes 688136 | tf_op jit(solution)/shard_map/ppermute | solution.py:138
  48.2 22.7 %collective-permute-start.2 = (bf16[128,2048]{1,0:T(8,128)(2,1)}, bf16[128,2048]{1,0:T(8,128)(2,1)S(1)}, u32[]{:S(2)}, u32[]{:S(2)}) collective-permute-start(bf16[128,2048]{1,0:T(8,128)(2,1)} %broadcast_select_fusion), channel_id=1, source_target_pairs={{0,32},{32,0},{1,33},{33,1},{2,34},{34,2},{3,35},{35,3},{4,36},{36... | collective-permute-start | bytes 1572872 | tf_op jit(solution)/shard_map/ppermute | solution.py:138
  55.2 17.5 %all-to-all-start.2 = ((f32[32,1,128]{2,1,0:T(1,128)}), f32[32,1,128]{2,1,0:T(1,128)S(1)}, u32[]{:S(2)}, u32[]{:S(2)}) async-start(f32[32,1,128]{2,1,0:T(1,128)} %broadcast_in_dim.11), calls=%async_computation.2 | async-start | bytes 32768 | tf_op jit(solution)/shard_map/all_to_all | solution.py:20
  65.6 2.0 %copy-start = (bf16[14336,128]{1,0:T(8,128)(2,1)S(1)}, bf16[14336,128]{1,0:T(8,128)(2,1)}, u32[]{:S(2)}) copy-start(bf16[14336,128]{1,0:T(8,128)(2,1)} %all-gather.3.cloned.1.call-done) | copy-start | bytes 11010052
  72.7 0.6 copy-start.7
  73.3 0.9 copy-start.9
  74.1 27.0 %copy-start.8 = (f32[32,1,128]{2,1,0:T(1,128)S(1)}, f32[32,1,128]{2,1,0:T(1,128)}, u32[]{:S(2)}) copy-start(f32[32,1,128]{2,1,0:T(1,128)} %copy-done.7) | copy-start | bytes 49156
  74.3 3.5 %collective-permute-start.3 = (f32[32,1152]{1,0:T(8,128)S(1)}, f32[32,1152]{1,0:T(8,128)S(1)}, u32[]{:S(2)}, u32[]{:S(2)}) collective-permute-start(f32[32,1152]{1,0:T(8,128)S(1)} %broadcast_select_fusion.2), channel_id=1, source_target_pairs={{0,16},{16,0},{1,17},{17,1},{2,18},{18,2},{3,19},{19,3},{4,20},{20... | collective-permute-start | bytes 442376 | tf_op jit(solution)/shard_map/ppermute | solution.py:138
  77.9 10.6 %collective-permute-start.4 = (f32[16,1152]{1,0:T(8,128)S(1)}, f32[16,1152]{1,0:T(8,128)S(1)}, u32[]{:S(2)}, u32[]{:S(2)}) collective-permute-start(f32[16,1152]{1,0:T(8,128)S(1)} %slice_select_fusion), channel_id=1, source_target_pairs={{0,64},{64,0},{1,65},{65,1},{2,66},{66,2},{3,67},{67,3},{4,68},{68... | collective-permute-start | bytes 221192 | tf_op jit(solution)/shard_map/ppermute | solution.py:138
  80.2 36.0 %all-to-all-start.3 = ((bf16[16,128,256]{2,1,0:T(8,128)(2,1)}), bf16[16,128,256]{2,1,0:T(8,128)(2,1)}, u32[]{:S(2)}, u32[]{:S(2)}) async-start(bf16[16,128,256]{2,1,0:T(8,128)(2,1)} %forward.1), calls=%async_computation.3 | async-start | bytes 2097152 | tf_op jit(solution)/shard_map/all_to_all | solution.py:253
  88.5 12.7 %collective-permute-start.5 = (f32[4,1152]{1,0:T(4,128)S(1)}, f32[4,1152]{1,0:T(4,128)S(1)}, u32[]{:S(2)}, u32[]{:S(2)}) collective-permute-start(f32[4,1152]{1,0:T(4,128)S(1)} %get-tuple-element.55), channel_id=1, source_target_pairs={{0,128},{128,256},{256,384},{384,0},{1,129},{129,257},{257,385},{3... | collective-permute-start | bytes 55304 | tf_op jit(solution)/shard_map/ppermute | solution.py:173
  91.6 9.6 %collective-permute-start.7 = (f32[4,1152]{1,0:T(4,128)S(1)}, f32[4,1152]{1,0:T(4,128)S(1)}, u32[]{:S(2)}, u32[]{:S(2)}) collective-permute-start(f32[4,1152]{1,0:T(4,128)S(1)} %get-tuple-element.56), channel_id=1, source_target_pairs={{0,384},{128,0},{256,128},{384,256},{1,385},{129,1},{257,129},{385... | collective-permute-start | bytes 55304 | tf_op jit(solution)/shard_map/ppermute | solution.py:173
  95.9 9.0 %collective-permute-start.6 = (f32[4,1152]{1,0:T(4,128)S(1)}, f32[4,1152]{1,0:T(4,128)S(1)}, u32[]{:S(2)}, u32[]{:S(2)}) collective-permute-start(f32[4,1152]{1,0:T(4,128)S(1)} %get-tuple-element.57), channel_id=1, source_target_pairs={{0,256},{128,384},{256,0},{384,128},{1,257},{129,385},{257,1},{385... | collective-permute-start | bytes 55304 | tf_op jit(solution)/shard_map/ppermute | solution.py:173
  105.0 6.5 %collective-permute-start.8 = (f32[2,1152]{1,0:T(2,128)S(1)}, f32[2,1152]{1,0:T(2,128)S(1)}, u32[]{:S(2)}, u32[]{:S(2)}) collective-permute-start(f32[2,1152]{1,0:T(2,128)S(1)} %broadcast_select_fusion.5), channel_id=1, source_target_pairs={{0,32},{32,0},{1,33},{33,1},{2,34},{34,2},{3,35},{35,3},{4,36},{36... | collective-permute-start | bytes 27656 | tf_op jit(solution)/shard_map/ppermute | solution.py:138
  107.1 2.0 %copy-start.1 = (bf16[14336,128]{1,0:T(8,128)(2,1)S(1)}, bf16[14336,128]{1,0:T(8,128)(2,1)}, u32[]{:S(2)}) copy-start(bf16[14336,128]{1,0:T(8,128)(2,1)} %all-gather.3.cloned.1.call-done) | copy-start | bytes 11010052
  118.8 25.5 %all-to-all-start.4 = ((bf16[64,2,1408]{2,1,0:T(2,128)(2,1)}), bf16[64,2,1408]{2,1,0:T(2,128)(2,1)S(1)}, u32[]{:S(2)}, u32[]{:S(2)}) async-start(bf16[64,2,1408]{2,1,0:T(2,128)(2,1)} %broadcast_in_dim.14), calls=%async_computation.4 | async-start | bytes 720896 | tf_op jit(solution)/shard_map/all_to_all | solution.py:20
  129.1 6.4 %collective-permute-start.9 = (bf16[128,256]{1,0:T(8,128)(2,1)S(1)}, bf16[128,256]{1,0:T(8,128)(2,1)S(1)}, u32[]{:S(2)}, u32[]{:S(2)}) collective-permute-start(bf16[128,256]{1,0:T(8,128)(2,1)S(1)} %multiply_convert_fusion.1), channel_id=1, source_target_pairs={{0,0},{1,32},{32,1},{33,33},{2,2},{3,34},{34,3},{35,35},{4,4},{5,3... | collective-permute-start | bytes 196616 | tf_op jit(solution)/shard_map/ppermute | solution.py:142
  129.8 13.7 %collective-permute-start.10 = (bf16[128,896]{1,0:T(8,128)(2,1)S(1)}, bf16[128,896]{1,0:T(8,128)(2,1)S(1)}, u32[]{:S(2)}, u32[]{:S(2)}) collective-permute-start(bf16[128,896]{1,0:T(8,128)(2,1)S(1)} %get-tuple-element.35), channel_id=1, source_target_pairs={{0,32},{32,0},{1,33},{33,1},{2,34},{34,2},{3,35},{35,3},{4,36},{36... | collective-permute-start | bytes 688136 | tf_op jit(solution)/shard_map/ppermute | solution.py:138
Sparse Core Ops, SparseCore 0:
  10.1 49.9 all-gather.2
